TPU v7x, 128 devices: a whole 4x4x4 slice. The times are simulated.
128 devices in a mesh: row: 8 (over x_lo, y), col: 16 (over x_hi, z, core).
Axes of the slice: x: 4 (x_hi: 2, x_lo: 2; x = x_hi * 2 + x_lo), y: 4, z: 4, core: 2. Of those that a mesh axis runs over, the one named last changes fastest.
Arguments:
- pair: bfloat16 [512, 512, 128], P('row', 'col'), may hold values from -6 to 6
- grad_out: bfloat16 [512, 512, 128], P('row', 'col'), may hold values from -6 to 6
- norm_gain: float32 [128], replicated, may hold values from 0.25 to 1.75
- norm_shift: float32 [128], replicated, may hold values from -3 to 3
- w_query: bfloat16 [128, 128], replicated
- w_key: bfloat16 [128, 128], replicated, may hold values from -0.5 to 0.5
- w_value: bfloat16 [128, 128], replicated, may hold values from -0.5 to 0.5
- w_gate: bfloat16 [128, 128], replicated, may hold values from -0.5 to 0.5
- w_bias: bfloat16 [128, 4], replicated, may hold values from -1 to 1
- w_out: bfloat16 [128, 128], replicated, may hold values from -0.5 to 0.5
Outputs:
- d_pair: bfloat16 [512, 512, 128], P('row', 'col')
- d_gain: float32 [128], replicated
- d_shift: float32 [128], replicated
- d_query: float32 [128, 128], replicated
- d_key: float32 [128, 128], replicated
- d_value: float32 [128, 128], replicated
- d_gate: float32 [128, 128], replicated
- d_bias: float32 [128, 4], replicated
- d_out: float32 [128, 128], replicated
All inputs are finite; a program needn't handle non-finite values.
Results may differ from a plain program's by a relative error of at most 0.012.
The roundings to bfloat16 on the way count: a program that leaves them out, or rounds other values in their place, can miss the bound.
Values may be sent and summed in bfloat16 or wider, within the bound.
No kernel may reach another device: no remote copies, remote signals or barrier semaphores. Data moves between devices by JAX's collectives and lax.ppermute only.
A program may use at most 192 MiB of HBM per device.

v0:
```python
import jax
import jax.numpy as jnp
from jax import lax
from jax.sharding import PartitionSpec as P

H = 4
DH = 32


EPS = 1e-05


def layer_norm(pair, norm_gain, norm_shift):
    values = pair.astype(jnp.float32)
    center = values - jnp.mean(values, axis=-1, keepdims=True)
    rstd = lax.rsqrt(jnp.mean(center * center, axis=-1, keepdims=True) + EPS)
    normed = center * rstd
    return ((normed * norm_gain + norm_shift).astype(jnp.bfloat16), normed, rstd)


def project(values, weight):
    return jnp.einsum(
        "...e,ce->...c", values, weight.astype(jnp.float32), precision=lax.Precision.HIGHEST
    )


def outer_sum(inputs, grads):
    return jnp.einsum(
        "ijc,ijd->cd", inputs.astype(jnp.float32), grads, precision=lax.Precision.HIGHEST
    )


def attend_grad(x_query, x_keys, bias, grad_rows, w_query, w_key, w_value, w_gate, w_out):
    rows, cols = (x_query.shape[0], x_query.shape[1])
    keys = x_keys.shape[1]
    scale = DH ** (-0.5)
    f32 = jnp.float32
    query = (
        jnp.einsum("ijc,cd->ijd", x_query, w_query, preferred_element_type=f32)
        .astype(jnp.bfloat16)
        .reshape(rows, cols, H, DH)
    )
    key_h = (
        jnp.einsum("ijc,cd->ijd", x_keys, w_key, preferred_element_type=f32)
        .astype(jnp.bfloat16)
        .reshape(rows, keys, H, DH)
    )
    value_h = (
        jnp.einsum("ijc,cd->ijd", x_keys, w_value, preferred_element_type=f32)
        .astype(jnp.bfloat16)
        .reshape(rows, keys, H, DH)
    )
    gate = jax.nn.sigmoid(jnp.einsum("ijc,cd->ijd", x_query, w_gate, preferred_element_type=f32))
    scores = jnp.einsum("ijhd,ikhd->ihjk", query, key_h, preferred_element_type=f32) * scale + bias[
        None
    ].astype(f32)
    expo = jnp.exp(scores - jnp.max(scores, axis=-1, keepdims=True))
    probs = expo / jnp.sum(expo, axis=-1, keepdims=True)
    probs_b = probs.astype(jnp.bfloat16)
    attended = jnp.einsum("ihjk,ikhd->ijhd", probs_b, value_h, preferred_element_type=f32)
    flat = attended.reshape(rows, cols, H * DH)
    gated = (gate * flat).astype(jnp.bfloat16)
    dgated = jnp.einsum("ijd,cd->ijc", grad_rows, w_out, preferred_element_type=f32)
    d_out = jnp.einsum("ijc,ijd->cd", gated, grad_rows, preferred_element_type=f32)
    dob = (dgated * gate).astype(jnp.bfloat16)
    dgraw = dgated * flat * gate * (1.0 - gate)
    dob_h = dob.reshape(rows, cols, H, DH)
    dprob = jnp.einsum("ijhd,ikhd->ihjk", dob_h, value_h, preferred_element_type=f32)
    dvalue = jnp.einsum("ihjk,ijhd->ikhd", probs_b, dob_h, preferred_element_type=f32)
    delta = jnp.sum(dob_h.astype(f32) * attended, axis=-1).transpose(0, 2, 1)[..., None]
    dscore = probs * (dprob - delta)
    dscore_b = dscore.astype(jnp.bfloat16)
    dquery = jnp.einsum("ihjk,ikhd->ijhd", dscore_b, key_h, preferred_element_type=f32) * scale
    dkey = jnp.einsum("ihjk,ijhd->ikhd", dscore_b, query, preferred_element_type=f32) * scale
    dbias = jnp.sum(dscore, axis=0)
    dquery = dquery.reshape(rows, cols, H * DH)
    dx_query = project(dquery, w_query) + project(dgraw, w_gate)
    return (
        dx_query,
        dkey.reshape(rows, keys, H * DH),
        dvalue.reshape(rows, keys, H * DH),
        dbias,
        outer_sum(x_query, dquery),
        outer_sum(x_query, dgraw),
        d_out,
    )


def on_device(
    pair, grad_out, norm_gain, norm_shift, w_query, w_key, w_value, w_gate, w_bias, w_out
):
    rows, cols = (pair.shape[0], pair.shape[1])
    x, normed, rstd = layer_norm(pair, norm_gain, norm_shift)
    tile_bias = jnp.einsum("ijc,ch->hij", x, w_bias, preferred_element_type=jnp.float32).astype(
        jnp.bfloat16
    )
    bias_wide = lax.all_gather(tile_bias, "col", axis=2, tiled=True)
    bias_full = lax.all_gather(bias_wide, "row", axis=1, tiled=True)
    row_start = lax.axis_index("row") * rows
    col_start = lax.axis_index("col") * cols
    x_keys = lax.all_gather(x, "col", axis=1, tiled=True)
    bias_query = lax.dynamic_slice_in_dim(bias_full, col_start, cols, 1)
    dx_q, dkey, dvalue, dbias, dwq, dwg, dwo = attend_grad(
        x, x_keys, bias_query, grad_out, w_query, w_key, w_value, w_gate, w_out
    )
    key_terms = project(dkey, w_key) + project(dvalue, w_value)
    dwk = outer_sum(x_keys, dkey)
    dwv = outer_sum(x_keys, dvalue)
    dx = dx_q + lax.psum_scatter(key_terms, "col", scatter_dimension=1, tiled=True)
    dbias_rows = lax.psum(dbias, "row")
    dbias_full = lax.all_gather(dbias_rows, "col", axis=1, tiled=True)
    anchor = row_start * 0
    dbias_tile = lax.dynamic_slice(
        dbias_full, (anchor, row_start, col_start), (H, rows, cols)
    ).transpose(1, 2, 0)
    dx = dx + project(dbias_tile, w_bias)
    dwb = outer_sum(x, dbias_tile)
    dgain = jnp.sum(dx * normed, axis=(0, 1))
    dshift = jnp.sum(dx, axis=(0, 1))
    dnorm = dx * norm_gain
    d_pair = rstd * (
        dnorm
        - jnp.mean(dnorm, axis=-1, keepdims=True)
        - normed * jnp.mean(dnorm * normed, axis=-1, keepdims=True)
    )
    sums = lax.psum((dwq, dwk, dwv, dwg, dwb, dwo, dgain, dshift), ("row", "col"))
    return (
        d_pair.astype(jnp.bfloat16),
        sums[6],
        sums[7],
        sums[0],
        sums[1],
        sums[2],
        sums[3],
        sums[4],
        sums[5],
    )


def solution(mesh):
    return jax.shard_map(
        on_device,
        mesh=mesh,
        in_specs=(
            P("row", "col", None),
            P("row", "col", None),
            P(),
            P(),
            P(),
            P(),
            P(),
            P(),
            P(),
            P(),
        ),
        out_specs=(P("row", "col", None), P(), P(), P(), P(), P(), P(), P(), P()),
        check_vma=False,
    )
```

profile of v0, /device:TPU:1, one launch (start us, length us, event | category | flops | bytes accessed | tf_op | source)
XLA Modules:
  0.0 675.0 jit_solution(3135058351394973310)
XLA Ops:
  13.7 28.2 %all_gather.13 = bf16[4,64,512]{1,0,2:T(4,128)(2,1)S(1)} all-gather(bf16[4,64,32]{1,0,2:T(4,128)(2,1)S(1)} %copy.92), channel_id=1, replica_groups=mesh['row'=8,'col'=16] {'col'}, dimensions={2}, use_global_device_ids=true | all-gather | bytes 278528 | tf_op jit(solution)/shard_map/all_gather | solution.py:97
  47.0 1.9 copy.121
  48.9 2.6 copy.95
  52.6 2.6 copy.90
  55.2 4.9 copy.91
  60.1 5.0 copy.97
  65.1 10.9 %all-gather.6.cloned.1.call-done = bf16[4,512,512]{2,0,1:T(4,128)(2,1)} async-done(((bf16[4,64,512]{2,0,1:T(4,128)(2,1)}), bf16[4,512,512]{2,0,1:T(4,128)(2,1)}) %all-gather.6.cloned.1.call-update) | async-done | bytes 2097168 | tf_op jit(solution)/shard_map/all_gather | solution.py:98
  77.0 84.0 %all-gather.4.cloned.1.call-done = bf16[64,512,128]{2,1,0:T(8,128)(2,1)} async-done(((bf16[64,32,128]{2,1,0:T(8,128)(2,1)}), bf16[64,512,128]{2,1,0:T(8,128)(2,1)}) %all-gather.4.cloned.1.call-update) | async-done | bytes 8388624 | tf_op jit(solution)/shard_map/all_gather | solution.py:101
  161.0 9.0 %convolution_convert_fusion.1 = bf16[64,512,128]{1,2,0:T(8,128)(2,1)} fusion(bf16[64,512,128]{2,1,0:T(8,128)(2,1)} %all-gather.4.cloned.1.call-done, bf16[128,128]{1,0:T(8,128)(2,1)S(1)} %copy-done.8), kind=kOutput, calls=%fused_computation.11 | convolution fusion | flops 1077936128 | bytes 16809984 | tf_op jit(solution)/shard_map/ijc,cd->ijd/dot_general | solution.py:44
  170.0 11.6 %fusion.53 = (f32[64,4,32]{2,1,0:T(4,128)}, f32[64,4,32,512]{3,2,1,0:T(8,128)}) fusion(f32[4,32,512]{2,1,0:T(8,128)S(1)} %copy_convert_fusion, bf16[64,32,4,32]{3,1,2,0:T(8,128)(2,1)} %copy.91, bf16[64,512,4,32]{1,3,2,0:T(8,128)(2,1)} %bitcast.123), kind=kOutput, calls=%fused_computation.83 | convolution fusion | flops 285213184 | bytes 25985024 | tf_op jit(solution)/shard_map/sub | solution.py:57
  181.6 9.4 %fusion.4 = bf16[64,4,32,512]{3,2,1,0:T(8,128)(2,1)} fusion(f32[64,4,32,512]{3,2,1,0:T(8,128)} %get-tuple-element.24, f32[64,4,32]{2,1,0:T(4,128)} %get-tuple-element.23), kind=kLoop, calls=%fused_computation.12 | loop fusion | flops 8388608 | bytes 25198592 | tf_op jit(solution)/shard_map/convert_element_type | solution.py:59
  191.0 9.0 %convolution_convert_fusion = bf16[64,512,128]{1,2,0:T(8,128)(2,1)} fusion(bf16[64,512,128]{2,1,0:T(8,128)(2,1)} %all-gather.4.cloned.1.call-done, bf16[128,128]{1,0:T(8,128)(2,1)S(1)} %copy-done.10), kind=kOutput, calls=%fused_computation.10 | convolution fusion | flops 1077936128 | bytes 16809984 | tf_op jit(solution)/shard_map/ijc,cd->ijd/dot_general | solution.py:49
  200.0 10.1 %fusion.5 = (f32[64,32,4]{1,2,0:T(4,128)S(1)}, f32[64,4,32,32]{3,2,1,0:T(8,128)}) fusion(bf16[64,32,128]{1,2,0:T(8,128)(2,1)S(1)} %copy.121, bf16[64,512,4,32]{1,3,2,0:T(8,128)(2,1)} %bitcast.125, bf16[64,4,32,512]{3,2,1,0:T(8,128)(2,1)} %fusion.4), kind=kOutput, calls=%fused_computation.14 | convolution fusion | flops 269213696 | bytes 18382848 | tf_op jit(solution)/shard_map/ihjk,ikhd->ijhd/dot_general | solution.py:60
  210.1 13.8 %fusion.54 = (f32[4,32,512]{2,1,0:T(8,128)}, bf16[64,4,32,512]{3,2,1,0:T(8,128)(2,1)}) fusion(f32[64,4,32]{2,1,0:T(4,128)S(1)} %bitcast.132, bf16[64,32,4,32]{3,1,2,0:T(8,128)(2,1)} %copy.97, bf16[64,512,4,32]{1,3,2,0:T(8,128)(2,1)} %bitcast.126, f32[64,4,32,512]{3,2,1,0:T(8,128)} %get-tuple-element.24, f32[64,4,32]{2,1,0:T(4,128)S(1)} %copy-done.7), kind=kOutput, calls=%fused_computation.84 | convolution fusion | flops 289341440 | bytes 34406400 | tf_op jit(solution)/shard_map/ijhd,ikhd->ihjk/dot_general | solution.py:68
  224.0 66.1 %all-reduce.5.cloned.1.call-done = f32[4,32,512]{2,1,0:T(8,128)} async-done(((f32[4,32,512]{2,1,0:T(8,128)}), f32[4,32,512]{2,1,0:T(8,128)}) %all-reduce.5.cloned.1.call-update) | async-done | bytes 262160 | tf_op jit(solution)/shard_map/psum | solution.py:110
  292.1 2.9 copy.123
  295.0 11.6 %fusion.55 = f32[64,4,32,512]{3,2,1,0:T(8,128)} fusion(bf16[64,32,4,32]{1,3,2,0:T(8,128)(2,1)S(1)} %bitcast.127, bf16[64,4,32,512]{3,2,1,0:T(8,128)(2,1)} %fusion.4), kind=kOutput, calls=%fused_computation.85 | convolution fusion | flops 268435456 | bytes 25690112 | tf_op jit(solution)/shard_map/ihjk,ijhd->ikhd/dot_general | solution.py:69
  306.6 8.0 %convolution_multiply_fusion = f32[64,4,32,512]{3,2,1,0:T(8,128)} fusion(bf16[64,32,4,32]{1,3,2,0:T(8,128)(2,1)S(1)} %bitcast.129, bf16[64,4,32,512]{3,2,1,0:T(8,128)(2,1)S(1)} %bitcast.120), kind=kOutput, calls=%fused_computation.6 | convolution fusion | flops 272629760 | bytes 25690112 | tf_op jit(solution)/shard_map/ihjk,ijhd->ikhd/dot_general | solution.py:74
  314.6 20.0 %fusion.45 = f32[64,512,128]{2,1,0:T(8,128)} fusion(f32[64,512,128]{1,2,0:T(8,128)} %bitcast.113, bf16[128,128]{1,0:T(8,128)(2,1)S(1)} %copy-done.8), kind=kOutput, calls=%fused_computation.70 | convolution fusion | flops 6442450944 | bytes 33587200 | tf_op jit(solution)/shard_map/...e,ce->...c/dot_general | solution.py:22
  334.6 22.9 %convolution_add_fusion = f32[64,512,128]{2,1,0:T(8,128)} fusion(f32[64,512,128]{2,1,0:T(8,128)} %fusion.45, f32[64,512,128]{1,2,0:T(8,128)} %bitcast.115, bf16[128,128]{1,0:T(8,128)(2,1)S(1)} %copy-done.10), kind=kOutput, calls=%fused_computation.5 | convolution fusion | flops 6446645248 | bytes 50364416 | tf_op jit(solution)/shard_map/...e,ce->...c/dot_general | solution.py:22
  357.6 3.0 copy.101
  361.6 2.7 convolution_bitcast_fusion
  364.3 8.1 %broadcast_multiply_fusion = f32[64,4,32,32]{3,2,1,0:T(8,128)S(1)} fusion(bf16[64,512,4,32]{1,3,2,0:T(8,128)(2,1)} %bitcast.124, bf16[64,4,32,512]{3,2,1,0:T(8,128)(2,1)} %get-tuple-element.28), kind=kOutput, calls=%fused_computation.18 | convolution fusion | flops 268697600 | bytes 17825792 | tf_op jit(solution)/shard_map/ihjk,ikhd->ijhd/dot_general | solution.py:73
  372.4 3.3 convolution_bitcast_fusion.4
  375.8 4.4 fusion.42
  380.2 18.9 %convolution_bitcast_fusion.3 = f32[128,128]{1,0:T(8,128)} fusion(bf16[64,512,128]{2,1,0:T(8,128)(2,1)} %all-gather.4.cloned.1.call-done, f32[64,512,128]{1,2,0:T(8,128)} %bitcast.114), kind=kOutput, calls=%fused_computation.41 | convolution fusion | flops 6442450944 | bytes 25231360 | tf_op jit(solution)/shard_map/ijc,ijd->cd/dot_general | solution.py:28
  399.1 15.0 %convolution_bitcast_fusion.2 = f32[128,128]{1,0:T(8,128)} fusion(bf16[64,512,128]{2,1,0:T(8,128)(2,1)S(1)} %bitcast.118, f32[64,512,128]{1,2,0:T(8,128)} %bitcast.116), kind=kOutput, calls=%fused_computation.40 | convolution fusion | flops 6442450944 | bytes 25231360 | tf_op jit(solution)/shard_map/ijc,ijd->cd/dot_general | solution.py:28
  415.6 93.6 %reduce-scatter.2.cloned.1.call-done = f32[64,32,128]{2,1,0:T(8,128)} async-done(((f32[64,512,128]{2,1,0:T(8,128)}), f32[64,32,128]{2,1,0:T(8,128)}) %reduce-scatter.2.cloned.1.call-update) | async-done | bytes 1048592 | tf_op jit(solution)/shard_map/reduce_scatter | solution.py:109
  509.2 2.6 fusion.12
  511.8 3.3 fusion.30
  515.1 64.7 %all-reduce = (f32[128]{0:T(128)}, f32[128]{0:T(128)}, f32[128,4]{0,1:T(4,128)}) all-reduce(f32[128]{0:T(128)S(1)} %get-tuple-element.9, f32[128]{0:T(128)S(1)} %get-tuple-element.12, f32[128,4]{0,1:T(4,128)S(1)} %convolution_bitcast_fusion.5), channel_id=1, replica_groups=mesh['row'=8,'col'=16] {'row','col'}, use_global_device_ids=true, to_apply=%region_11.0 | all-reduce | flops 768 | bytes 6144 | tf_op jit(solution)/shard_map/psum | solution.py:126
  581.7 78.8 %all-reduce.7.cloned.1.call-done = (f32[128,128]{1,0:T(8,128)}, f32[128,128]{1,0:T(8,128)}, f32[128,128]{1,0:T(8,128)}, f32[128,128]{1,0:T(8,128)}, f32[128,128]{1,0:T(8,128)}) async-done(((f32[128,128]{1,0:T(8,128)}, f32[128,128]{1,0:T(8,128)}, f32[128,128]{1,0:T(8,128)}, f32[128,128]{1,0:T(8,128)}, f32[128,128]{1,0:T(8,128)}), (f32[128,128]{1,0:T(8,128)}, f32[128,128]{1,0:T(8,128)}, f32[128,128]{1,0:T(8,128)}, ...) | async-done | bytes 327696 | tf_op jit(solution)/shard_map/psum | solution.py:126
  (76 shorter events, 27.2 us)
Async XLA Ops:
  7.2 38.3 %copy-start = (bf16[64,32,128]{2,1,0:T(8,128)(2,1)S(1)}, bf16[64,32,128]{2,1,0:T(8,128)(2,1)}, u32[]{:S(2)}) copy-start(bf16[64,32,128]{2,1,0:T(8,128)(2,1)} %param.11) | copy-start | bytes 1572868
  7.2 38.3 %copy-start.11 = (bf16[128,128]{1,0:T(8,128)(2,1)S(1)}, bf16[128,128]{1,0:T(8,128)(2,1)}, u32[]{:S(2)}) copy-start(bf16[128,128]{1,0:T(8,128)(2,1)} %param.19) | copy-start | bytes 98308
  7.2 68.8 %all-gather.6.cloned.1.call-start = ((), (), s32[]{:S(2)}) async-start(), calls=%async_computation.2 | async-start | bytes 2359296 | tf_op jit(solution)/shard_map/all_gather | solution.py:98
  8.7 42.8 %copy-start.9 = (bf16[128,128]{1,0:T(8,128)(2,1)S(1)}, bf16[128,128]{1,0:T(8,128)(2,1)}, u32[]{:S(2)}) copy-start(bf16[128,128]{1,0:T(8,128)(2,1)} %param.14) | copy-start | bytes 98308
  12.1 31.0 %copy-start.1 = (bf16[64,32,128]{2,1,0:T(8,128)(2,1)}, bf16[64,32,128]{2,1,0:T(8,128)(2,1)S(1)}, u32[]{:S(2)}) copy-start(bf16[64,32,128]{2,1,0:T(8,128)(2,1)S(1)} %fusion.25) | copy-start | bytes 1572868
  43.0 118.0 %all-gather.4.cloned.1.call-start = ((), (), s32[]{:S(2)}) async-start(), calls=%async_computation.1 | async-start | bytes 8912896 | tf_op jit(solution)/shard_map/all_gather | solution.py:101
  43.8 7.8 %copy-start.2 = (bf16[64,32,128]{2,1,0:T(8,128)(2,1)S(1)}, bf16[64,32,128]{2,1,0:T(8,128)(2,1)}, u32[]{:S(2)}) copy-start(bf16[64,32,128]{2,1,0:T(8,128)(2,1)} %copy-done.1) | copy-start | bytes 1572868
  43.8 246.4 %all-reduce.5.cloned.1.call-start = ((), (), s32[]{:S(2)}) async-start(), calls=%async_computation.4 | async-start | bytes 524288 | tf_op jit(solution)/shard_map/psum | solution.py:110
  45.5 1.5 copy-start.3
  45.5 115.5 %copy-start.8 = (bf16[128,128]{1,0:T(8,128)(2,1)S(1)}, bf16[128,128]{1,0:T(8,128)(2,1)}, u32[]{:S(2)}) copy-start(bf16[128,128]{1,0:T(8,128)(2,1)} %param.15) | copy-start | bytes 98308
  181.6 9.4 %copy-start.10 = (bf16[128,128]{1,0:T(8,128)(2,1)S(1)}, bf16[128,128]{1,0:T(8,128)(2,1)}, u32[]{:S(2)}) copy-start(bf16[128,128]{1,0:T(8,128)(2,1)} %param.16) | copy-start | bytes 98308
  200.0 10.1 %copy-start.7 = (f32[64,4,32]{2,1,0:T(4,128)S(1)}, f32[64,4,32]{2,1,0:T(4,128)}, u32[]{:S(2)}) copy-start(f32[64,4,32]{2,1,0:T(4,128)} %get-tuple-element.23) | copy-start | bytes 98308
  224.0 190.2 %all-gather.8.cloned.1.call-start = ((), (), s32[]{:S(2)}) async-start(), calls=%async_computation.5 | async-start | bytes 4456448 | tf_op jit(solution)/shard_map/all_gather | solution.py:111
  292.0 217.2 %reduce-scatter.2.cloned.1.call-start = ((), (), s32[]{:S(2)}) async-start(), calls=%async_computation.3 | async-start | bytes 17825792 | tf_op jit(solution)/shard_map/reduce_scatter | solution.py:109
  295.0 11.6 %slice-start.2 = ((s8[8388608]{0:T(1024)(128)(4,1)}), s8[4194304]{0:T(1024)(128)(4,1)S(1)}, s32[]{:S(2)}) async-start(s8[8388608]{0:T(1024)(128)(4,1)} %bitcast.119), calls=%async_computation.9 | async-start | bytes 8388608
  295.0 11.6 %slice-start.3 = ((s8[8388608]{0:T(1024)(128)(4,1)}), s8[4194304]{0:T(1024)(128)(4,1)S(1)}, s32[]{:S(2)}) async-start(s8[8388608]{0:T(1024)(128)(4,1)} %bitcast.119), calls=%async_computation.10 | async-start | bytes 8388608
  295.0 11.6 %copy-start.5 = (bf16[64,32,128]{1,2,0:T(8,128)(2,1)S(1)}, bf16[64,32,128]{1,2,0:T(8,128)(2,1)}, u32[]{:S(2)}) copy-start(bf16[64,32,128]{1,2,0:T(8,128)(2,1)} %copy.123) | copy-start | bytes 1572868
  357.5 3.1 copy-start.4
  357.5 302.9 %all-reduce.7.cloned.1.call-start = ((), (), s32[]{:S(2)}) async-start(), calls=%async_computation.6 | async-start | bytes 655360 | tf_op jit(solution)/shard_map/psum | solution.py:126
  375.8 23.3 %slice-start = ((s8[8388608]{0:T(1024)(128)(4,1)}), s8[4194304]{0:T(1024)(128)(4,1)S(1)}, s32[]{:S(2)}) async-start(s8[8388608]{0:T(1024)(128)(4,1)} %bitcast.117), calls=%async_computation.7 | async-start | bytes 8388608
  380.2 18.9 %slice-start.1 = ((s8[8388608]{0:T(1024)(128)(4,1)}), s8[4194304]{0:T(1024)(128)(4,1)S(1)}, s32[]{:S(2)}) async-start(s8[8388608]{0:T(1024)(128)(4,1)} %bitcast.117), calls=%async_computation.8 | async-start | bytes 8388608
  399.1 110.1 %copy-start.12 = (bf16[128,128]{1,0:T(8,128)(2,1)S(1)}, bf16[128,128]{1,0:T(8,128)(2,1)}, u32[]{:S(2)}) copy-start(bf16[128,128]{1,0:T(8,128)(2,1)} %param.17) | copy-start | bytes 98308
  399.1 112.7 %copy-start.13 = (f32[128]{0:T(128)S(1)}, f32[128]{0:T(128)}, u32[]{:S(2)}) copy-start(f32[128]{0:T(128)} %param.12) | copy-start | bytes 1540
  399.1 112.7 %copy-start.14 = (bf16[128,4]{0,1:T(4,128)(2,1)S(1)}, bf16[128,4]{0,1:T(4,128)(2,1)}, u32[]{:S(2)}) copy-start(bf16[128,4]{0,1:T(4,128)(2,1)} %param.18) | copy-start | bytes 3076
  415.6 164.2 %copy-start.6 = (bf16[64,32,128]{2,1,0:T(8,128)(2,1)S(1)}, bf16[64,32,128]{2,1,0:T(8,128)(2,1)}, u32[]{:S(2)}) copy-start(bf16[64,32,128]{2,1,0:T(8,128)(2,1)} %param.10) | copy-start | bytes 1572868
Sparse Core Ops, SparseCore 0:
  43.1 32.8 all-gather.5
  78.9 82.1 all-gather.3
  224.1 66.0 all-reduce.4
  293.4 60.3 all-gather.7
  358.5 150.6 reduce-scatter.1
  516.8 143.6 all-reduce.6
where the time goes:
time: 678 us; the launch traced here: 675 us
  waiting for transfers between devices  334 us (49%)
  matrix products  182 us (27%)
  blocking collectives  92.9 us (14%)
  local copies, waits for them, and re-layouts  34.4 us (5%)
  other arithmetic  16.1 us (2%)
  between operations  14.7 us (2%)
    reduce_scatter x1, waiting for transfers between devices, on_device(): lax.psum_scatter(key_terms, 'col', scatter_dimension=1, tiled=True)  93.6 us
    all_gather x1, waiting for transfers between devices, on_device(): x_keys = lax.all_gather(x, 'col', axis=1, tiled=True)  84 us
    psum x1, waiting for transfers between devices, on_device(): lax.psum((dwq, dwk, dwv, dwg, dwb, dwo, dgain, dshift), ('row', 'col'))  78.8 us
    psum x1, waiting for transfers between devices, on_device(): dbias_rows = lax.psum(dbias, 'row')  66.1 us
    psum x1, blocking collectives, on_device(): lax.psum((dwq, dwk, dwv, dwg, dwb, dwo, dgain, dshift), ('row', 'col'))  64.7 us
    dot_general x5, matrix products, project(): jnp.einsum('...e,ce->...c', values, weight.astype(jnp.float32), precision...  53.2 us
    dot_general x5, matrix products, outer_sum(): jnp.einsum('ijc,ijd->cd', inputs.astype(jnp.float32), grads, precision=la...  41.4 us
    all_gather x1, blocking collectives, on_device(): bias_wide = lax.all_gather(tile_bias, 'col', axis=2, tiled=True)  28.2 us
  transfers between devices with their start and end apart: 6, of which 5 were waited for; matrix products, arithmetic and copies ran while one was open for 23% of the time, Pallas kernels for 0%

commit v1 on v0

v1 whole, which is shorter than its diff:
```python
import jax
import jax.numpy as jnp
from jax import lax
from jax.experimental import pallas as pl
from jax.experimental.pallas import tpu as pltpu
from jax.sharding import PartitionSpec as P

H = 4
DH = 32
C = 128
EPS = 1e-05
LOG2E = 1.4426950408889634
F32 = jnp.float32
BF16 = jnp.bfloat16
VMEM_LIMIT = 56 * 1024 * 1024


def dot_nn(a, b):
    return lax.dot_general(a, b, (((1,), (0,)), ((), ())), preferred_element_type=F32)


def dot_nt(a, b):
    return lax.dot_general(a, b, (((1,), (1,)), ((), ())), preferred_element_type=F32)


def dot_tn(a, b):
    return lax.dot_general(a, b, (((0,), (0,)), ((), ())), preferred_element_type=F32)


def normalize(values):
    center = values - jnp.mean(values, axis=-1, keepdims=True)
    rstd = lax.rsqrt(jnp.mean(center * center, axis=-1, keepdims=True) + EPS)
    return center * rstd, rstd


def call(kernel, out_shape, n_in, scratch=(), smem=0):
    specs = [pl.BlockSpec(memory_space=pltpu.SMEM)] * smem
    specs += [pl.BlockSpec(memory_space=pltpu.VMEM)] * n_in
    outs = jax.tree.map(lambda _: pl.BlockSpec(memory_space=pltpu.VMEM), out_shape)
    return pl.pallas_call(
        kernel,
        out_shape=out_shape,
        in_specs=specs,
        out_specs=outs,
        scratch_shapes=list(scratch),
        compiler_params=pltpu.CompilerParams(vmem_limit_bytes=VMEM_LIMIT),
    )


def pack_kernel(pair_ref, grad_ref, gain_ref, shift_ref, wb_ref, out_ref, xt_ref, x_scr, b_scr):
    rows, cols = pair_ref.shape[0], pair_ref.shape[1]
    out_ref[:, 0, 0:cols, :] = pair_ref[...]
    out_ref[:, 1, 0:cols, :] = grad_ref[...]
    normed, _ = normalize(pair_ref[...].reshape(rows * cols, C).astype(F32))
    x_scr[...] = normed * gain_ref[...] + shift_ref[...]
    for k in range(cols):
        xt_ref[k * rows : (k + 1) * rows, :] = x_scr[pl.ds(k, rows, stride=cols), :].astype(BF16)
    bias = dot_nt(wb_ref[...], xt_ref[...])
    for pair in range(2):
        for k in range(cols):
            part = bias[2 * pair : 2 * pair + 2, k * rows : (k + 1) * rows]
            b_scr[k : k + 1, :] = jnp.concatenate([part[0:1], part[1:2]], axis=1)
        packed = b_scr[...].astype(BF16)
        out_ref[:, pair, cols : 2 * cols, :] = jnp.broadcast_to(packed[None], (rows, cols, C))


def attend_kernel(
    core_ref, mine_ref, other_ref, gain_ref, shift_ref, wq_ref, wk_ref, wv_ref, wg_ref, wo_ref,
    out_ref, bias_scr, acc_scr, w_scr, wacc_scr, d_scr,
):
    core = core_ref[0]
    groups, blocks, cols = 8, 16, 32
    n = blocks * cols
    scale = DH ** (-0.5)
    lane = lax.broadcasted_iota(jnp.int32, (n, C), 1)
    low = lane < 64

    for slot, ref in enumerate((wq_ref, wg_ref, wk_ref, wv_ref)):
        turned = jnp.transpose(ref[...].astype(F32)).astype(BF16)
        w_scr[slot * 64 : (slot + 1) * 64, :] = jnp.where(core == 0, turned[0:64], turned[64:128])
    w_scr[256:320, :] = jnp.where(core == 0, wo_ref[0:64, :], wo_ref[64:128, :])

    for r in range(0, groups, 2):
        b0 = mine_ref[r * blocks : (r + 1) * blocks, cols : 2 * cols, :].reshape(n, C).astype(F32)
        b1 = mine_ref[(r + 1) * blocks : (r + 2) * blocks, cols : 2 * cols, :].reshape(n, C)
        b1 = b1.astype(F32)
        sl = slice(r * 64, r * 64 + 128)
        bias_scr[0, :, sl] = jnp.where(low, b0, pltpu.roll(b1, 64, 1)) * LOG2E
        bias_scr[1, :, sl] = jnp.where(low, pltpu.roll(b0, 64, 1), b1) * LOG2E
    acc_scr[...] = jnp.zeros_like(acc_scr)
    wacc_scr[...] = jnp.zeros_like(wacc_scr)

    def one_row(r, carry):
        src = pl.ds(r * blocks, blocks)
        mine = mine_ref[src, 0:cols, :].reshape(n, C)
        other = other_ref[src, :, :].reshape(n, C)
        pair = jnp.where(core == 0, mine, other)
        grad = jnp.where(core == 0, other, mine)
        normed, _ = normalize(pair.astype(F32))
        x = (normed * gain_ref[...] + shift_ref[...]).astype(BF16)
        wide = dot_nt(w_scr[0:256, :], x)
        q_t = wide[0:64].astype(BF16)
        gate = jax.nn.sigmoid(wide[64:128])
        k_t = wide[128:192].astype(BF16)
        v_t = wide[192:256].astype(BF16)
        dgated = dot_nt(w_scr[256:320, :], grad)
        dob_t = (dgated * gate).astype(BF16)
        for h in range(2):
            hs = slice(h * DH, (h + 1) * DH)
            key = dot_nt(x, w_scr[128 + h * DH : 128 + (h + 1) * DH, :]).astype(BF16)
            value = dot_nt(x, w_scr[192 + h * DH : 192 + (h + 1) * DH, :]).astype(BF16)
            s = dot_nn(key, q_t[hs]) * (scale * LOG2E) + bias_scr[h]
            expo = jnp.exp2(s - jnp.max(s, axis=0, keepdims=True))
            probs = expo * (1.0 / jnp.sum(expo, axis=0, keepdims=True))
            probs_b = probs.astype(BF16)
            o_t = dot_nn(v_t[hs], probs_b)
            dob_h = dob_t[hs]
            delta = jnp.sum(dob_h.astype(F32) * o_t, axis=0, keepdims=True)
            ds = probs * (dot_nn(value, dob_h) - delta)
            acc_scr[h] += ds
            ds_b = ds.astype(BF16)
            dg, ga = dgated[hs], gate[hs]
            d_scr[h * DH : (h + 1) * DH, :] = (dot_nn(k_t[hs], ds_b) * scale).astype(BF16)
            d_scr[64 + h * DH : 64 + (h + 1) * DH, :] = (dg * o_t * ga * (1.0 - ga)).astype(BF16)
            d_scr[128 + h * DH : 128 + (h + 1) * DH, :] = (
                dot_nt(q_t[hs], ds_b) * scale
            ).astype(BF16)
            d_scr[192 + h * DH : 192 + (h + 1) * DH, :] = dot_nt(dob_h, probs_b).astype(BF16)
            gated = (ga * o_t).astype(BF16)
            wacc_scr[256 + h * DH : 256 + (h + 1) * DH, :] += dot_nn(gated, grad)
        d = d_scr[...]
        dx = dot_tn(d, w_scr[0:256, :])
        out_ref[src, 0:cols, :] = dx.astype(BF16).reshape(blocks, cols, C)
        wacc_scr[0:256, :] += dot_nn(d, x)
        return carry

    lax.fori_loop(0, groups, one_row, 0)

    for r in range(0, groups, 2):
        sl = slice(r * 64, r * 64 + 128)
        h0, h1 = acc_scr[0, :, sl], acc_scr[1, :, sl]
        b0 = jnp.where(low, h0, pltpu.roll(h1, 64, 1)).astype(BF16)
        b1 = jnp.where(low, pltpu.roll(h0, 64, 1), h1).astype(BF16)
        out_ref[r * blocks : (r + 1) * blocks, cols : 2 * cols, :] = b0.reshape(blocks, cols, C)
        out_ref[(r + 1) * blocks : (r + 2) * blocks, cols : 2 * cols, :] = b1.reshape(
            blocks, cols, C
        )
    for i in range(64):
        part = wacc_scr[5 * i : 5 * i + 8, :]
        high = part.astype(BF16).astype(F32)
        both = jnp.concatenate([high, part - high], axis=0).astype(BF16)
        out_ref[2 * i, 64:80, :] = both
        out_ref[2 * i + 1, 64:80, :] = both


def owner_kernel(
    core_ref, got_ref, pair_ref, xt_ref, gain_ref, wb_ref,
    dpair_ref, sums_ref, z_scr, dxb_scr, wb_scr, s_scr,
):
    core = core_ref[0]
    rows, cols = pair_ref.shape[0], pair_ref.shape[1]
    z_scr[...] = jnp.zeros_like(z_scr)
    wb_scr[...] = jnp.zeros_like(wb_scr)
    wb_scr[0:4, :] = wb_ref[...].astype(F32)
    for pair in range(2):

        def add(i, total, pair=pair):
            return total + got_ref[i, pair, cols : 2 * cols, :].astype(F32)

        total = lax.fori_loop(0, rows, add, jnp.zeros((cols, C), F32), unroll=8)
        for k in range(cols):
            for h in range(2):
                z_scr[2 * pair + h : 2 * pair + h + 1, k * rows : (k + 1) * rows] = total[
                    k : k + 1, h * 64 : (h + 1) * 64
                ]
    z = z_scr[...].astype(BF16)
    dxb_scr[...] = dot_tn(z, wb_scr[...].astype(BF16))
    dwb = dot_nn(z, xt_ref[...])

    def add_w(i, total):
        return total + got_ref[i, core, 64:80, :].astype(F32)

    w = lax.fori_loop(0, rows, add_w, jnp.zeros((16, C), F32), unroll=8)
    gain = gain_ref[...]

    def one(i, carry):
        dgain, dshift = carry
        normed, rstd = normalize(pair_ref[i].astype(F32))
        dx = got_ref[i, 0, 0:cols, :].astype(F32) + got_ref[i, 1, 0:cols, :].astype(F32)
        dx = dx + dxb_scr[pl.ds(i, cols, stride=rows), :]
        dn = dx * gain
        out = rstd * (
            dn
            - jnp.mean(dn, axis=-1, keepdims=True)
            - normed * jnp.mean(dn * normed, axis=-1, keepdims=True)
        )
        dpair_ref[i] = out.astype(BF16)
        return dgain + dx * normed, dshift + dx

    zero = jnp.zeros((cols, C), F32)
    dgain, dshift = lax.fori_loop(0, rows, one, (zero, zero), unroll=8)
    dgain = jnp.sum(dgain, axis=0, keepdims=True)
    dshift = jnp.sum(dshift, axis=0, keepdims=True)
    s_scr[0:8, :] = w[0:8] + w[8:16]
    s_scr[8:12, :] = dwb[0:4]
    s_scr[12:13, :] = dgain
    s_scr[13:14, :] = dshift
    s_scr[14:15, :] = dgain - dgain.astype(BF16).astype(F32)
    s_scr[15:16, :] = dshift - dshift.astype(BF16).astype(F32)
    sums_ref[...] = jnp.broadcast_to(s_scr[...].astype(BF16)[None], sums_ref.shape)


def final_kernel(
    got_ref, dgain_ref, dshift_ref, dq_ref, dk_ref, dv_ref, dg_ref, db_ref, do_ref, w_scr
):
    chips = got_ref.shape[0]
    zero = jnp.zeros((16, C), F32)

    def add(i, total):
        return total + (got_ref[i, 0].astype(F32) + got_ref[i, 1].astype(F32))

    total = lax.fori_loop(0, chips, add, zero, unroll=8)
    db_ref[...] = total[8:12]
    dgain_ref[...] = total[12:13] + total[14:15]
    dshift_ref[...] = total[13:14] + total[15:16]
    for core in range(2):
        for i in range(chips):
            w_scr[core, 5 * i : 5 * i + 8, :] = got_ref[i, core].astype(F32)[0:8]
    for slot, ref in enumerate((dq_ref, dg_ref, dk_ref, dv_ref)):
        sl = slice(slot * 64, (slot + 1) * 64)
        both = jnp.concatenate([w_scr[0, sl, :], w_scr[1, sl, :]], axis=0)
        ref[...] = jnp.transpose(both)
    do_ref[0:64, :] = w_scr[0, 256:320, :]
    do_ref[64:128, :] = w_scr[1, 256:320, :]


def on_device(
    pair, grad_out, norm_gain, norm_shift, w_query, w_key, w_value, w_gate, w_bias, w_out
):
    axes = ("row", "col")
    rows, cols = pair.shape[0], pair.shape[1]
    devices = 2 * rows
    sds = jax.ShapeDtypeStruct
    gain, shift = norm_gain.reshape(1, C), norm_shift.reshape(1, C)
    wb = w_bias.T
    core = (lax.axis_index("col") % 2).astype(jnp.int32).reshape(1)

    packed, xt = call(
        pack_kernel,
        (sds((rows, 2, 64, C), BF16), sds((rows * cols, C), BF16)),
        5,
        (pltpu.VMEM((rows * cols, C), F32), pltpu.VMEM((cols, C), F32)),
    )(pair, grad_out, gain, shift, wb)
    mine = lax.all_to_all(packed.reshape(devices, 64, C), axes, 0, 0, tiled=True)
    swap = [(i, i ^ 1) for i in range(16)]
    other = lax.ppermute(mine[:, 0:cols, :], "col", swap)
    terms = call(
        attend_kernel,
        sds((devices, 80, C), BF16),
        9,
        (
            pltpu.VMEM((2, 512, 512), F32),
            pltpu.VMEM((2, 512, 512), F32),
            pltpu.VMEM((320, C), BF16),
            pltpu.VMEM((328, C), F32),
            pltpu.VMEM((256, 512), BF16),
        ),
        smem=1,
    )(core, mine, other, gain, shift, w_query, w_key, w_value, w_gate, w_out)
    got = lax.all_to_all(terms, axes, 0, 0, tiled=True).reshape(rows, 2, 80, C)
    d_pair, sums = call(
        owner_kernel,
        (sds(pair.shape, BF16), sds((devices, 16, C), BF16)),
        5,
        (
            pltpu.VMEM((8, rows * cols), F32),
            pltpu.VMEM((rows * cols, C), F32),
            pltpu.VMEM((8, C), F32),
            pltpu.VMEM((16, C), F32),
        ),
        smem=1,
    )(core, got, pair, xt, gain, wb)
    all_sums = lax.all_to_all(sums, axes, 0, 0, tiled=True).reshape(rows, 2, 16, C)
    square = sds((C, C), F32)
    d_gain, d_shift, d_query, d_key, d_value, d_gate, d_bias, d_out = call(
        final_kernel,
        (sds((1, C), F32), sds((1, C), F32), square, square, square, square, sds((H, C), F32), square),
        1,
        (pltpu.VMEM((2, 328, C), F32),),
    )(all_sums)
    return (
        d_pair,
        d_gain.reshape(C),
        d_shift.reshape(C),
        d_query,
        d_key,
        d_value,
        d_gate,
        d_bias.T,
        d_out,
    )


def solution(mesh):
    return jax.shard_map(
        on_device,
        mesh=mesh,
        in_specs=(P("row", "col", None), P("row", "col", None)) + (P(),) * 8,
        out_specs=(P("row", "col", None),) + (P(),) * 8,
        check_vma=False,
    )
```

time: 678 us -> 149 us (0.22)
  waiting for transfers between devices: 334 us -> 2.5 us
  matrix products: 182 us -> 0 us
  Pallas kernels: 0 us -> 40.9 us
  local copies, waits for them, and re-layouts: 34.4 us -> 2.22 us
  other arithmetic: 16.1 us -> 0 us
  between operations: 14.7 us -> 0.65 us
  blocking collectives: 92.9 us -> 102 us
    dot_general x22 -> x0, matrix products: 171 us -> none  [the longest x5 53.2 us: project(): jnp.einsum('...e,ce->...c', values, weight.astype(jnp.float32), precision...]
    psum x2 -> x0, waiting for transfers between devices: 145 us -> none  [the longest x1 78.8 us: on_device(): lax.psum((dwq, dwk, dwv, dwg, dwb, dwo, dgain, dshift), ('row', 'col'))]
    all_to_all x0 -> x3, blocking collectives: none -> 102 us  [the longest x1 42 us: on_device(): lax.all_to_all(packed.reshape(devices, 64, C), axes, 0, 0, tiled=True)]
    all_gather x3 -> x0, waiting for transfers between devices: 95 us -> none  [the longest x1 84 us: on_device(): x_keys = lax.all_gather(x, 'col', axis=1, tiled=True)]
    reduce_scatter x1 -> x0, waiting for transfers between devices: 93.6 us -> none  [on_device(): lax.psum_scatter(key_terms, 'col', scatter_dimension=1, tiled=True)]
    psum x1 -> x0, blocking collectives: 64.7 us -> none  [on_device(): lax.psum((dwq, dwk, dwv, dwg, dwb, dwo, dgain, dshift), ('row', 'col'))]
    pallas_call x0 -> x4, Pallas kernels: none -> 40.9 us  [the longest x1 28.6 us: on_device(): call(attend_kernel, sds((devices, 80, C), BF16), 9, (pltpu.VMEM((2, 512,...]
    all_gather x1 -> x0, blocking collectives: 28.2 us -> none  [on_device(): bias_wide = lax.all_gather(tile_bias, 'col', axis=2, tiled=True)]
  transfers between devices with their start and end apart: 6 -> 1, of which waited for: 5 -> 1; matrix products, arithmetic and copies ran while one was open for 23% -> 0% of each run, Pallas kernels for 0% -> 0%
where the time goes in v1:
time: 149 us
  blocking collectives  102 us (68%)
  Pallas kernels  40.9 us (27%)
  waiting for transfers between devices  2.5 us (2%)
  local copies, waits for them, and re-layouts  2.22 us (1%)
    all_to_all x1, blocking collectives, on_device(): lax.all_to_all(packed.reshape(devices, 64, C), axes, 0, 0, tiled=True)  42 us
    all_to_all x1, blocking collectives, on_device(): got = lax.all_to_all(terms, axes, 0, 0, tiled=True).reshape(rows, 2, 80, C)  40.7 us
    pallas_call x1, Pallas kernels, on_device(): call(attend_kernel, sds((devices, 80, C), BF16), 9, (pltpu.VMEM((2, 512,...  28.6 us
    all_to_all x1, blocking collectives, on_device(): lax.all_to_all(sums, axes, 0, 0, tiled=True).reshape(rows, 2, 16, C)  19.1 us
    pallas_call x1, Pallas kernels, on_device(): call(owner_kernel, (sds(pair.shape, BF16), sds((devices, 16, C), BF16)),...  6.22 us
    pallas_call x1, Pallas kernels, on_device(): call(pack_kernel, (sds((rows, 2, 64, C), BF16), sds((rows * cols, C), BF1...  4.07 us
  transfers between devices with their start and end apart: 1, of which 1 were waited for; matrix products, arithmetic and copies ran while one was open for 0% of the time, Pallas kernels for 0%

profile of v1, /device:TPU:1, one launch (start us, length us, event | category | flops | bytes accessed | tf_op | source)
XLA Modules:
  0.0 148.6 jit_solution(4201048783234037539)
XLA Ops:
  0.6 4.1 %shard_map.169 = (bf16[64,2,64,128]{3,2,1,0:T(8,128)(2,1)}, bf16[2048,128]{1,0:T(8,128)(2,1)}) custom-call(bf16[64,32,128]{2,1,0:T(8,128)(2,1)} %pair_ref.3, bf16[64,32,128]{2,1,0:T(8,128)(2,1)} %grad_ref.1, f32[1,128]{1,0:T(1,128)} %bitcast.13, f32[1,128]{1,0:T(1,128)} %bitcast.18, bf16[4,128]{1,0:T(4,128)(2,1)} %bitcast.16), custom_call_target="tpu_custom_call" | custom-call | tf_op jit(solution)/shard_map/pallas_call | solution.py:248
  4.7 42.0 %all_to_all.15.mine_ref = bf16[128,64,128]{2,1,0:T(8,128)(2,1)S(1)} all-to-all(bf16[128,64,128]{2,1,0:T(8,128)(2,1)} %bitcast.11), channel_id=1, replica_groups=mesh['row'=8,'col'=16] {'row','col'}, dimensions={0} | all-to-all | bytes 4194304 | tf_op jit(solution)/shard_map/all_to_all | solution.py:254
  46.7 0.0 copy-start
  46.7 1.2 slice.4
  47.9 0.5 collective-permute-start
  48.4 2.5 %collective-permute-done.other_ref = bf16[128,32,128]{2,1,0:T(8,128)(2,1)S(1)} collective-permute-done((bf16[128,32,128]{2,1,0:T(8,128)(2,1)}, bf16[128,32,128]{2,1,0:T(8,128)(2,1)S(1)}, u32[]{:S(2)}, u32[]{:S(2)}) %collective-permute-start) | collective-permute-done | bytes 1048608 | tf_op jit(solution)/shard_map/ppermute | solution.py:256
  50.9 0.0 copy-start.1
  50.9 0.0 copy-done
  50.9 1.0 copy-done.1
  52.0 28.6 %shard_map.170 = bf16[128,80,128]{2,1,0:T(8,128)(2,1)} custom-call(s32[1]{0:T(128)} %bitcast.core_ref, bf16[128,64,128]{2,1,0:T(8,128)(2,1)} %copy-done, bf16[128,32,128]{2,1,0:T(8,128)(2,1)} %copy-done.1, f32[1,128]{1,0:T(1,128)} %bitcast.14, f32[1,128]{1,0:T(1,128)} %bitcast.19, bf16[128,128]{1,0:T(8,128)(2,1)} %wq_ref.1, bf16[128,128]{1,0:T(8,128)(2,1)} %wk_ref.1, ...), custom_call_target="tpu_custom_call" | custom-call | tf_op jit(solution)/shard_map/pallas_call | solution.py:257
  80.6 40.7 %all_to_all.16 = bf16[128,80,128]{2,1,0:T(8,128)(2,1)} all-to-all(bf16[128,80,128]{2,1,0:T(8,128)(2,1)} %shard_map.170), channel_id=1, replica_groups=mesh['row'=8,'col'=16] {'row','col'}, dimensions={0} | all-to-all | bytes 5242880 | tf_op jit(solution)/shard_map/all_to_all | solution.py:270
  121.3 6.2 %shard_map.171 = (bf16[64,32,128]{2,1,0:T(8,128)(2,1)}, bf16[128,16,128]{2,1,0:T(8,128)(2,1)}) custom-call(s32[1]{0:T(128)} %bitcast.core_ref, bf16[64,2,80,128]{3,2,1,0:T(8,128)(2,1)} %bitcast.10, bf16[64,32,128]{2,1,0:T(8,128)(2,1)} %pair_ref.3, bf16[2048,128]{1,0:T(8,128)(2,1)} %get-tuple-element.22.xt_ref, f32[1,128]{1,0:T(1,128)} %bitcast.15, ...), custom_call_target="tpu_custom_call" | custom-call | tf_op jit(solution)/shard_map/pallas_call | solution.py:271
  127.6 19.1 %all_to_all.17 = bf16[128,16,128]{2,1,0:T(8,128)(2,1)} all-to-all(bf16[128,16,128]{2,1,0:T(8,128)(2,1)} %get-tuple-element.24), channel_id=1, replica_groups=mesh['row'=8,'col'=16] {'row','col'}, dimensions={0} | all-to-all | bytes 1048576 | tf_op jit(solution)/shard_map/all_to_all | solution.py:283
  146.6 2.0 %shard_map.172 = (f32[1,128]{1,0:T(1,128)}, f32[1,128]{1,0:T(1,128)}, f32[128,128]{1,0:T(8,128)}, f32[128,128]{1,0:T(8,128)}, f32[128,128]{1,0:T(8,128)}, /*inde...) custom-call(bf16[64,2,16,128]{3,2,1,0:T(8,128)(2,1)} %bitcast.12), custom_call_target="tpu_custom_call" | custom-call | tf_op jit(solution)/shard_map/pallas_call | solution.py:285
Async XLA Ops:
  46.7 4.2 %copy-start = (bf16[128,64,128]{2,1,0:T(8,128)(2,1)}, bf16[128,64,128]{2,1,0:T(8,128)(2,1)S(1)}, u32[]{:S(2)}) copy-start(bf16[128,64,128]{2,1,0:T(8,128)(2,1)S(1)} %all_to_all.15.mine_ref) | copy-start | bytes 6291460
  47.9 3.0 %collective-permute-start = (bf16[128,32,128]{2,1,0:T(8,128)(2,1)}, bf16[128,32,128]{2,1,0:T(8,128)(2,1)S(1)}, u32[]{:S(2)}, u32[]{:S(2)}) collective-permute-start(bf16[128,32,128]{2,1,0:T(8,128)(2,1)} %slice.4), channel_id=1, source_target_pairs={{0,1},{1,0},{2,3},{3,2},{4,5},{5,4},{6,7},{7,6},{8,9},{9,8},{10,11... | collective-permute-start | bytes 3145736 | tf_op jit(solution)/shard_map/ppermute | solution.py:256
  50.9 1.0 copy-start.1

commit v2 on v1

v2 whole, which is shorter than its diff:
```python
import jax
import jax.numpy as jnp
from jax import lax
from jax.experimental import pallas as pl
from jax.experimental.pallas import tpu as pltpu
from jax.sharding import PartitionSpec as P

H = 4
DH = 32
C = 128
EPS = 1e-05
LOG2E = 1.4426950408889634
F32 = jnp.float32
BF16 = jnp.bfloat16
MIB = 1024 * 1024


def dot_nn(a, b):
    return lax.dot_general(a, b, (((1,), (0,)), ((), ())), preferred_element_type=F32)


def dot_nt(a, b):
    return lax.dot_general(a, b, (((1,), (1,)), ((), ())), preferred_element_type=F32)


def dot_tn(a, b):
    return lax.dot_general(a, b, (((0,), (0,)), ((), ())), preferred_element_type=F32)


def normalize(values):
    center = values - jnp.mean(values, axis=-1, keepdims=True)
    rstd = lax.rsqrt(jnp.mean(center * center, axis=-1, keepdims=True) + EPS)
    return center * rstd, rstd


def call(kernel, out_shape, n_in, scratch=(), smem=0, vmem=16, flops=0, moved=0):
    specs = [pl.BlockSpec(memory_space=pltpu.SMEM)] * smem
    specs += [pl.BlockSpec(memory_space=pltpu.VMEM)] * n_in
    outs = jax.tree.map(lambda _: pl.BlockSpec(memory_space=pltpu.VMEM), out_shape)
    return pl.pallas_call(
        kernel,
        out_shape=out_shape,
        in_specs=specs,
        out_specs=outs,
        scratch_shapes=list(scratch),
        cost_estimate=pl.CostEstimate(flops=flops, bytes_accessed=moved, transcendentals=0),
        compiler_params=pltpu.CompilerParams(vmem_limit_bytes=vmem * MIB),
    )


def pack_kernel(
    pair_ref, grad_ref, gain_ref, shift_ref, wb_ref, out_ref, xt_ref, nt_ref, n_scr, b_scr
):
    rows, cols = pair_ref.shape[0], pair_ref.shape[1]
    out_ref[:, 0, 0:cols, :] = pair_ref[...]
    out_ref[:, 1, 0:cols, :] = grad_ref[...]
    normed, _ = normalize(pair_ref[...].reshape(rows * cols, C).astype(F32))
    n_scr[...] = normed
    for k in range(cols):
        part = n_scr[pl.ds(k, rows, stride=cols), :]
        nt_ref[k * rows : (k + 1) * rows, :] = part.astype(BF16)
        xt_ref[k * rows : (k + 1) * rows, :] = (part * gain_ref[...] + shift_ref[...]).astype(BF16)
    bias = dot_nt(wb_ref[...], xt_ref[...])
    for pair in range(2):
        for k in range(cols):
            part = bias[2 * pair : 2 * pair + 2, k * rows : (k + 1) * rows]
            b_scr[k : k + 1, :] = jnp.concatenate([part[0:1], part[1:2]], axis=1)
        packed = b_scr[...].astype(BF16)
        out_ref[:, pair, cols : 2 * cols, :] = jnp.broadcast_to(packed[None], (rows, cols, C))


def attend_kernel(
    core_ref, mine_ref, other_ref, gain_ref, shift_ref, wq_ref, wk_ref, wv_ref, wg_ref, wo_ref,
    out_ref, norm_ref, bias_scr, acc_scr, w_scr, wacc_scr, d_scr, rhs_scr,
):
    core = core_ref[0]
    groups, blocks, cols, step_rows = 8, 16, 32, 2
    n = blocks * cols
    scale = DH ** (-0.5)
    lane = lax.broadcasted_iota(jnp.int32, (n, C), 1)
    low = lane < 64

    for slot, ref in enumerate((wq_ref, wg_ref, wk_ref, wv_ref)):
        turned = jnp.transpose(ref[...].astype(F32)).astype(BF16)
        w_scr[slot * 64 : (slot + 1) * 64, :] = jnp.where(core == 0, turned[0:64], turned[64:128])
    w_scr[256:320, :] = jnp.where(core == 0, wo_ref[0:64, :], wo_ref[64:128, :])

    for r in range(0, groups, 2):
        b0 = mine_ref[r * blocks : (r + 1) * blocks, cols : 2 * cols, :].reshape(n, C).astype(F32)
        b1 = mine_ref[(r + 1) * blocks : (r + 2) * blocks, cols : 2 * cols, :].reshape(n, C)
        b1 = b1.astype(F32)
        sl = slice(r * 64, r * 64 + 128)
        bias_scr[0, :, sl] = jnp.where(low, b0, pltpu.roll(b1, 64, 1)) * LOG2E
        bias_scr[1, :, sl] = jnp.where(low, pltpu.roll(b0, 64, 1), b1) * LOG2E
    acc_scr[...] = jnp.zeros_like(acc_scr)
    wacc_scr[...] = jnp.zeros_like(wacc_scr)
    rhs_scr[...] = jnp.zeros_like(rhs_scr)
    norm_ref[...] = jnp.zeros_like(norm_ref)

    def some_rows(it, carry):
        held, items = [], []
        for a in range(step_rows):
            src = pl.ds((it * step_rows + a) * blocks, blocks)
            mine = mine_ref[src, 0:cols, :].reshape(n, C)
            other = other_ref[src, :, :].reshape(n, C)
            pair = jnp.where(core == 0, mine, other)
            grad = jnp.where(core == 0, other, mine)
            normed, _ = normalize(pair.astype(F32))
            x = (normed * gain_ref[...] + shift_ref[...]).astype(BF16)
            wide = dot_nt(w_scr[0:256, :], x)
            q_t = wide[0:64].astype(BF16)
            gate = jax.nn.sigmoid(wide[64:128])
            k_t = wide[128:192].astype(BF16)
            v_t = wide[192:256].astype(BF16)
            dgated = dot_nt(w_scr[256:320, :], grad)
            dob_t = (dgated * gate).astype(BF16)
            kv = dot_nt(x, w_scr[128:256, :]).astype(BF16)
            row = dict(src=src, x=x, normed=normed, grad=grad, gate=gate, dgated=dgated, o=[])
            held.append(row)
            for h in range(2):
                hs = slice(h * DH, (h + 1) * DH)
                slot = 4 * a + 2 * h
                rhs_scr[slot, hs, :] = q_t[hs]
                rhs_scr[slot + 1, 64 + h * DH : 64 + (h + 1) * DH, :] = dob_t[hs]
                items.append(
                    dict(a=a, h=h, slot=slot, kv=kv, q=q_t[hs], k=k_t[hs], v=v_t[hs], dob=dob_t[hs])
                )

        def score(t):
            t["s"] = dot_nn(t["kv"], rhs_scr[t["slot"]]) * (scale * LOG2E) + bias_scr[t["h"]]

        def soften(t):
            expo = jnp.exp2(t["s"] - jnp.max(t["s"], axis=0, keepdims=True))
            t["p"] = expo * (1.0 / jnp.sum(expo, axis=0, keepdims=True))
            t["pb"] = t["p"].astype(BF16)

        def apply(t):
            t["o"] = dot_nn(t["v"], t["pb"])
            t["dp"] = dot_nn(t["kv"], rhs_scr[t["slot"] + 1])

        def back(t):
            delta = jnp.sum(t["dob"].astype(F32) * t["o"], axis=0, keepdims=True)
            t["ds"] = t["p"] * (t["dp"] - delta)
            t["dsb"] = t["ds"].astype(BF16)
            t["dv"] = dot_nt(t["dob"], t["pb"])

        def spread(t):
            h, base = t["h"], 256 * t["a"]
            dq = dot_nn(t["k"], t["dsb"]) * scale
            dk = dot_nt(t["q"], t["dsb"]) * scale
            d_scr[base + h * DH : base + (h + 1) * DH, :] = dq.astype(BF16)
            d_scr[base + 128 + h * DH : base + 128 + (h + 1) * DH, :] = dk.astype(BF16)
            d_scr[base + 192 + h * DH : base + 192 + (h + 1) * DH, :] = t["dv"].astype(BF16)

        stages = (score, soften, apply, back, spread)
        for time in range(len(items) + len(stages) - 1):
            for place, t in enumerate(items):
                if 0 <= time - place < len(stages):
                    stages[time - place](t)
        for h in range(2):
            acc_scr[h] += sum(t["ds"] for t in items[1:] if t["h"] == h and t["a"]) + items[h]["ds"]
        for a, row in enumerate(held):
            base = 256 * a
            o_t = jnp.concatenate([items[2 * a]["o"], items[2 * a + 1]["o"]], axis=0)
            gate = row["gate"]
            d_scr[base + 64 : base + 128, :] = (
                row["dgated"] * o_t * gate * (1.0 - gate)
            ).astype(BF16)
            wacc_scr[256:320, :] += dot_nn((gate * o_t).astype(BF16), row["grad"])
            d = d_scr[base : base + 256, :]
            dx = dot_tn(d, w_scr[0:256, :])
            out_ref[row["src"], 0:cols, :] = dx.astype(BF16).reshape(blocks, cols, C)
            wacc_scr[0:256, :] += dot_nn(d, row["x"])
            norm_ref[0:8, :] += jnp.sum((dx * row["normed"]).reshape(64, 8, C), axis=0)
            norm_ref[8:16, :] += jnp.sum(dx.reshape(64, 8, C), axis=0)
        return carry

    lax.fori_loop(0, groups // step_rows, some_rows, 0)

    for r in range(0, groups, 2):
        sl = slice(r * 64, r * 64 + 128)
        h0, h1 = acc_scr[0, :, sl], acc_scr[1, :, sl]
        b0 = jnp.where(low, h0, pltpu.roll(h1, 64, 1)).astype(BF16)
        b1 = jnp.where(low, pltpu.roll(h0, 64, 1), h1).astype(BF16)
        out_ref[r * blocks : (r + 1) * blocks, cols : 2 * cols, :] = b0.reshape(blocks, cols, C)
        out_ref[(r + 1) * blocks : (r + 2) * blocks, cols : 2 * cols, :] = b1.reshape(
            blocks, cols, C
        )
    for i in range(64):
        part = wacc_scr[5 * i : 5 * i + 8, :].astype(BF16)
        out_ref[2 * i, 64:72, :] = part
        out_ref[2 * i + 1, 64:72, :] = part


def sums_kernel(
    core_ref, got_ref, xt_ref, nt_ref, norm_ref, wb_ref, z_ref, sums_ref, z_scr, s_scr
):
    core = core_ref[0]
    rows, cols = got_ref.shape[0], 32
    z_scr[...] = jnp.zeros_like(z_scr)
    for pair in range(2):

        def add(i, total, pair=pair):
            return total + got_ref[i, pair, cols : 2 * cols, :].astype(F32)

        total = lax.fori_loop(0, rows, add, jnp.zeros((cols, C), F32), unroll=8)
        for k in range(cols):
            for h in range(2):
                z_scr[2 * pair + h : 2 * pair + h + 1, k * rows : (k + 1) * rows] = total[
                    k : k + 1, h * 64 : (h + 1) * 64
                ]
    z = z_scr[...].astype(BF16)
    z_ref[...] = z
    dwb = dot_nn(z, xt_ref[...])
    dgn = dot_nn(z, nt_ref[...])

    def add_w(i, total):
        return total + got_ref[i, core, 64:72, :].astype(F32)

    s_scr[0:8, :] = lax.fori_loop(0, rows, add_w, jnp.zeros((8, C), F32), unroll=8)
    s_scr[8:12, :] = dwb[0:4]
    wb = wb_ref[...].astype(F32)
    dgain = jnp.sum(norm_ref[0:8, :], axis=0, keepdims=True)
    dgain = dgain + jnp.sum(dgn[0:4] * wb, axis=0, keepdims=True)
    dshift = jnp.sum(norm_ref[8:16, :], axis=0, keepdims=True)
    total = jnp.sum(z_scr[0:4, :], axis=1, keepdims=True)
    dshift = dshift + jnp.sum(total * wb, axis=0, keepdims=True)
    s_scr[12:13, :] = dgain
    s_scr[13:14, :] = dshift
    s_scr[14:15, :] = dgain - dgain.astype(BF16).astype(F32)
    s_scr[15:16, :] = dshift - dshift.astype(BF16).astype(F32)
    sums_ref[...] = jnp.broadcast_to(s_scr[...].astype(BF16)[None], sums_ref.shape)


def owner_kernel(got_ref, z_ref, pair_ref, gain_ref, wb_ref, dpair_ref, dxb_scr, wb_scr):
    rows, cols = pair_ref.shape[0], pair_ref.shape[1]
    wb_scr[...] = jnp.zeros_like(wb_scr)
    wb_scr[0:4, :] = wb_ref[...].astype(F32)
    dxb_scr[...] = dot_tn(z_ref[...], wb_scr[...].astype(BF16))
    gain = gain_ref[...]

    def some(it, carry):
        i0 = it * 8
        normed, rstd = normalize(pair_ref[pl.ds(i0, 8)].astype(F32))
        dx = got_ref[pl.ds(i0, 8), 0, 0:cols, :].astype(F32)
        dx = dx + got_ref[pl.ds(i0, 8), 1, 0:cols, :].astype(F32)
        parts = [dxb_scr[pl.ds(i0 + u, cols, stride=rows), :][None] for u in range(8)]
        dn = (dx + jnp.concatenate(parts, axis=0)) * gain
        out = rstd * (
            dn
            - jnp.mean(dn, axis=-1, keepdims=True)
            - normed * jnp.mean(dn * normed, axis=-1, keepdims=True)
        )
        dpair_ref[pl.ds(i0, 8)] = out.astype(BF16)
        return carry

    lax.fori_loop(0, rows // 8, some, 0)


def final_kernel(
    got_ref, dgain_ref, dshift_ref, dq_ref, dk_ref, dv_ref, dg_ref, db_ref, do_ref, w_scr
):
    chips = got_ref.shape[0]
    zero = jnp.zeros((16, C), F32)

    def add(i, total):
        return total + (got_ref[i, 0].astype(F32) + got_ref[i, 1].astype(F32))

    total = lax.fori_loop(0, chips, add, zero, unroll=8)
    db_ref[...] = total[8:12]
    dgain_ref[...] = total[12:13] + total[14:15]
    dshift_ref[...] = total[13:14] + total[15:16]
    for core in range(2):
        for i in range(chips):
            w_scr[core, 5 * i : 5 * i + 8, :] = got_ref[i, core].astype(F32)[0:8]
    for slot, ref in enumerate((dq_ref, dg_ref, dk_ref, dv_ref)):
        sl = slice(slot * 64, (slot + 1) * 64)
        both = jnp.concatenate([w_scr[0, sl, :], w_scr[1, sl, :]], axis=0)
        ref[...] = jnp.transpose(both)
    do_ref[0:64, :] = w_scr[0, 256:320, :]
    do_ref[64:128, :] = w_scr[1, 256:320, :]


def on_device(
    pair, grad_out, norm_gain, norm_shift, w_query, w_key, w_value, w_gate, w_bias, w_out
):
    axes = ("row", "col")
    rows, cols = pair.shape[0], pair.shape[1]
    devices = 2 * rows
    sds = jax.ShapeDtypeStruct
    gain, shift = norm_gain.reshape(1, C), norm_shift.reshape(1, C)
    wb = w_bias.T
    core = (lax.axis_index("col") % 2).astype(jnp.int32).reshape(1)

    turned = sds((rows * cols, C), BF16)
    packed, xt, nt = call(
        pack_kernel,
        (sds((rows, 2, 64, C), BF16), turned, turned),
        5,
        (pltpu.VMEM((rows * cols, C), F32), pltpu.VMEM((cols, C), F32)),
        flops=10**8,
        moved=4 * MIB,
    )(pair, grad_out, gain, shift, wb)
    mine = lax.all_to_all(packed.reshape(devices, 64, C), axes, 0, 0, tiled=True)
    swap = [(i, i ^ 1) for i in range(16)]
    other = lax.ppermute(mine[:, 0:cols, :], "col", swap)
    terms, norms = call(
        attend_kernel,
        (sds((devices, 72, C), BF16), sds((16, C), F32)),
        9,
        (
            pltpu.VMEM((2, 512, 512), F32),
            pltpu.VMEM((2, 512, 512), F32),
            pltpu.VMEM((320, C), BF16),
            pltpu.VMEM((328, C), F32),
            pltpu.VMEM((512, 512), BF16),
            pltpu.VMEM((8, C, 512), BF16),
        ),
        smem=1,
        vmem=32,
        flops=10**10,
        moved=6 * MIB,
    )(core, mine, other, gain, shift, w_query, w_key, w_value, w_gate, w_out)
    got = lax.all_to_all(terms, axes, 0, 0, tiled=True).reshape(rows, 2, 72, C)
    z, sums = call(
        sums_kernel,
        (sds((8, rows * cols), BF16), sds((devices, 16, C), BF16)),
        5,
        (pltpu.VMEM((8, rows * cols), F32), pltpu.VMEM((16, C), F32)),
        smem=1,
        flops=10**8,
        moved=4 * MIB,
    )(core, got, xt, nt, norms, wb)
    all_sums = lax.all_to_all(sums, axes, 0, 0, tiled=True).reshape(rows, 2, 16, C)
    d_pair = call(
        owner_kernel,
        sds(pair.shape, BF16),
        5,
        (pltpu.VMEM((rows * cols, C), F32), pltpu.VMEM((8, C), F32)),
        flops=10**8,
        moved=8 * MIB,
    )(got, z, pair, gain, wb)
    square = sds((C, C), F32)
    d_gain, d_shift, d_query, d_key, d_value, d_gate, d_bias, d_out = call(
        final_kernel,
        (sds((1, C), F32), sds((1, C), F32), square, square, square, square, sds((H, C), F32), square),
        1,
        (pltpu.VMEM((2, 328, C), F32),),
        moved=MIB,
    )(all_sums)
    return (
        d_pair,
        d_gain.reshape(C),
        d_shift.reshape(C),
        d_query,
        d_key,
        d_value,
        d_gate,
        d_bias.T,
        d_out,
    )


def solution(mesh):
    return jax.shard_map(
        on_device,
        mesh=mesh,
        in_specs=(P("row", "col", None), P("row", "col", None)) + (P(),) * 8,
        out_specs=(P("row", "col", None),) + (P(),) * 8,
        check_vma=False,
    )
```

time: 149 us -> 131 us (0.88)
  blocking collectives: 102 us -> 79 us
  Pallas kernels: 40.9 us -> 26.1 us
  waiting for transfers between devices: 2.5 us -> 13.1 us
  starting transfers between devices: 0.55 us -> 5.08 us
  local copies, waits for them, and re-layouts: 2.22 us -> 6.02 us
    all_to_all x2 -> x1, blocking collectives: 59.8 us -> 37.2 us  [on_device(): got = lax.all_to_all(terms, axes, 0, 0, tiled=True).reshape(rows, 2, 72, C)]
    pallas_call x3 -> x4, Pallas kernels: 38.9 us -> 25.1 us  [the longest x1 19.2 us: on_device(): call(attend_kernel, (sds((devices, 72, C), BF16), sds((16, C), F32)), 9,...]
    all_to_all x0 -> x1, waiting for transfers between devices: none -> 10.4 us  [on_device(): lax.all_to_all(sums, axes, 0, 0, tiled=True).reshape(rows, 2, 16, C)]
    all_to_all x0 -> x1, starting transfers between devices: none -> 4.53 us  [on_device(): lax.all_to_all(sums, axes, 0, 0, tiled=True).reshape(rows, 2, 16, C)]
    unnamed x4 -> x34, local copies, waits for them, and re-layouts: 1.02 us -> 4.93 us
  transfers between devices with their start and end apart: 1 -> 2, of which waited for: 1 -> 2; matrix products, arithmetic and copies ran while one was open for 0% -> 0% of each run, Pallas kernels for 0% -> 3%
where the time goes in v2:
time: 131 us; the launch traced here: 130 us
  blocking collectives  79 us (60%)
  Pallas kernels  26.1 us (20%)
  waiting for transfers between devices  13.1 us (10%)
  local copies, waits for them, and re-layouts  6.02 us (5%)
  starting transfers between devices  5.08 us (4%)
    all_to_all x1, blocking collectives, on_device(): lax.all_to_all(packed.reshape(devices, 64, C), axes, 0, 0, tiled=True)  41.8 us
    all_to_all x1, blocking collectives, on_device(): got = lax.all_to_all(terms, axes, 0, 0, tiled=True).reshape(rows, 2, 72, C)  37.2 us
    pallas_call x1, Pallas kernels, on_device(): call(attend_kernel, (sds((devices, 72, C), BF16), sds((16, C), F32)), 9,...  19.2 us
    all_to_all x1, waiting for transfers between devices, on_device(): lax.all_to_all(sums, axes, 0, 0, tiled=True).reshape(rows, 2, 16, C)  10.4 us
    unnamed x34, local copies, waits for them, and re-layouts  4.93 us
    all_to_all x1, starting transfers between devices, on_device(): lax.all_to_all(sums, axes, 0, 0, tiled=True).reshape(rows, 2, 16, C)  4.53 us
    pallas_call x1, Pallas kernels, on_device(): call(owner_kernel, sds(pair.shape, BF16), 5, (pltpu.VMEM((rows * cols, C)...  3.39 us
    ppermute x1, waiting for transfers between devices, on_device(): other = lax.ppermute(mine[:, 0:cols, :], 'col', swap)  2.63 us
  transfers between devices with their start and end apart: 2, of which 2 were waited for; matrix products, arithmetic and copies ran while one was open for 0% of the time, Pallas kernels for 3%

profile of v2, /device:TPU:1, one launch (start us, length us, event | category | flops | bytes accessed | tf_op | source)
XLA Modules:
  0.0 130.1 jit_solution(6620779215726958808)
XLA Ops:
  0.6 0.0 copy-start
  0.7 1.0 copy-done
  1.7 1.0 copy-done.2
  2.7 0.7 copy-done.6
  3.4 0.7 copy-done.8
  4.1 0.7 copy-done.10
  4.7 1.6 %shard_map.169 = (bf16[64,2,64,128]{3,2,1,0:T(8,128)(2,1)S(1)}, bf16[2048,128]{1,0:T(8,128)(2,1)S(1)}, bf16[2048,128]{1,0:T(8,128)(2,1)S(1)}) custom-call(bf16[64,32,128]{2,1,0:T(8,128)(2,1)S(1)} %copy-done, bf16[64,32,128]{2,1,0:T(8,128)(2,1)S(1)} %copy-done.2, f32[1,128]{1,0:T(1,128)S(1)} %bitcast.17, f32[1,128]{1,0:T(1,128)S(1)} %bitcast.20, ...), custom_call_target="tpu_custom_call" | custom-call | flops 100000000 | bytes 4194304 | tf_op jit(solution)/shard_map/pallas_call | solution.py:296
  6.4 0.0 copy-start.4
  6.4 0.0 copy-start.9
  6.4 0.0 copy-start.11
  6.4 0.0 copy-start.12
  6.4 0.0 copy-start.13
  6.4 0.0 copy-start.14
  6.4 0.0 copy-start.15
  6.5 0.0 copy-start.16
  6.5 41.8 %all_to_all.15.mine_ref = bf16[128,64,128]{2,1,0:T(8,128)(2,1)S(1)} all-to-all(bf16[128,64,128]{2,1,0:T(8,128)(2,1)S(1)} %bitcast.12), channel_id=1, replica_groups=mesh['row'=8,'col'=16] {'row','col'}, dimensions={0} | all-to-all | bytes 4194304 | tf_op jit(solution)/shard_map/all_to_all | solution.py:304
  48.2 1.1 slice.4
  49.4 0.5 collective-permute-start
  49.9 2.6 %collective-permute-done.other_ref = bf16[128,32,128]{2,1,0:T(8,128)(2,1)} collective-permute-done((bf16[128,32,128]{2,1,0:T(8,128)(2,1)}, bf16[128,32,128]{2,1,0:T(8,128)(2,1)}, u32[]{:S(2)}, u32[]{:S(2)}) %collective-permute-start) | collective-permute-done | bytes 1048608 | tf_op jit(solution)/shard_map/ppermute | solution.py:306
  52.5 0.0 copy-done.13
  52.5 0.0 copy-done.14
  52.5 0.0 copy-done.15
  52.6 19.2 %shard_map.170 = (bf16[128,72,128]{2,1,0:T(8,128)(2,1)S(1)}, f32[16,128]{1,0:T(8,128)S(1)}) custom-call(s32[1]{0:T(128)} %bitcast.core_ref, bf16[128,64,128]{2,1,0:T(8,128)(2,1)S(1)} %all_to_all.15.mine_ref, bf16[128,32,128]{2,1,0:T(8,128)(2,1)} %collective-permute-done.other_ref, f32[1,128]{1,0:T(1,128)S(1)} %bitcast.18, f32[1,128]{1,0:T(1,128)S(1)} %bitcast.21, ...), custom_call_target="tpu_custom_call" | custom-call | flops 10000000000 | bytes 6291456 | tf_op jit(solution)/shard_map/pallas_call | solution.py:307
  71.8 0.0 copy-start.5
  71.8 0.0 copy-start.7
  71.8 37.2 %all_to_all.16 = bf16[128,72,128]{2,1,0:T(8,128)(2,1)S(1)} all-to-all(bf16[128,72,128]{2,1,0:T(8,128)(2,1)S(1)} %get-tuple-element.25), channel_id=1, replica_groups=mesh['row'=8,'col'=16] {'row','col'}, dimensions={0} | all-to-all | bytes 4718592 | tf_op jit(solution)/shard_map/all_to_all | solution.py:324
  109.1 0.9 shard_map.171
  110.0 0.8 copy-done.3
  110.8 4.5 %all-to-all-start.2 = ((bf16[128,16,128]{2,1,0:T(8,128)(2,1)}), bf16[128,16,128]{2,1,0:T(8,128)(2,1)S(1)}, u32[]{:S(2)}, u32[]{:S(2)}) async-start(bf16[128,16,128]{2,1,0:T(8,128)(2,1)} %copy-done.3), calls=%async_computation.2 | async-start | bytes 1048576 | tf_op jit(solution)/shard_map/all_to_all | solution.py:334
  115.3 3.4 %shard_map.172 = bf16[64,32,128]{2,1,0:T(8,128)(2,1)} custom-call(bf16[64,2,72,128]{3,2,1,0:T(8,128)(2,1)S(1)} %bitcast.11, bf16[8,2048]{1,0:T(8,128)(2,1)S(1)} %get-tuple-element.29.z_ref, bf16[64,32,128]{2,1,0:T(8,128)(2,1)S(1)} %copy-done.1, f32[1,128]{1,0:T(1,128)S(1)} %bitcast.19, bf16[4,128]{1,0:T(4,128)(2,1)S(1)} %bitcast.16), custom_call_target="tpu_custom_call" | custom-call | flops 100000000 | bytes 8388608 | tf_op jit(solution)/shard_map/pallas_call | solution.py:335
  118.7 10.4 %all-to-all-done.2 = bf16[128,16,128]{2,1,0:T(8,128)(2,1)S(1)} async-done(((bf16[128,16,128]{2,1,0:T(8,128)(2,1)}), bf16[128,16,128]{2,1,0:T(8,128)(2,1)S(1)}, u32[]{:S(2)}, u32[]{:S(2)}) %all-to-all-start.2) | async-done | bytes 524320 | tf_op jit(solution)/shard_map/all_to_all | solution.py:334
  129.2 0.9 shard_map.173
  (14 shorter events, 0.0 us)
Async XLA Ops:
  0.6 1.0 copy-start
  1.7 1.0 copy-start.2
  2.7 0.7 copy-start.6
  3.4 0.7 copy-start.8
  4.1 0.7 copy-start.10
  6.4 43.0 %copy-start.4 = (bf16[2048,128]{1,0:T(8,128)(2,1)}, bf16[2048,128]{1,0:T(8,128)(2,1)S(1)}, u32[]{:S(2)}) copy-start(bf16[2048,128]{1,0:T(8,128)(2,1)S(1)} %get-tuple-element.27.nt_ref) | copy-start | bytes 1572868
  6.4 46.1 %copy-start.9 = (f32[128]{0:T(128)S(1)}, f32[128]{0:T(128)}, u32[]{:S(2)}) copy-start(f32[128]{0:T(128)} %param.12) | copy-start | bytes 1540
  6.4 46.1 %copy-start.11 = (f32[128]{0:T(128)S(1)}, f32[128]{0:T(128)}, u32[]{:S(2)}) copy-start(f32[128]{0:T(128)} %param.13) | copy-start | bytes 1540
  6.4 46.1 %copy-start.12 = (bf16[128,128]{1,0:T(8,128)(2,1)S(1)}, bf16[128,128]{1,0:T(8,128)(2,1)}, u32[]{:S(2)}) copy-start(bf16[128,128]{1,0:T(8,128)(2,1)} %wq_ref.1) | copy-start | bytes 98308
  6.4 46.1 %copy-start.13 = (bf16[128,128]{1,0:T(8,128)(2,1)S(1)}, bf16[128,128]{1,0:T(8,128)(2,1)}, u32[]{:S(2)}) copy-start(bf16[128,128]{1,0:T(8,128)(2,1)} %wk_ref.1) | copy-start | bytes 98308
  6.4 46.1 %copy-start.14 = (bf16[128,128]{1,0:T(8,128)(2,1)S(1)}, bf16[128,128]{1,0:T(8,128)(2,1)}, u32[]{:S(2)}) copy-start(bf16[128,128]{1,0:T(8,128)(2,1)} %wv_ref.1) | copy-start | bytes 98308
  6.4 46.1 %copy-start.15 = (bf16[128,128]{1,0:T(8,128)(2,1)S(1)}, bf16[128,128]{1,0:T(8,128)(2,1)}, u32[]{:S(2)}) copy-start(bf16[128,128]{1,0:T(8,128)(2,1)} %wg_ref.1) | copy-start | bytes 98308
  6.5 46.1 %copy-start.16 = (bf16[128,128]{1,0:T(8,128)(2,1)S(1)}, bf16[128,128]{1,0:T(8,128)(2,1)}, u32[]{:S(2)}) copy-start(bf16[128,128]{1,0:T(8,128)(2,1)} %wo_ref.1) | copy-start | bytes 98308
  49.4 3.2 %collective-permute-start = (bf16[128,32,128]{2,1,0:T(8,128)(2,1)}, bf16[128,32,128]{2,1,0:T(8,128)(2,1)}, u32[]{:S(2)}, u32[]{:S(2)}) collective-permute-start(bf16[128,32,128]{2,1,0:T(8,128)(2,1)} %slice.4), channel_id=1, source_target_pairs={{0,1},{1,0},{2,3},{3,2},{4,5},{5,4},{6,7},{7,6},{8,9},{9,8},{10,11... | collective-permute-start | bytes 3145736 | tf_op jit(solution)/shard_map/ppermute | solution.py:306
  71.8 37.3 %copy-start.5 = (bf16[2048,128]{1,0:T(8,128)(2,1)S(1)}, bf16[2048,128]{1,0:T(8,128)(2,1)}, u32[]{:S(2)}) copy-start(bf16[2048,128]{1,0:T(8,128)(2,1)} %copy-done.4) | copy-start | bytes 1572868
  71.8 37.3 %copy-start.7 = (bf16[128,4]{0,1:T(4,128)(2,1)S(1)}, bf16[128,4]{0,1:T(4,128)(2,1)}, u32[]{:S(2)}) copy-start(bf16[128,4]{0,1:T(4,128)(2,1)} %param.18) | copy-start | bytes 3076
  109.1 6.2 %copy-start.1 = (bf16[64,32,128]{2,1,0:T(8,128)(2,1)S(1)}, bf16[64,32,128]{2,1,0:T(8,128)(2,1)}, u32[]{:S(2)}) copy-start(bf16[64,32,128]{2,1,0:T(8,128)(2,1)} %pair_ref.3) | copy-start | bytes 1572868
  110.0 0.8 copy-start.3
  110.8 18.4 %all-to-all-start.2 = ((bf16[128,16,128]{2,1,0:T(8,128)(2,1)}), bf16[128,16,128]{2,1,0:T(8,128)(2,1)S(1)}, u32[]{:S(2)}, u32[]{:S(2)}) async-start(bf16[128,16,128]{2,1,0:T(8,128)(2,1)} %copy-done.3), calls=%async_computation.2 | async-start | bytes 1048576 | tf_op jit(solution)/shard_map/all_to_all | solution.py:334

commit v3 on v2

v3 whole, which is shorter than its diff:
```python
import jax
import jax.numpy as jnp
from jax import lax
from jax.experimental import pallas as pl
from jax.experimental.pallas import tpu as pltpu
from jax.sharding import PartitionSpec as P

H = 4
DH = 32
C = 128
EPS = 1e-05
LOG2E = 1.4426950408889634
F32 = jnp.float32
BF16 = jnp.bfloat16
MIB = 1024 * 1024


def dot_nn(a, b):
    return lax.dot_general(a, b, (((1,), (0,)), ((), ())), preferred_element_type=F32)


def dot_nt(a, b):
    return lax.dot_general(a, b, (((1,), (1,)), ((), ())), preferred_element_type=F32)


def dot_tn(a, b):
    return lax.dot_general(a, b, (((0,), (0,)), ((), ())), preferred_element_type=F32)


def normalize(values):
    center = values - jnp.mean(values, axis=-1, keepdims=True)
    rstd = lax.rsqrt(jnp.mean(center * center, axis=-1, keepdims=True) + EPS)
    return center * rstd, rstd


def call(
    kernel, out_shape, n_in, scratch=(), smem=0, hbm=0, to_hbm=(), vmem=16, flops=0, moved=0
):
    specs = [pl.BlockSpec(memory_space=pltpu.SMEM)] * smem
    specs += [pl.BlockSpec(memory_space=pltpu.HBM)] * hbm
    specs += [pl.BlockSpec(memory_space=pltpu.VMEM)] * n_in
    many = isinstance(out_shape, tuple)
    shapes = out_shape if many else (out_shape,)
    spaces = [pltpu.HBM if i in to_hbm else pltpu.VMEM for i in range(len(shapes))]
    outs = [pl.BlockSpec(memory_space=space) for space in spaces]
    outs = tuple(outs) if many else outs[0]
    return pl.pallas_call(
        kernel,
        out_shape=out_shape,
        in_specs=specs,
        out_specs=outs,
        scratch_shapes=list(scratch),
        cost_estimate=pl.CostEstimate(flops=flops, bytes_accessed=moved, transcendentals=0),
        compiler_params=pltpu.CompilerParams(vmem_limit_bytes=vmem * MIB),
    )


def in_hbm(array):
    return pltpu.with_memory_space_constraint(array, pltpu.HBM)


def pack_kernel(
    pair_hbm, grad_hbm, gain_hbm, shift_hbm, wb_hbm,
    out_ref, xt_ref, nt_ref, n_scr, b_scr, gain_scr, shift_scr, wb_scr, sems,
):
    rows, cols = pair_hbm.shape[0], pair_hbm.shape[1]
    copies = [
        pltpu.make_async_copy(src, dst, sems.at[i])
        for i, (src, dst) in enumerate(
            (
                (pair_hbm, out_ref.at[:, 0, 0:cols, :]),
                (gain_hbm, gain_scr),
                (shift_hbm, shift_scr),
                (wb_hbm, wb_scr),
                (grad_hbm, out_ref.at[:, 1, 0:cols, :]),
            )
        )
    ]
    for copy in copies:
        copy.start()
    for copy in copies[:-1]:
        copy.wait()
    normed, _ = normalize(out_ref[:, 0, 0:cols, :].reshape(rows * cols, C).astype(F32))
    n_scr[...] = normed
    for k in range(cols):
        part = n_scr[pl.ds(k, rows, stride=cols), :]
        nt_ref[k * rows : (k + 1) * rows, :] = part.astype(BF16)
        xt_ref[k * rows : (k + 1) * rows, :] = (part * gain_scr[...] + shift_scr[...]).astype(BF16)
    bias = dot_nt(wb_scr[...], xt_ref[...])
    for pair in range(2):
        for k in range(cols):
            part = bias[2 * pair : 2 * pair + 2, k * rows : (k + 1) * rows]
            b_scr[k : k + 1, :] = jnp.concatenate([part[0:1], part[1:2]], axis=1)
        packed = b_scr[...].astype(BF16)
        out_ref[:, pair, cols : 2 * cols, :] = jnp.broadcast_to(packed[None], (rows, cols, C))
    copies[-1].wait()


def attend_kernel(
    core_ref, mine_ref, other_ref, gain_ref, shift_ref, wq_ref, wk_ref, wv_ref, wg_ref, wo_ref,
    out_hbm, d_hbm, w_scr, bias_scr, acc_scr, wacc_scr, rhs_scr, out_ref, d_ref, sems, d_sems,
):
    core = core_ref[0]
    groups, blocks, cols, step_rows = 8, 16, 32, 4
    n = blocks * cols
    scale = DH ** (-0.5)
    lane = lax.broadcasted_iota(jnp.int32, (n, C), 1)
    low = lane < 64

    for slot, ref in enumerate((wq_ref, wg_ref, wk_ref, wv_ref)):
        turned = jnp.transpose(ref[...].astype(F32)).astype(BF16)
        w_scr[slot * 64 : (slot + 1) * 64, :] = jnp.where(core == 0, turned[0:64], turned[64:128])
    w_scr[256:320, :] = jnp.where(core == 0, wo_ref[0:64, :], wo_ref[64:128, :])

    for r in range(0, groups, 2):
        b0 = mine_ref[r * blocks : (r + 1) * blocks, cols : 2 * cols, :].reshape(n, C).astype(F32)
        b1 = mine_ref[(r + 1) * blocks : (r + 2) * blocks, cols : 2 * cols, :].reshape(n, C)
        b1 = b1.astype(F32)
        sl = slice(r * 64, r * 64 + 128)
        bias_scr[0, :, sl] = jnp.where(low, b0, pltpu.roll(b1, 64, 1)) * LOG2E
        bias_scr[1, :, sl] = jnp.where(low, pltpu.roll(b0, 64, 1), b1) * LOG2E
    acc_scr[...] = jnp.zeros_like(acc_scr)
    wacc_scr[...] = jnp.zeros_like(wacc_scr)
    rhs_scr[...] = jnp.zeros_like(rhs_scr)

    def some_rows(it, carry):
        def prepare(a, row, items):
            src = pl.ds((it * step_rows + a) * blocks, blocks)
            mine = mine_ref[src, 0:cols, :].reshape(n, C)
            other = other_ref[src, :, :].reshape(n, C)
            pair = jnp.where(core == 0, mine, other)
            grad = jnp.where(core == 0, other, mine)
            normed, _ = normalize(pair.astype(F32))
            x = (normed * gain_ref[...] + shift_ref[...]).astype(BF16)
            wide = dot_nt(w_scr[0:256, :], x)
            q_t = wide[0:64].astype(BF16)
            gate = jax.nn.sigmoid(wide[64:128])
            k_t = wide[128:192].astype(BF16)
            v_t = wide[192:256].astype(BF16)
            dgated = dot_nt(w_scr[256:320, :], grad)
            dob_t = (dgated * gate).astype(BF16)
            kv = dot_nt(x, w_scr[128:256, :]).astype(BF16)
            row.update(x=x, grad=grad, gate=gate, dgated=dgated)
            for h in range(2):
                hs = slice(h * DH, (h + 1) * DH)
                slot = 4 * a + 2 * h
                rhs_scr[slot, hs, :] = q_t[hs]
                rhs_scr[slot + 1, 64 + h * DH : 64 + (h + 1) * DH, :] = dob_t[hs]
                items[h].update(a=a, h=h, slot=slot, kv=kv)
                items[h].update(q=q_t[hs], k=k_t[hs], v=v_t[hs], dob=dob_t[hs])

        def score(t):
            t["s"] = dot_nn(t["kv"], rhs_scr[t["slot"]]) * (scale * LOG2E) + bias_scr[t["h"]]

        def soften(t):
            expo = jnp.exp2(t["s"] - jnp.max(t["s"], axis=0, keepdims=True))
            t["p"] = expo * (1.0 / jnp.sum(expo, axis=0, keepdims=True))
            t["pb"] = t["p"].astype(BF16)

        def apply(t):
            t["o"] = dot_nn(t["v"], t["pb"])
            t["dp"] = dot_nn(t["kv"], rhs_scr[t["slot"] + 1])

        def back(t):
            delta = jnp.sum(t["dob"].astype(F32) * t["o"], axis=0, keepdims=True)
            ds = t["p"] * (t["dp"] - delta)
            t["dsb"] = ds.astype(BF16)
            t["dv"] = dot_nt(t["dob"], t["pb"])
            acc_scr[t["h"]] += ds

        def spread(t):
            h, here = t["h"], it * step_rows + t["a"]
            dq = dot_nn(t["k"], t["dsb"]) * scale
            dk = dot_nt(t["q"], t["dsb"]) * scale
            d_ref[here, h * DH : (h + 1) * DH, :] = dq.astype(BF16)
            d_ref[here, 128 + h * DH : 128 + (h + 1) * DH, :] = dk.astype(BF16)
            d_ref[here, 192 + h * DH : 192 + (h + 1) * DH, :] = t["dv"].astype(BF16)

        def finish(a, row, items):
            here = it * step_rows + a
            o_t = jnp.concatenate([items[0]["o"], items[1]["o"]], axis=0)
            gate = row["gate"]
            d_ref[here, 64:128, :] = (
                row["dgated"] * o_t * gate * (1.0 - gate)
            ).astype(BF16)
            wacc_scr[256:320, :] += dot_nn((gate * o_t).astype(BF16), row["grad"])
            pltpu.make_async_copy(d_ref.at[here], d_hbm.at[here], d_sems.at[here]).start()
            wacc_scr[0:256, :] += dot_nn(d_ref[here], row["x"])

        def both(t):
            apply(t)
            back(t)

        stages = (score, soften, both, spread)
        depth = len(stages)
        plan = []
        for a in range(step_rows):
            row, items = {}, ({}, {})
            ready = lambda a=a, row=row, items=items: prepare(a, row, items)
            plan.append((2 * a - 1, 0, ready))
            for h in range(2):
                for place, stage in enumerate(stages):
                    when = 2 * a + h + place
                    plan.append((when, 1 + 2 * a + h, lambda stage=stage, t=items[h]: stage(t)))
            done = lambda a=a, row=row, items=items: finish(a, row, items)
            plan.append((2 * a + depth, 2 * a + 2.5, done))
        for _, _, act in sorted(plan, key=lambda e: (e[0], e[1])):
            act()
        return carry

    lax.fori_loop(0, groups // step_rows, some_rows, 0)

    for i in range(64):
        part = wacc_scr[5 * i : 5 * i + 8, :].astype(BF16)
        out_ref[2 * i, cols : cols + 8, :] = part
        out_ref[2 * i + 1, cols : cols + 8, :] = part
    copies = []
    for r in range(0, groups, 2):
        sl = slice(r * 64, r * 64 + 128)
        h0, h1 = acc_scr[0, :, sl], acc_scr[1, :, sl]
        b0 = jnp.where(low, h0, pltpu.roll(h1, 64, 1)).astype(BF16)
        b1 = jnp.where(low, pltpu.roll(h0, 64, 1), h1).astype(BF16)
        out_ref[r * blocks : (r + 1) * blocks, 0:cols, :] = b0.reshape(blocks, cols, C)
        out_ref[(r + 1) * blocks : (r + 2) * blocks, 0:cols, :] = b1.reshape(blocks, cols, C)
        part = pl.ds(r * blocks, 2 * blocks)
        copies.append(pltpu.make_async_copy(out_ref.at[part], out_hbm.at[part], sems.at[r // 2]))
        copies[-1].start()
    for r in range(groups):
        copies.append(pltpu.make_async_copy(d_ref.at[r], d_hbm.at[r], d_sems.at[r]))
    for copy in copies:
        copy.wait()


def dx_kernel(core_ref, mine_ref, other_ref, d_ref, w_ref, keep_ref, send_ref, norm_ref):
    core = core_ref[0]
    groups, blocks, cols = 8, 16, 32
    n, half = blocks * cols, cols // 2
    norm_ref[...] = jnp.zeros_like(norm_ref)

    def one_row(r, carry):
        src = pl.ds(r * blocks, blocks)
        mine = mine_ref[src, 0:cols, :].reshape(n, C)
        pair = jnp.where(core == 0, mine, other_ref[src, :, :].reshape(n, C))
        normed, _ = normalize(pair.astype(F32))
        dx = dot_tn(d_ref[r], w_ref[0:256, :])
        norm_ref[0:8, :] += jnp.sum((dx * normed).reshape(n // 8, 8, C), axis=0)
        norm_ref[8:16, :] += jnp.sum(dx.reshape(n // 8, 8, C), axis=0)
        dx = dx.astype(BF16).reshape(blocks, cols, C)
        keep_ref[src] = jnp.where(core == 0, dx[:, 0:half], dx[:, half:cols])
        send_ref[src] = jnp.where(core == 0, dx[:, half:cols], dx[:, 0:half])
        return carry

    lax.fori_loop(0, groups, one_row, 0, unroll=2)


def sums_kernel(
    core_ref, both_hbm, xt_hbm, nt_hbm, got_ref, norm_ref, wb_ref,
    z_ref, sums_hbm, z_scr, s_scr, sums_ref, xt_ref, nt_ref, sems,
):
    core = core_ref[0]
    rows, cols = got_ref.shape[0], 32
    copies = [
        pltpu.make_async_copy(xt_hbm, xt_ref, sems.at[0]),
        pltpu.make_async_copy(nt_hbm, nt_ref, sems.at[1]),
        pltpu.make_async_copy(both_hbm, sums_ref.at[:, 16:32, :], sems.at[2]),
    ]
    for copy in copies:
        copy.start()
    z_scr[...] = jnp.zeros_like(z_scr)
    for pair in range(2):

        def add(i, total, pair=pair):
            return total + got_ref[i, pair, 0:cols, :].astype(F32)

        total = lax.fori_loop(0, rows, add, jnp.zeros((cols, C), F32), unroll=8)
        for k in range(cols):
            for h in range(2):
                z_scr[2 * pair + h : 2 * pair + h + 1, k * rows : (k + 1) * rows] = total[
                    k : k + 1, h * 64 : (h + 1) * 64
                ]
    z = z_scr[...].astype(BF16)
    z_ref[...] = z
    copies[2].wait()
    last = pltpu.make_async_copy(sums_ref.at[:, 16:32, :], sums_hbm.at[:, 16:32, :], sems.at[3])
    last.start()
    copies[0].wait()
    copies[1].wait()
    dwb = dot_nn(z, xt_ref[...])
    dgn = dot_nn(z, nt_ref[...])

    def add_w(i, total):
        return total + got_ref[i, core, cols : cols + 8, :].astype(F32)

    s_scr[0:8, :] = lax.fori_loop(0, rows, add_w, jnp.zeros((8, C), F32), unroll=8)
    s_scr[8:12, :] = dwb[0:4]
    wb = wb_ref[...].astype(F32)
    dgain = jnp.sum(norm_ref[0:8, :], axis=0, keepdims=True)
    dgain = dgain + jnp.sum(dgn[0:4] * wb, axis=0, keepdims=True)
    dshift = jnp.sum(norm_ref[8:16, :], axis=0, keepdims=True)
    total = jnp.sum(z_scr[0:4, :], axis=1, keepdims=True)
    dshift = dshift + jnp.sum(total * wb, axis=0, keepdims=True)
    s_scr[12:13, :] = dgain
    s_scr[13:14, :] = dshift
    s_scr[14:15, :] = dgain - dgain.astype(BF16).astype(F32)
    s_scr[15:16, :] = dshift - dshift.astype(BF16).astype(F32)
    sums_ref[:, 0:16, :] = jnp.broadcast_to(s_scr[...].astype(BF16)[None], (2 * rows, 16, C))
    first = pltpu.make_async_copy(sums_ref.at[:, 0:16, :], sums_hbm.at[:, 0:16, :], sems.at[4])
    first.start()
    last.wait()
    first.wait()


def ready_kernel(
    z_ref, pair_ref, wb_ref, dxb_hbm, normed_hbm, rstd_hbm,
    dxb_scr, wb_scr, dxb_ref, normed_ref, rstd_ref, sems,
):
    rows, cols = pair_ref.shape[0], pair_ref.shape[1]
    wb_scr[...] = jnp.zeros_like(wb_scr)
    wb_scr[0:4, :] = wb_ref[...].astype(F32)
    dxb_scr[...] = dot_tn(z_ref[...], wb_scr[...].astype(BF16))

    def some(it, carry):
        i0 = it * 8
        part = pl.ds(i0, 8)
        normed, rstd = normalize(pair_ref[part].astype(F32))
        normed_ref[part] = normed
        rstd_ref[part] = jnp.broadcast_to(rstd, normed.shape)
        for u in range(8):
            dxb_ref[i0 + u] = dxb_scr[pl.ds(i0 + u, cols, stride=rows), :]
        return carry

    lax.fori_loop(0, rows // 8, some, 0)
    copies = [
        pltpu.make_async_copy(src, dst, sems.at[i])
        for i, (src, dst) in enumerate(
            ((dxb_ref, dxb_hbm), (normed_ref, normed_hbm), (rstd_ref, rstd_hbm))
        )
    ]
    for copy in copies:
        copy.start()
    for copy in copies:
        copy.wait()


def final_kernel(
    dxb_hbm, normed_hbm, rstd_hbm, got_ref, gain_ref,
    dpair_hbm, dgain_ref, dshift_ref, dq_ref, dk_ref, dv_ref, dg_ref, db_ref, do_ref,
    w_scr, dxb_ref, normed_ref, rstd_ref, dpair_ref, sems, out_sems,
):
    chips, cols, parts = got_ref.shape[0], dxb_ref.shape[1], out_sems.shape[0]
    size = chips // parts
    fetched = []
    for p in range(parts):
        part = pl.ds(p * size, size)
        fetched.append(
            [
                pltpu.make_async_copy(src.at[part], dst.at[part], sems.at[i, p])
                for i, (src, dst) in enumerate(
                    ((dxb_hbm, dxb_ref), (normed_hbm, normed_ref), (rstd_hbm, rstd_ref))
                )
            ]
        )
        for copy in fetched[-1]:
            copy.start()
    zero = jnp.zeros((16, C), F32)

    def add(i, total):
        return total + (got_ref[i, 0, 0:16, :].astype(F32) + got_ref[i, 1, 0:16, :].astype(F32))

    total = lax.fori_loop(0, chips, add, zero, unroll=8)
    db_ref[...] = total[8:12]
    dgain_ref[...] = total[12:13] + total[14:15]
    dshift_ref[...] = total[13:14] + total[15:16]
    gain = gain_ref[...]
    sent = []
    for p in range(parts):
        for copy in fetched[p]:
            copy.wait()

        def some(it, carry, p=p):
            part = pl.ds(p * size + it * 8, 8)
            normed, rstd = normed_ref[part], rstd_ref[part]
            dx = jnp.concatenate([got_ref[part, 0, 16:32, :], got_ref[part, 1, 16:32, :]], axis=1)
            dn = (dx.astype(F32) + dxb_ref[part]) * gain
            out = rstd * (
                dn
                - jnp.mean(dn, axis=-1, keepdims=True)
                - normed * jnp.mean(dn * normed, axis=-1, keepdims=True)
            )
            dpair_ref[part] = out.astype(BF16)
            return carry

        lax.fori_loop(0, size // 8, some, 0)
        part = pl.ds(p * size, size)
        sent.append(pltpu.make_async_copy(dpair_ref.at[part], dpair_hbm.at[part], out_sems.at[p]))
        sent[-1].start()
    for core in range(2):
        for i in range(chips):
            w_scr[core, 5 * i : 5 * i + 8, :] = got_ref[i, core, 0:16, :].astype(F32)[0:8]
    for slot, ref in enumerate((dq_ref, dg_ref, dk_ref, dv_ref)):
        sl = slice(slot * 64, (slot + 1) * 64)
        heads = jnp.concatenate([w_scr[0, sl, :], w_scr[1, sl, :]], axis=0)
        ref[...] = jnp.transpose(heads)
    do_ref[0:64, :] = w_scr[0, 256:320, :]
    do_ref[64:128, :] = w_scr[1, 256:320, :]
    for copy in sent:
        copy.wait()


def on_device(
    pair, grad_out, norm_gain, norm_shift, w_query, w_key, w_value, w_gate, w_bias, w_out
):
    axes = ("row", "col")
    rows, cols = pair.shape[0], pair.shape[1]
    devices = 2 * rows
    sds = jax.ShapeDtypeStruct
    gain, shift = norm_gain.reshape(1, C), norm_shift.reshape(1, C)
    wb = w_bias.T
    core = (lax.axis_index("col") % 2).astype(jnp.int32).reshape(1)

    turned = sds((rows * cols, C), BF16)
    turned_scr = pltpu.VMEM((rows * cols, C), BF16)
    packed, xt, nt = call(
        pack_kernel,
        (sds((rows, 2, 64, C), BF16), turned, turned),
        0,
        (
            pltpu.VMEM((rows * cols, C), F32),
            pltpu.VMEM((cols, C), F32),
            pltpu.VMEM((1, C), F32),
            pltpu.VMEM((1, C), F32),
            pltpu.VMEM((H, C), BF16),
            pltpu.SemaphoreType.DMA((5,)),
        ),
        hbm=5,
        flops=10**8,
        moved=4 * MIB,
    )(*(in_hbm(a) for a in (pair, grad_out, gain, shift, wb)))
    mine = lax.all_to_all(packed.reshape(devices, 64, C), axes, 0, 0, tiled=True)
    swap = [(i, i ^ 1) for i in range(16)]
    other = lax.ppermute(mine[:, 0:cols, :], "col", swap)
    terms, spread, turned_w = call(
        attend_kernel,
        (
            pltpu.HBM((devices, 40, C), BF16),
            pltpu.HBM((8, 256, 512), BF16),
            sds((320, C), BF16),
        ),
        9,
        (
            pltpu.VMEM((2, 512, 512), F32),
            pltpu.VMEM((2, 512, 512), F32),
            pltpu.VMEM((328, C), F32),
            pltpu.VMEM((16, C, 512), BF16),
            pltpu.VMEM((devices, 40, C), BF16),
            pltpu.VMEM((8, 256, 512), BF16),
            pltpu.SemaphoreType.DMA((4,)),
            pltpu.SemaphoreType.DMA((8,)),
        ),
        smem=1,
        to_hbm=(0, 1),
        vmem=36,
        flops=10**10,
        moved=6 * MIB,
    )(core, mine, other, gain, shift, w_query, w_key, w_value, w_gate, w_out)
    got = lax.all_to_all(terms, axes, 0, 0, tiled=True).reshape(rows, 2, 40, C)
    halves = sds((devices, cols // 2, C), BF16)
    keep, send, norms = call(
        dx_kernel,
        (halves, halves, sds((16, C), F32)),
        4,
        smem=1,
        flops=10**9,
        moved=6 * MIB,
    )(core, mine, other, spread, turned_w)
    came = lax.ppermute(send, "col", swap)
    both = (keep.astype(F32) + came.astype(F32)).astype(BF16)
    z, sums = call(
        sums_kernel,
        (sds((8, rows * cols), BF16), pltpu.HBM((devices, 32, C), BF16)),
        3,
        (
            pltpu.VMEM((8, rows * cols), F32),
            pltpu.VMEM((16, C), F32),
            pltpu.VMEM((devices, 32, C), BF16),
            turned_scr,
            turned_scr,
            pltpu.SemaphoreType.DMA((5,)),
        ),
        smem=1,
        hbm=3,
        to_hbm=(1,),
        flops=10**8,
        moved=4 * MIB,
    )(core, in_hbm(both), in_hbm(xt), in_hbm(nt), got, norms, wb)
    last = lax.all_to_all(sums, axes, 0, 0, tiled=True).reshape(rows, 2, 32, C)
    tile = pltpu.HBM(pair.shape, F32)
    tile_scr = pltpu.VMEM(pair.shape, F32)
    dxb, normed, rstd = call(
        ready_kernel,
        (tile, tile, tile),
        3,
        (
            pltpu.VMEM((rows * cols, C), F32),
            pltpu.VMEM((8, C), F32),
            tile_scr,
            tile_scr,
            tile_scr,
            pltpu.SemaphoreType.DMA((3,)),
        ),
        to_hbm=(0, 1, 2),
        flops=10**8,
        moved=8 * MIB,
    )(z, pair, wb)
    square = sds((C, C), F32)
    d_pair, d_gain, d_shift, d_query, d_key, d_value, d_gate, d_bias, d_out = call(
        final_kernel,
        (
            pltpu.HBM(pair.shape, BF16),
            sds((1, C), F32),
            sds((1, C), F32),
            square,
            square,
            square,
            square,
            sds((H, C), F32),
            square,
        ),
        2,
        (
            pltpu.VMEM((2, 328, C), F32),
            tile_scr,
            tile_scr,
            tile_scr,
            pltpu.VMEM(pair.shape, BF16),
            pltpu.SemaphoreType.DMA((3, 4)),
            pltpu.SemaphoreType.DMA((4,)),
        ),
        hbm=3,
        to_hbm=(0,),
        moved=8 * MIB,
    )(in_hbm(dxb), in_hbm(normed), in_hbm(rstd), last, gain)
    return (
        d_pair,
        d_gain.reshape(C),
        d_shift.reshape(C),
        d_query,
        d_key,
        d_value,
        d_gate,
        d_bias.T,
        d_out,
    )


def solution(mesh):
    return jax.shard_map(
        on_device,
        mesh=mesh,
        in_specs=(P("row", "col", None), P("row", "col", None)) + (P(),) * 8,
        out_specs=(P("row", "col", None),) + (P(),) * 8,
        check_vma=False,
    )
```

time: 131 us -> 124 us (0.947)
  blocking collectives: 79 us -> 41.8 us
  waiting for transfers between devices: 13.1 us -> 32.6 us
  Pallas kernels: 26.1 us -> 32.8 us
  starting transfers between devices: 5.08 us -> 10.7 us
  local copies, waits for them, and re-layouts: 6.02 us -> 3.97 us
    all_to_all x1 -> x0, blocking collectives: 37.2 us -> none  [on_device(): got = lax.all_to_all(terms, axes, 0, 0, tiled=True).reshape(rows, 2, 72, C)]
    all_to_all x1 -> x2, waiting for transfers between devices: 10.4 us -> 28.6 us  [the longest x1 15.5 us: on_device(): last = lax.all_to_all(sums, axes, 0, 0, tiled=True).reshape(rows, 2, 32, C)]
    pallas_call x5 -> x6, Pallas kernels: 26.1 us -> 32.8 us  [the longest x1 17.3 us: on_device(): call(attend_kernel, (pltpu.HBM((devices, 40, C), BF16), pltpu.HBM((8, 256...]
    all_to_all x1 -> x2, starting transfers between devices: 4.53 us -> 8.79 us  [the longest x1 4.5 us: on_device(): last = lax.all_to_all(sums, axes, 0, 0, tiled=True).reshape(rows, 2, 32, C)]
    unnamed x34 -> x28, local copies, waits for them, and re-layouts: 4.93 us -> 2.87 us
    ppermute x0 -> x1, waiting for transfers between devices: none -> 1.54 us  [on_device(): came = lax.ppermute(send, 'col', swap)]
    ppermute x0 -> x1, starting transfers between devices: none -> 1.33 us  [on_device(): came = lax.ppermute(send, 'col', swap)]
  transfers between devices with their start and end apart: 2 -> 4, of which waited for: 2 -> 4; matrix products, arithmetic and copies ran while one was open for 0% -> 1% of each run, Pallas kernels for 3% -> 5%
where the time goes in v3:
time: 124 us
  blocking collectives  41.8 us (34%)
  Pallas kernels  32.8 us (26%)
  waiting for transfers between devices  32.6 us (26%)
  starting transfers between devices  10.7 us (9%)
  local copies, waits for them, and re-layouts  3.97 us (3%)
    all_to_all x1, blocking collectives, on_device(): lax.all_to_all(packed.reshape(devices, 64, C), axes, 0, 0, tiled=True)  41.8 us
    pallas_call x1, Pallas kernels, on_device(): call(attend_kernel, (pltpu.HBM((devices, 40, C), BF16), pltpu.HBM((8, 256...  17.3 us
    all_to_all x1, waiting for transfers between devices, on_device(): last = lax.all_to_all(sums, axes, 0, 0, tiled=True).reshape(rows, 2, 32, C)  15.5 us
    all_to_all x1, waiting for transfers between devices, on_device(): got = lax.all_to_all(terms, axes, 0, 0, tiled=True).reshape(rows, 2, 40, C)  13.1 us
    all_to_all x1, starting transfers between devices, on_device(): last = lax.all_to_all(sums, axes, 0, 0, tiled=True).reshape(rows, 2, 32, C)  4.5 us
    all_to_all x1, starting transfers between devices, on_device(): got = lax.all_to_all(terms, axes, 0, 0, tiled=True).reshape(rows, 2, 40, C)  4.29 us
    pallas_call x1, Pallas kernels, on_device(): call(final_kernel, (pltpu.HBM(pair.shape, BF16), sds((1, C), F32), sds((1...  3.93 us
    pallas_call x1, Pallas kernels, on_device(): call(ready_kernel, (tile, tile, tile), 3, (pltpu.VMEM((rows * cols, C), F...  3.73 us
  transfers between devices with their start and end apart: 4, of which 4 were waited for; matrix products, arithmetic and copies ran while one was open for 1% of the time, Pallas kernels for 5%

profile of v3, /device:TPU:1, one launch (start us, length us, event | category | flops | bytes accessed | tf_op | source)
XLA Modules:
  0.0 123.7 jit_solution(1228241743601495265)
XLA Ops:
  0.6 2.6 %shard_map.169 = (bf16[64,2,64,128]{3,2,1,0:T(8,128)(2,1)S(1)}, bf16[2048,128]{1,0:T(8,128)(2,1)S(1)}, bf16[2048,128]{1,0:T(8,128)(2,1)S(1)}) custom-call(bf16[64,32,128]{2,1,0:T(8,128)(2,1)} %pair_ref.1, bf16[64,32,128]{2,1,0:T(8,128)(2,1)} %grad_hbm.1, f32[1,128]{1,0:T(1,128)} %bitcast.16, f32[1,128]{1,0:T(1,128)} %bitcast.19, bf16[4,128]{1,0:T(4,128)(2,1)} %bitcast.13), custom_call_target="tpu_custom_call" | custom-call | flops 100000000 | bytes 4194304 | tf_op jit(solution)/shard_map/pallas_call | solution.py:423
  3.3 0.0 copy-start.4
  3.3 0.0 copy-start.5
  3.3 41.8 %all_to_all.15.mine_ref = bf16[128,64,128]{2,1,0:T(8,128)(2,1)S(1)} all-to-all(bf16[128,64,128]{2,1,0:T(8,128)(2,1)S(1)} %bitcast.12), channel_id=1, replica_groups=mesh['row'=8,'col'=16] {'row','col'}, dimensions={0} | all-to-all | bytes 4194304 | tf_op jit(solution)/shard_map/all_to_all | solution.py:439
  45.1 0.0 copy-done.4
  45.1 0.0 copy-done.5
  45.1 0.0 copy-start.9
  45.1 0.0 copy-start.10
  45.1 0.0 copy-start.11
  45.1 0.0 copy-start.12
  45.1 0.0 copy-start.13
  45.1 1.1 slice.4
  46.2 0.5 collective-permute-start
  46.8 2.5 %collective-permute-done.other_ref = bf16[128,32,128]{2,1,0:T(8,128)(2,1)S(1)} collective-permute-done((bf16[128,32,128]{2,1,0:T(8,128)(2,1)}, bf16[128,32,128]{2,1,0:T(8,128)(2,1)S(1)}, u32[]{:S(2)}, u32[]{:S(2)}) %collective-permute-start) | collective-permute-done | bytes 1048608 | tf_op jit(solution)/shard_map/ppermute | solution.py:441
  49.3 0.0 copy-done.7
  49.3 0.0 copy-done.8
  49.3 17.3 %shard_map.170 = (bf16[128,40,128]{2,1,0:T(8,128)(2,1)}, bf16[8,256,512]{2,1,0:T(8,128)(2,1)}, bf16[320,128]{1,0:T(8,128)(2,1)S(1)}) custom-call(s32[1]{0:T(128)} %bitcast.core_ref, bf16[128,64,128]{2,1,0:T(8,128)(2,1)S(1)} %all_to_all.15.mine_ref, bf16[128,32,128]{2,1,0:T(8,128)(2,1)S(1)} %collective-permute-done.other_ref, f32[1,128]{1,0:T(1,128)S(1)} %bitcast.17, ...), custom_call_target="tpu_custom_call" | custom-call | flops 10000000000 | bytes 6291456 | tf_op jit(solution)/shard_map/pallas_call | solution.py:442
  66.7 4.3 %all-to-all-start.1 = ((bf16[128,40,128]{2,1,0:T(8,128)(2,1)}), bf16[128,40,128]{2,1,0:T(8,128)(2,1)S(1)}, u32[]{:S(2)}, u32[]{:S(2)}) async-start(bf16[128,40,128]{2,1,0:T(8,128)(2,1)} %get-tuple-element.39), calls=%async_computation.1 | async-start | bytes 2621440 | tf_op jit(solution)/shard_map/all_to_all | solution.py:466
  71.0 1.6 %copy-done = bf16[8,256,512]{2,1,0:T(8,128)(2,1)S(1)} copy-done((bf16[8,256,512]{2,1,0:T(8,128)(2,1)S(1)}, bf16[8,256,512]{2,1,0:T(8,128)(2,1)}, u32[]{:S(2)}) %copy-start) | copy-done | bytes 2097176
  72.6 1.2 copy-done.3
  73.8 2.4 %shard_map.171 = (bf16[128,16,128]{2,1,0:T(8,128)(2,1)S(1)}, bf16[128,16,128]{2,1,0:T(8,128)(2,1)S(1)}, f32[16,128]{1,0:T(8,128)S(1)}) custom-call(s32[1]{0:T(128)} %bitcast.core_ref, bf16[128,64,128]{2,1,0:T(8,128)(2,1)S(1)} %all_to_all.15.mine_ref, bf16[128,32,128]{2,1,0:T(8,128)(2,1)S(1)} %copy-done.3, bf16[8,256,512]{2,1,0:T(8,128)(2,1)S(1)} %copy-done, ...), custom_call_target="tpu_custom_call" | custom-call | flops 1000000000 | bytes 6291456 | tf_op jit(solution)/shard_map/pallas_call | solution.py:468
  76.2 1.3 %collective-permute-start.1 = (bf16[128,16,128]{2,1,0:T(8,128)(2,1)S(1)}, bf16[128,16,128]{2,1,0:T(8,128)(2,1)S(1)}, u32[]{:S(2)}, u32[]{:S(2)}) collective-permute-start(bf16[128,16,128]{2,1,0:T(8,128)(2,1)S(1)} %get-tuple-element.36), channel_id=1, source_target_pairs={{0,1},{1,0},{2,3},{3,2},{4,5},{5,4},{6,7},{7,6},{8,9},{9,8},{10,11... | collective-permute-start | bytes 1572872 | tf_op jit(solution)/shard_map/ppermute | solution.py:476
  77.6 1.5 %collective-permute-done.1 = bf16[128,16,128]{2,1,0:T(8,128)(2,1)S(1)} collective-permute-done((bf16[128,16,128]{2,1,0:T(8,128)(2,1)S(1)}, bf16[128,16,128]{2,1,0:T(8,128)(2,1)S(1)}, u32[]{:S(2)}, u32[]{:S(2)}) %collective-permute-start.1) | collective-permute-done | bytes 524320 | tf_op jit(solution)/shard_map/ppermute | solution.py:476
  79.1 0.9 add_convert_fusion.both_hbm
  80.0 13.1 %all-to-all-done.1 = bf16[128,40,128]{2,1,0:T(8,128)(2,1)S(1)} async-done(((bf16[128,40,128]{2,1,0:T(8,128)(2,1)}), bf16[128,40,128]{2,1,0:T(8,128)(2,1)S(1)}, u32[]{:S(2)}, u32[]{:S(2)}) %all-to-all-start.1) | async-done | bytes 1310752 | tf_op jit(solution)/shard_map/all_to_all | solution.py:466
  93.1 0.0 copy-done.6
  93.1 2.8 %shard_map.172 = (bf16[8,2048]{1,0:T(8,128)(2,1)S(1)}, bf16[128,32,128]{2,1,0:T(8,128)(2,1)}) custom-call(s32[1]{0:T(128)} %bitcast.core_ref, bf16[128,16,128]{2,1,0:T(8,128)(2,1)} %add_convert_fusion.both_hbm, bf16[2048,128]{1,0:T(8,128)(2,1)} %copy-done.4, bf16[2048,128]{1,0:T(8,128)(2,1)} %copy-done.5, bf16[64,2,40,128]{3,2,1,0:T(8,128)(2,1)S(1)} %bitcast.10, ...), custom_call_target="tpu_custom_call" | custom-call | flops 100000000 | bytes 4194304 | tf_op jit(solution)/shard_map/pallas_call | solution.py:478
  95.9 4.5 %all-to-all-start.2 = ((bf16[128,32,128]{2,1,0:T(8,128)(2,1)}), bf16[128,32,128]{2,1,0:T(8,128)(2,1)S(1)}, u32[]{:S(2)}, u32[]{:S(2)}) async-start(bf16[128,32,128]{2,1,0:T(8,128)(2,1)} %get-tuple-element.45), calls=%async_computation.2 | async-start | bytes 2097152 | tf_op jit(solution)/shard_map/all_to_all | solution.py:496
  100.4 0.0 copy-done.1
  100.4 3.7 %shard_map.173 = (f32[64,32,128]{2,1,0:T(8,128)}, f32[64,32,128]{2,1,0:T(8,128)}, f32[64,32,128]{2,1,0:T(8,128)}) custom-call(bf16[8,2048]{1,0:T(8,128)(2,1)S(1)} %get-tuple-element.41.z_ref, bf16[64,32,128]{2,1,0:T(8,128)(2,1)S(1)} %copy-done.1, bf16[4,128]{1,0:T(4,128)(2,1)S(1)} %bitcast.15), custom_call_target="tpu_custom_call" | custom-call | flops 100000000 | bytes 8388608 | tf_op jit(solution)/shard_map/pallas_call | solution.py:499
  104.1 15.5 %all-to-all-done.2 = bf16[128,32,128]{2,1,0:T(8,128)(2,1)S(1)} async-done(((bf16[128,32,128]{2,1,0:T(8,128)(2,1)}), bf16[128,32,128]{2,1,0:T(8,128)(2,1)S(1)}, u32[]{:S(2)}, u32[]{:S(2)}) %all-to-all-start.2) | async-done | bytes 1048608 | tf_op jit(solution)/shard_map/all_to_all | solution.py:496
  119.7 3.9 %shard_map.174 = (bf16[64,32,128]{2,1,0:T(8,128)(2,1)}, f32[1,128]{1,0:T(1,128)}, f32[1,128]{1,0:T(1,128)}, f32[128,128]{1,0:T(8,128)}, f32[128,128]{1,0:T(8,128...) custom-call(f32[64,32,128]{2,1,0:T(8,128)} %get-tuple-element.42.dxb_hbm, ...), custom_call_target="tpu_custom_call" | custom-call | bytes 8388608 | tf_op jit(solution)/shard_map/pallas_call | solution.py:516
  (13 shorter events, 0.0 us)
Async XLA Ops:
  3.3 41.8 %copy-start.4 = (bf16[2048,128]{1,0:T(8,128)(2,1)}, bf16[2048,128]{1,0:T(8,128)(2,1)S(1)}, u32[]{:S(2)}) copy-start(bf16[2048,128]{1,0:T(8,128)(2,1)S(1)} %get-tuple-element.37.xt_hbm) | copy-start | bytes 1572868
  3.3 41.8 %copy-start.5 = (bf16[2048,128]{1,0:T(8,128)(2,1)}, bf16[2048,128]{1,0:T(8,128)(2,1)S(1)}, u32[]{:S(2)}) copy-start(bf16[2048,128]{1,0:T(8,128)(2,1)S(1)} %get-tuple-element.38.nt_hbm) | copy-start | bytes 1572868
  45.1 4.2 %copy-start.7 = (f32[128]{0:T(128)S(1)}, f32[128]{0:T(128)}, u32[]{:S(2)}) copy-start(f32[128]{0:T(128)} %param.12) | copy-start | bytes 1540
  45.1 4.2 %copy-start.8 = (f32[128]{0:T(128)S(1)}, f32[128]{0:T(128)}, u32[]{:S(2)}) copy-start(f32[128]{0:T(128)} %param.13) | copy-start | bytes 1540
  45.1 4.2 %copy-start.9 = (bf16[128,128]{1,0:T(8,128)(2,1)S(1)}, bf16[128,128]{1,0:T(8,128)(2,1)}, u32[]{:S(2)}) copy-start(bf16[128,128]{1,0:T(8,128)(2,1)} %wq_ref.1) | copy-start | bytes 98308
  45.1 4.2 %copy-start.10 = (bf16[128,128]{1,0:T(8,128)(2,1)S(1)}, bf16[128,128]{1,0:T(8,128)(2,1)}, u32[]{:S(2)}) copy-start(bf16[128,128]{1,0:T(8,128)(2,1)} %wk_ref.1) | copy-start | bytes 98308
  45.1 4.2 %copy-start.11 = (bf16[128,128]{1,0:T(8,128)(2,1)S(1)}, bf16[128,128]{1,0:T(8,128)(2,1)}, u32[]{:S(2)}) copy-start(bf16[128,128]{1,0:T(8,128)(2,1)} %wv_ref.1) | copy-start | bytes 98308
  45.1 4.2 %copy-start.12 = (bf16[128,128]{1,0:T(8,128)(2,1)S(1)}, bf16[128,128]{1,0:T(8,128)(2,1)}, u32[]{:S(2)}) copy-start(bf16[128,128]{1,0:T(8,128)(2,1)} %wg_ref.1) | copy-start | bytes 98308
  45.1 4.2 %copy-start.13 = (bf16[128,128]{1,0:T(8,128)(2,1)S(1)}, bf16[128,128]{1,0:T(8,128)(2,1)}, u32[]{:S(2)}) copy-start(bf16[128,128]{1,0:T(8,128)(2,1)} %wo_ref.1) | copy-start | bytes 98308
  46.2 3.0 %collective-permute-start = (bf16[128,32,128]{2,1,0:T(8,128)(2,1)}, bf16[128,32,128]{2,1,0:T(8,128)(2,1)S(1)}, u32[]{:S(2)}, u32[]{:S(2)}) collective-permute-start(bf16[128,32,128]{2,1,0:T(8,128)(2,1)} %slice.4), channel_id=1, source_target_pairs={{0,1},{1,0},{2,3},{3,2},{4,5},{5,4},{6,7},{7,6},{8,9},{9,8},{10,11... | collective-permute-start | bytes 3145736 | tf_op jit(solution)/shard_map/ppermute | solution.py:441
  49.3 17.4 %copy-start.2 = (bf16[128,32,128]{2,1,0:T(8,128)(2,1)}, bf16[128,32,128]{2,1,0:T(8,128)(2,1)S(1)}, u32[]{:S(2)}) copy-start(bf16[128,32,128]{2,1,0:T(8,128)(2,1)S(1)} %collective-permute-done.other_ref) | copy-start | bytes 3145732
  66.7 26.4 %all-to-all-start.1 = ((bf16[128,40,128]{2,1,0:T(8,128)(2,1)}), bf16[128,40,128]{2,1,0:T(8,128)(2,1)S(1)}, u32[]{:S(2)}, u32[]{:S(2)}) async-start(bf16[128,40,128]{2,1,0:T(8,128)(2,1)} %get-tuple-element.39), calls=%async_computation.1 | async-start | bytes 2621440 | tf_op jit(solution)/shard_map/all_to_all | solution.py:466
  71.0 1.6 %copy-start = (bf16[8,256,512]{2,1,0:T(8,128)(2,1)S(1)}, bf16[8,256,512]{2,1,0:T(8,128)(2,1)}, u32[]{:S(2)}) copy-start(bf16[8,256,512]{2,1,0:T(8,128)(2,1)} %get-tuple-element.33.d_ref) | copy-start | bytes 6291460
  72.6 1.2 copy-start.3
  73.8 19.3 %copy-start.6 = (bf16[128,4]{0,1:T(4,128)(2,1)S(1)}, bf16[128,4]{0,1:T(4,128)(2,1)}, u32[]{:S(2)}) copy-start(bf16[128,4]{0,1:T(4,128)(2,1)} %param.18) | copy-start | bytes 3076
  76.2 2.9 %collective-permute-start.1 = (bf16[128,16,128]{2,1,0:T(8,128)(2,1)S(1)}, bf16[128,16,128]{2,1,0:T(8,128)(2,1)S(1)}, u32[]{:S(2)}, u32[]{:S(2)}) collective-permute-start(bf16[128,16,128]{2,1,0:T(8,128)(2,1)S(1)} %get-tuple-element.36), channel_id=1, source_target_pairs={{0,1},{1,0},{2,3},{3,2},{4,5},{5,4},{6,7},{7,6},{8,9},{9,8},{10,11... | collective-permute-start | bytes 1572872 | tf_op jit(solution)/shard_map/ppermute | solution.py:476
  93.1 7.3 %copy-start.1 = (bf16[64,32,128]{2,1,0:T(8,128)(2,1)S(1)}, bf16[64,32,128]{2,1,0:T(8,128)(2,1)}, u32[]{:S(2)}) copy-start(bf16[64,32,128]{2,1,0:T(8,128)(2,1)} %pair_ref.1) | copy-start | bytes 1572868
  95.9 23.8 %all-to-all-start.2 = ((bf16[128,32,128]{2,1,0:T(8,128)(2,1)}), bf16[128,32,128]{2,1,0:T(8,128)(2,1)S(1)}, u32[]{:S(2)}, u32[]{:S(2)}) async-start(bf16[128,32,128]{2,1,0:T(8,128)(2,1)} %get-tuple-element.45), calls=%async_computation.2 | async-start | bytes 2097152 | tf_op jit(solution)/shard_map/all_to_all | solution.py:496

commit v4 on v3

--- a/solution.py
+++ b/solution.py
@@ -31,6 +31,10 @@
     center = values - jnp.mean(values, axis=-1, keepdims=True)
     rstd = lax.rsqrt(jnp.mean(center * center, axis=-1, keepdims=True) + EPS)
     return center * rstd, rstd
+
+
+def mean_lanes(values):
+    return dot_nn(values.astype(BF16), jnp.full((C, C), 1.0 / C, BF16))
 
 
 def call(
@@ -61,7 +65,7 @@
 
 def pack_kernel(
     pair_hbm, grad_hbm, gain_hbm, shift_hbm, wb_hbm,
-    out_ref, xt_ref, nt_ref, n_scr, b_scr, gain_scr, shift_scr, wb_scr, sems,
+    out_ref, nt_ref, n_scr, b_scr, gain_scr, shift_scr, wb_scr, xt_ref, sems,
 ):
     rows, cols = pair_hbm.shape[0], pair_hbm.shape[1]
     copies = [
@@ -187,11 +191,15 @@
             pltpu.make_async_copy(d_ref.at[here], d_hbm.at[here], d_sems.at[here]).start()
             wacc_scr[0:256, :] += dot_nn(d_ref[here], row["x"])
 
-        def both(t):
+        def forward(t):
+            soften(t)
             apply(t)
+
+        def backward(t):
             back(t)
-
-        stages = (score, soften, both, spread)
+            spread(t)
+
+        stages = (score, forward, backward)
         depth = len(stages)
         plan = []
         for a in range(step_rows):
@@ -253,19 +261,21 @@
     lax.fori_loop(0, groups, one_row, 0, unroll=2)
 
 
+def merge_kernel(keep_ref, came_ref, nt_ref, out_ref):
+    devices, half = keep_ref.shape[0], keep_ref.shape[1]
+    out_ref[:, 0:half, :] = nt_ref[...].reshape(devices, half, C)
+    both = keep_ref[...].astype(F32) + came_ref[...].astype(F32)
+    out_ref[:, half : 2 * half, :] = both.astype(BF16)
+
+
 def sums_kernel(
-    core_ref, both_hbm, xt_hbm, nt_hbm, got_ref, norm_ref, wb_ref,
-    z_ref, sums_hbm, z_scr, s_scr, sums_ref, xt_ref, nt_ref, sems,
+    core_ref, held_ref, got_ref, norm_ref, gain_ref, shift_ref, wb_ref,
+    z_ref, sums_hbm, z_scr, s_scr, sums_ref, sems,
 ):
     core = core_ref[0]
     rows, cols = got_ref.shape[0], 32
-    copies = [
-        pltpu.make_async_copy(xt_hbm, xt_ref, sems.at[0]),
-        pltpu.make_async_copy(nt_hbm, nt_ref, sems.at[1]),
-        pltpu.make_async_copy(both_hbm, sums_ref.at[:, 16:32, :], sems.at[2]),
-    ]
-    for copy in copies:
-        copy.start()
+    last = pltpu.make_async_copy(held_ref.at[:, 16:32, :], sums_hbm.at[:, 16:32, :], sems.at[0])
+    last.start()
     z_scr[...] = jnp.zeros_like(z_scr)
     for pair in range(2):
 
@@ -280,88 +290,78 @@
                 ]
     z = z_scr[...].astype(BF16)
     z_ref[...] = z
-    copies[2].wait()
-    last = pltpu.make_async_copy(sums_ref.at[:, 16:32, :], sums_hbm.at[:, 16:32, :], sems.at[3])
-    last.start()
-    copies[0].wait()
-    copies[1].wait()
-    dwb = dot_nn(z, xt_ref[...])
-    dgn = dot_nn(z, nt_ref[...])
+    nt = held_ref[:, 0:16, :].reshape(z.shape[1], C)
+    dgn = dot_nn(z, nt)[0:4]
+    total = jnp.sum(z_scr[0:4, :], axis=1, keepdims=True)
 
     def add_w(i, total):
         return total + got_ref[i, core, cols : cols + 8, :].astype(F32)
 
     s_scr[0:8, :] = lax.fori_loop(0, rows, add_w, jnp.zeros((8, C), F32), unroll=8)
-    s_scr[8:12, :] = dwb[0:4]
+    s_scr[8:12, :] = dgn * gain_ref[...] + total * shift_ref[...]
     wb = wb_ref[...].astype(F32)
     dgain = jnp.sum(norm_ref[0:8, :], axis=0, keepdims=True)
-    dgain = dgain + jnp.sum(dgn[0:4] * wb, axis=0, keepdims=True)
+    dgain = dgain + jnp.sum(dgn * wb, axis=0, keepdims=True)
     dshift = jnp.sum(norm_ref[8:16, :], axis=0, keepdims=True)
-    total = jnp.sum(z_scr[0:4, :], axis=1, keepdims=True)
     dshift = dshift + jnp.sum(total * wb, axis=0, keepdims=True)
     s_scr[12:13, :] = dgain
     s_scr[13:14, :] = dshift
     s_scr[14:15, :] = dgain - dgain.astype(BF16).astype(F32)
     s_scr[15:16, :] = dshift - dshift.astype(BF16).astype(F32)
-    sums_ref[:, 0:16, :] = jnp.broadcast_to(s_scr[...].astype(BF16)[None], (2 * rows, 16, C))
-    first = pltpu.make_async_copy(sums_ref.at[:, 0:16, :], sums_hbm.at[:, 0:16, :], sems.at[4])
+    sums_ref[...] = jnp.broadcast_to(s_scr[...].astype(BF16)[None], sums_ref.shape)
+    first = pltpu.make_async_copy(sums_ref, sums_hbm.at[:, 0:16, :], sems.at[1])
     first.start()
     last.wait()
     first.wait()
 
 
-def ready_kernel(
-    z_ref, pair_ref, wb_ref, dxb_hbm, normed_hbm, rstd_hbm,
-    dxb_scr, wb_scr, dxb_ref, normed_ref, rstd_ref, sems,
-):
+def ready_kernel(z_ref, pair_ref, gain_ref, wb_ref, ready_ref, dxb_scr, wb_scr):
     rows, cols = pair_ref.shape[0], pair_ref.shape[1]
     wb_scr[...] = jnp.zeros_like(wb_scr)
     wb_scr[0:4, :] = wb_ref[...].astype(F32)
     dxb_scr[...] = dot_tn(z_ref[...], wb_scr[...].astype(BF16))
+    gain = gain_ref[...]
 
     def some(it, carry):
         i0 = it * 8
         part = pl.ds(i0, 8)
         normed, rstd = normalize(pair_ref[part].astype(F32))
-        normed_ref[part] = normed
-        rstd_ref[part] = jnp.broadcast_to(rstd, normed.shape)
-        for u in range(8):
-            dxb_ref[i0 + u] = dxb_scr[pl.ds(i0 + u, cols, stride=rows), :]
+        ready_ref[part, cols : 2 * cols, :] = normed.astype(BF16)
+        ready_ref[part, 2 * cols : 3 * cols, :] = jnp.broadcast_to(rstd, normed.shape).astype(BF16)
+        dxb = [dxb_scr[pl.ds(i0 + u, cols, stride=rows), :][None] for u in range(8)]
+        dn = jnp.concatenate(dxb, axis=0) * gain
+        base = rstd * (
+            dn
+            - jnp.mean(dn, axis=-1, keepdims=True)
+            - normed * jnp.mean(dn * normed, axis=-1, keepdims=True)
+        )
+        ready_ref[part, 0:cols, :] = base.astype(BF16)
         return carry
 
     lax.fori_loop(0, rows // 8, some, 0)
-    copies = [
-        pltpu.make_async_copy(src, dst, sems.at[i])
-        for i, (src, dst) in enumerate(
-            ((dxb_ref, dxb_hbm), (normed_ref, normed_hbm), (rstd_ref, rstd_hbm))
-        )
-    ]
-    for copy in copies:
+
+
+def final_kernel(
+    ready_ref, got_ref, gain_ref,
+    dpair_hbm, dgain_ref, dshift_ref, dq_hbm, dk_hbm, dv_hbm, dg_hbm, db_ref, do_hbm,
+    w_scr, dpair_ref, turn_scr, out_sems, w_sems,
+):
+    chips, cols, parts = got_ref.shape[0], dpair_ref.shape[1], out_sems.shape[0]
+    size = chips // parts
+    for core in range(2):
+        for i in range(chips):
+            w_scr[core, 5 * i : 5 * i + 8, :] = got_ref[i, core, 0:16, :].astype(F32)[0:8]
+    sent = []
+    for slot, out in enumerate((dq_hbm, dg_hbm, dk_hbm, dv_hbm)):
+        sl = slice(slot * 64, (slot + 1) * 64)
+        heads = jnp.concatenate([w_scr[0, sl, :], w_scr[1, sl, :]], axis=0)
+        turn_scr[slot] = jnp.transpose(heads)
+        sent.append(pltpu.make_async_copy(turn_scr.at[slot], out, w_sems.at[slot]))
+    turn_scr[4, 0:64, :] = w_scr[0, 256:320, :]
+    turn_scr[4, 64:128, :] = w_scr[1, 256:320, :]
+    sent.append(pltpu.make_async_copy(turn_scr.at[4], do_hbm, w_sems.at[4]))
+    for copy in sent:
         copy.start()
-    for copy in copies:
-        copy.wait()
-
-
-def final_kernel(
-    dxb_hbm, normed_hbm, rstd_hbm, got_ref, gain_ref,
-    dpair_hbm, dgain_ref, dshift_ref, dq_ref, dk_ref, dv_ref, dg_ref, db_ref, do_ref,
-    w_scr, dxb_ref, normed_ref, rstd_ref, dpair_ref, sems, out_sems,
-):
-    chips, cols, parts = got_ref.shape[0], dxb_ref.shape[1], out_sems.shape[0]
-    size = chips // parts
-    fetched = []
-    for p in range(parts):
-        part = pl.ds(p * size, size)
-        fetched.append(
-            [
-                pltpu.make_async_copy(src.at[part], dst.at[part], sems.at[i, p])
-                for i, (src, dst) in enumerate(
-                    ((dxb_hbm, dxb_ref), (normed_hbm, normed_ref), (rstd_hbm, rstd_ref))
-                )
-            ]
-        )
-        for copy in fetched[-1]:
-            copy.start()
     zero = jnp.zeros((16, C), F32)
 
     def add(i, total):
@@ -372,37 +372,17 @@
     dgain_ref[...] = total[12:13] + total[14:15]
     dshift_ref[...] = total[13:14] + total[15:16]
     gain = gain_ref[...]
-    sent = []
     for p in range(parts):
-        for copy in fetched[p]:
-            copy.wait()
-
-        def some(it, carry, p=p):
-            part = pl.ds(p * size + it * 8, 8)
-            normed, rstd = normed_ref[part], rstd_ref[part]
-            dx = jnp.concatenate([got_ref[part, 0, 16:32, :], got_ref[part, 1, 16:32, :]], axis=1)
-            dn = (dx.astype(F32) + dxb_ref[part]) * gain
-            out = rstd * (
-                dn
-                - jnp.mean(dn, axis=-1, keepdims=True)
-                - normed * jnp.mean(dn * normed, axis=-1, keepdims=True)
-            )
-            dpair_ref[part] = out.astype(BF16)
-            return carry
-
-        lax.fori_loop(0, size // 8, some, 0)
         part = pl.ds(p * size, size)
+        normed = ready_ref[part, cols : 2 * cols, :].astype(F32).reshape(size * cols, C)
+        dx = jnp.concatenate([got_ref[part, 0, 16:32, :], got_ref[part, 1, 16:32, :]], axis=1)
+        dn = dx.astype(F32).reshape(size * cols, C) * gain
+        out = dn - mean_lanes(dn) - normed * mean_lanes(dn * normed)
+        rstd = ready_ref[part, 2 * cols : 3 * cols, :].astype(F32)
+        out = out.reshape(size, cols, C) * rstd + ready_ref[part, 0:cols, :].astype(F32)
+        dpair_ref[part] = out.astype(BF16)
         sent.append(pltpu.make_async_copy(dpair_ref.at[part], dpair_hbm.at[part], out_sems.at[p]))
         sent[-1].start()
-    for core in range(2):
-        for i in range(chips):
-            w_scr[core, 5 * i : 5 * i + 8, :] = got_ref[i, core, 0:16, :].astype(F32)[0:8]
-    for slot, ref in enumerate((dq_ref, dg_ref, dk_ref, dv_ref)):
-        sl = slice(slot * 64, (slot + 1) * 64)
-        heads = jnp.concatenate([w_scr[0, sl, :], w_scr[1, sl, :]], axis=0)
-        ref[...] = jnp.transpose(heads)
-    do_ref[0:64, :] = w_scr[0, 256:320, :]
-    do_ref[64:128, :] = w_scr[1, 256:320, :]
     for copy in sent:
         copy.wait()
 
@@ -418,11 +398,10 @@
     wb = w_bias.T
     core = (lax.axis_index("col") % 2).astype(jnp.int32).reshape(1)
 
-    turned = sds((rows * cols, C), BF16)
     turned_scr = pltpu.VMEM((rows * cols, C), BF16)
-    packed, xt, nt = call(
+    packed, nt = call(
         pack_kernel,
-        (sds((rows, 2, 64, C), BF16), turned, turned),
+        (sds((rows, 2, 64, C), BF16), sds((rows * cols, C), BF16)),
         0,
         (
             pltpu.VMEM((rows * cols, C), F32),
@@ -430,6 +409,7 @@
             pltpu.VMEM((1, C), F32),
             pltpu.VMEM((1, C), F32),
             pltpu.VMEM((H, C), BF16),
+            turned_scr,
             pltpu.SemaphoreType.DMA((5,)),
         ),
         hbm=5,
@@ -474,45 +454,34 @@
         moved=6 * MIB,
     )(core, mine, other, spread, turned_w)
     came = lax.ppermute(send, "col", swap)
-    both = (keep.astype(F32) + came.astype(F32)).astype(BF16)
+    held = call(
+        merge_kernel, sds((devices, cols, C), BF16), 3, flops=10**7, moved=2 * MIB
+    )(keep, came, nt)
     z, sums = call(
         sums_kernel,
         (sds((8, rows * cols), BF16), pltpu.HBM((devices, 32, C), BF16)),
-        3,
+        6,
         (
             pltpu.VMEM((8, rows * cols), F32),
             pltpu.VMEM((16, C), F32),
-            pltpu.VMEM((devices, 32, C), BF16),
-            turned_scr,
-            turned_scr,
-            pltpu.SemaphoreType.DMA((5,)),
+            pltpu.VMEM((devices, 16, C), BF16),
+            pltpu.SemaphoreType.DMA((2,)),
         ),
         smem=1,
-        hbm=3,
         to_hbm=(1,),
         flops=10**8,
         moved=4 * MIB,
-    )(core, in_hbm(both), in_hbm(xt), in_hbm(nt), got, norms, wb)
+    )(core, held, got, norms, gain, shift, wb)
     last = lax.all_to_all(sums, axes, 0, 0, tiled=True).reshape(rows, 2, 32, C)
-    tile = pltpu.HBM(pair.shape, F32)
-    tile_scr = pltpu.VMEM(pair.shape, F32)
-    dxb, normed, rstd = call(
+    ready = call(
         ready_kernel,
-        (tile, tile, tile),
-        3,
-        (
-            pltpu.VMEM((rows * cols, C), F32),
-            pltpu.VMEM((8, C), F32),
-            tile_scr,
-            tile_scr,
-            tile_scr,
-            pltpu.SemaphoreType.DMA((3,)),
-        ),
-        to_hbm=(0, 1, 2),
+        sds((rows, 3 * cols, C), BF16),
+        4,
+        (pltpu.VMEM((rows * cols, C), F32), pltpu.VMEM((8, C), F32)),
         flops=10**8,
         moved=8 * MIB,
-    )(z, pair, wb)
-    square = sds((C, C), F32)
+    )(z, pair, gain, wb)
+    square = pltpu.HBM((C, C), F32)
     d_pair, d_gain, d_shift, d_query, d_key, d_value, d_gate, d_bias, d_out = call(
         final_kernel,
         (
@@ -526,20 +495,17 @@
             sds((H, C), F32),
             square,
         ),
-        2,
+        3,
         (
             pltpu.VMEM((2, 328, C), F32),
-            tile_scr,
-            tile_scr,
-            tile_scr,
             pltpu.VMEM(pair.shape, BF16),
-            pltpu.SemaphoreType.DMA((3, 4)),
+            pltpu.VMEM((5, C, C), F32),
             pltpu.SemaphoreType.DMA((4,)),
+            pltpu.SemaphoreType.DMA((5,)),
         ),
-        hbm=3,
-        to_hbm=(0,),
+        to_hbm=(0, 3, 4, 5, 6, 8),
         moved=8 * MIB,
-    )(in_hbm(dxb), in_hbm(normed), in_hbm(rstd), last, gain)
+    )(ready, last, gain)
     return (
         d_pair,
         d_gain.reshape(C),

time: 124 us -> 121 us (0.976)
  Pallas kernels: 32.8 us -> 28.3 us
  waiting for transfers between devices: 32.6 us -> 34.5 us
    pallas_call x1, Pallas kernels: 3.93 us -> 2.12 us  [on_device(): call(final_kernel, (pltpu.HBM(pair.shape, BF16), sds((1, C), F32), sds((1...]
    pallas_call x2 -> x3, Pallas kernels: 6.33 us -> 5.34 us  [the longest x1 2.59 us: on_device(): call(ready_kernel, sds((rows, 3 * cols, C), BF16), 4, (pltpu.VMEM((rows *...]
  transfers between devices with their start and end apart: 4 -> 4, of which waited for: 4 -> 4; matrix products, arithmetic and copies ran while one was open for 1% -> 0% of each run, Pallas kernels for 5% -> 4%
where the time goes in v4:
time: 121 us; the launch traced here: 120 us
  blocking collectives  41.8 us (35%)
  waiting for transfers between devices  34.5 us (29%)
  Pallas kernels  28.3 us (23%)
  starting transfers between devices  10.6 us (9%)
  local copies, waits for them, and re-layouts  3.96 us (3%)
    all_to_all x1, blocking collectives, on_device(): lax.all_to_all(packed.reshape(devices, 64, C), axes, 0, 0, tiled=True)  41.8 us
    pallas_call x1, Pallas kernels, on_device(): call(attend_kernel, (pltpu.HBM((devices, 40, C), BF16), pltpu.HBM((8, 256...  16.9 us
    all_to_all x1, waiting for transfers between devices, on_device(): last = lax.all_to_all(sums, axes, 0, 0, tiled=True).reshape(rows, 2, 32, C)  16.7 us
    all_to_all x1, waiting for transfers between devices, on_device(): got = lax.all_to_all(terms, axes, 0, 0, tiled=True).reshape(rows, 2, 40, C)  13.8 us
    all_to_all x1, starting transfers between devices, on_device(): last = lax.all_to_all(sums, axes, 0, 0, tiled=True).reshape(rows, 2, 32, C)  4.5 us
    all_to_all x1, starting transfers between devices, on_device(): got = lax.all_to_all(terms, axes, 0, 0, tiled=True).reshape(rows, 2, 40, C)  4.28 us
    unnamed x28, local copies, waits for them, and re-layouts  2.87 us
    pallas_call x1, Pallas kernels, on_device(): call(ready_kernel, sds((rows, 3 * cols, C), BF16), 4, (pltpu.VMEM((rows *...  2.59 us
  transfers between devices with their start and end apart: 4, of which 4 were waited for; matrix products, arithmetic and copies ran while one was open for 0% of the time, Pallas kernels for 4%

profile of v4, /device:TPU:1, one launch (start us, length us, event | category | flops | bytes accessed | tf_op | source)
XLA Modules:
  0.0 120.2 jit_solution(2328180288526200939)
XLA Ops:
  0.6 2.6 %shard_map.169 = (bf16[64,2,64,128]{3,2,1,0:T(8,128)(2,1)S(1)}, bf16[2048,128]{1,0:T(8,128)(2,1)S(1)}) custom-call(bf16[64,32,128]{2,1,0:T(8,128)(2,1)} %pair_ref.1, bf16[64,32,128]{2,1,0:T(8,128)(2,1)} %grad_hbm.1, f32[1,128]{1,0:T(1,128)} %bitcast.16, f32[1,128]{1,0:T(1,128)} %bitcast.21, bf16[4,128]{1,0:T(4,128)(2,1)} %bitcast.13), custom_call_target="tpu_custom_call" | custom-call | flops 100000000 | bytes 4194304 | tf_op jit(solution)/shard_map/pallas_call | solution.py:402
  3.2 0.0 copy-start.4
  3.2 41.8 %all_to_all.15.mine_ref = bf16[128,64,128]{2,1,0:T(8,128)(2,1)S(1)} all-to-all(bf16[128,64,128]{2,1,0:T(8,128)(2,1)S(1)} %bitcast.12), channel_id=1, replica_groups=mesh['row'=8,'col'=16] {'row','col'}, dimensions={0} | all-to-all | bytes 4194304 | tf_op jit(solution)/shard_map/all_to_all | solution.py:419
  45.0 0.0 copy-done.4
  45.0 0.0 copy-start.10
  45.0 0.0 copy-start.11
  45.1 0.0 copy-start.12
  45.1 0.0 copy-start.13
  45.1 1.1 slice.4
  46.2 0.5 collective-permute-start
  46.7 2.5 %collective-permute-done.other_ref = bf16[128,32,128]{2,1,0:T(8,128)(2,1)S(1)} collective-permute-done((bf16[128,32,128]{2,1,0:T(8,128)(2,1)}, bf16[128,32,128]{2,1,0:T(8,128)(2,1)S(1)}, u32[]{:S(2)}, u32[]{:S(2)}) %collective-permute-start) | collective-permute-done | bytes 1048608 | tf_op jit(solution)/shard_map/ppermute | solution.py:421
  49.2 0.0 copy-done.7
  49.2 0.0 copy-done.8
  49.3 16.9 %shard_map.170 = (bf16[128,40,128]{2,1,0:T(8,128)(2,1)}, bf16[8,256,512]{2,1,0:T(8,128)(2,1)}, bf16[320,128]{1,0:T(8,128)(2,1)S(1)}) custom-call(s32[1]{0:T(128)} %bitcast.core_ref, bf16[128,64,128]{2,1,0:T(8,128)(2,1)S(1)} %all_to_all.15.mine_ref, bf16[128,32,128]{2,1,0:T(8,128)(2,1)S(1)} %collective-permute-done.other_ref, f32[1,128]{1,0:T(1,128)S(1)} %bitcast.17, ...), custom_call_target="tpu_custom_call" | custom-call | flops 10000000000 | bytes 6291456 | tf_op jit(solution)/shard_map/pallas_call | solution.py:422
  66.2 0.0 copy-done.2
  66.2 4.3 %all-to-all-start.1 = ((bf16[128,40,128]{2,1,0:T(8,128)(2,1)}), bf16[128,40,128]{2,1,0:T(8,128)(2,1)S(1)}, u32[]{:S(2)}, u32[]{:S(2)}) async-start(bf16[128,40,128]{2,1,0:T(8,128)(2,1)} %get-tuple-element.34), calls=%async_computation.1 | async-start | bytes 2621440 | tf_op jit(solution)/shard_map/all_to_all | solution.py:446
  70.5 1.6 %copy-done = bf16[8,256,512]{2,1,0:T(8,128)(2,1)S(1)} copy-done((bf16[8,256,512]{2,1,0:T(8,128)(2,1)S(1)}, bf16[8,256,512]{2,1,0:T(8,128)(2,1)}, u32[]{:S(2)}) %copy-start) | copy-done | bytes 2097176
  72.1 1.2 %copy-done.3 = bf16[128,32,128]{2,1,0:T(8,128)(2,1)S(1)} copy-done((bf16[128,32,128]{2,1,0:T(8,128)(2,1)S(1)}, bf16[128,32,128]{2,1,0:T(8,128)(2,1)}, u32[]{:S(2)}) %copy-start.3) | copy-done | bytes 1048600
  73.3 2.4 %shard_map.171 = (bf16[128,16,128]{2,1,0:T(8,128)(2,1)S(1)}, bf16[128,16,128]{2,1,0:T(8,128)(2,1)S(1)}, f32[16,128]{1,0:T(8,128)S(1)}) custom-call(s32[1]{0:T(128)} %bitcast.core_ref, bf16[128,64,128]{2,1,0:T(8,128)(2,1)S(1)} %all_to_all.15.mine_ref, bf16[128,32,128]{2,1,0:T(8,128)(2,1)S(1)} %copy-done.3, bf16[8,256,512]{2,1,0:T(8,128)(2,1)S(1)} %copy-done, ...), custom_call_target="tpu_custom_call" | custom-call | flops 1000000000 | bytes 6291456 | tf_op jit(solution)/shard_map/pallas_call | solution.py:448
  75.7 0.0 copy-start.6
  75.8 1.3 %collective-permute-start.1 = (bf16[128,16,128]{2,1,0:T(8,128)(2,1)S(1)}, bf16[128,16,128]{2,1,0:T(8,128)(2,1)S(1)}, u32[]{:S(2)}, u32[]{:S(2)}) collective-permute-start(bf16[128,16,128]{2,1,0:T(8,128)(2,1)S(1)} %get-tuple-element.32), channel_id=1, source_target_pairs={{0,1},{1,0},{2,3},{3,2},{4,5},{5,4},{6,7},{7,6},{8,9},{9,8},{10,11... | collective-permute-start | bytes 1572872 | tf_op jit(solution)/shard_map/ppermute | solution.py:456
  77.1 1.5 %collective-permute-done.1.came_ref = bf16[128,16,128]{2,1,0:T(8,128)(2,1)S(1)} collective-permute-done((bf16[128,16,128]{2,1,0:T(8,128)(2,1)S(1)}, bf16[128,16,128]{2,1,0:T(8,128)(2,1)S(1)}, u32[]{:S(2)}, u32[]{:S(2)}) %collective-permute-start.1) | collective-permute-done | bytes 524320 | tf_op jit(solution)/shard_map/ppermute | solution.py:456
  78.6 0.0 copy-done.5
  78.6 0.2 shard_map.172.held_ref
  78.8 13.8 %all-to-all-done.1 = bf16[128,40,128]{2,1,0:T(8,128)(2,1)S(1)} async-done(((bf16[128,40,128]{2,1,0:T(8,128)(2,1)}), bf16[128,40,128]{2,1,0:T(8,128)(2,1)S(1)}, u32[]{:S(2)}, u32[]{:S(2)}) %all-to-all-start.1) | async-done | bytes 1310752 | tf_op jit(solution)/shard_map/all_to_all | solution.py:446
  92.6 1.5 %shard_map.173 = (bf16[8,2048]{1,0:T(8,128)(2,1)S(1)}, bf16[128,32,128]{2,1,0:T(8,128)(2,1)}) custom-call(s32[1]{0:T(128)} %bitcast.core_ref, bf16[128,32,128]{2,1,0:T(8,128)(2,1)S(1)} %shard_map.172.held_ref, bf16[64,2,40,128]{3,2,1,0:T(8,128)(2,1)S(1)} %bitcast.10, f32[16,128]{1,0:T(8,128)S(1)} %get-tuple-element.35.norm_ref, f32[1,128]{1,0:T(1,128)S(1)} %bitcast.18, ...), custom_call_target="tpu_custom_call" | custom-call | flops 100000000 | bytes 4194304 | tf_op jit(solution)/shard_map/pallas_call | solution.py:460
  94.2 0.0 copy-start.1
  94.2 4.5 %all-to-all-start.2 = ((bf16[128,32,128]{2,1,0:T(8,128)(2,1)}), bf16[128,32,128]{2,1,0:T(8,128)(2,1)S(1)}, u32[]{:S(2)}, u32[]{:S(2)}) async-start(bf16[128,32,128]{2,1,0:T(8,128)(2,1)} %get-tuple-element.37), calls=%async_computation.2 | async-start | bytes 2097152 | tf_op jit(solution)/shard_map/all_to_all | solution.py:475
  98.7 0.0 copy-done.1
  98.7 2.6 %shard_map.174.ready_ref = bf16[64,96,128]{2,1,0:T(8,128)(2,1)S(1)} custom-call(bf16[8,2048]{1,0:T(8,128)(2,1)S(1)} %get-tuple-element.36.z_ref, bf16[64,32,128]{2,1,0:T(8,128)(2,1)S(1)} %copy-done.1, f32[1,128]{1,0:T(1,128)S(1)} %bitcast.19, bf16[4,128]{1,0:T(4,128)(2,1)S(1)} %bitcast.15), custom_call_target="tpu_custom_call" | custom-call | flops 100000000 | bytes 8388608 | tf_op jit(solution)/shard_map/pallas_call | solution.py:476
  101.3 16.7 %all-to-all-done.2 = bf16[128,32,128]{2,1,0:T(8,128)(2,1)S(1)} async-done(((bf16[128,32,128]{2,1,0:T(8,128)(2,1)}), bf16[128,32,128]{2,1,0:T(8,128)(2,1)S(1)}, u32[]{:S(2)}, u32[]{:S(2)}) %all-to-all-start.2) | async-done | bytes 1048608 | tf_op jit(solution)/shard_map/all_to_all | solution.py:475
  117.9 2.1 %shard_map.175 = (bf16[64,32,128]{2,1,0:T(8,128)(2,1)}, f32[1,128]{1,0:T(1,128)}, f32[1,128]{1,0:T(1,128)}, f32[128,128]{1,0:T(8,128)}, f32[128,128]{1,0:T(8,128...) custom-call(bf16[64,96,128]{2,1,0:T(8,128)(2,1)S(1)} %shard_map.174.ready_ref, ...), custom_call_target="tpu_custom_call" | custom-call | bytes 8388608 | tf_op jit(solution)/shard_map/pallas_call | solution.py:485
  (13 shorter events, 0.0 us)
Async XLA Ops:
  3.2 41.8 %copy-start.4 = (bf16[2048,128]{1,0:T(8,128)(2,1)}, bf16[2048,128]{1,0:T(8,128)(2,1)S(1)}, u32[]{:S(2)}) copy-start(bf16[2048,128]{1,0:T(8,128)(2,1)S(1)} %get-tuple-element.33.nt_ref) | copy-start | bytes 1572868
  45.0 4.2 %copy-start.7 = (f32[128]{0:T(128)S(1)}, f32[128]{0:T(128)}, u32[]{:S(2)}) copy-start(f32[128]{0:T(128)} %param.12) | copy-start | bytes 1540
  45.0 4.2 %copy-start.8 = (f32[128]{0:T(128)S(1)}, f32[128]{0:T(128)}, u32[]{:S(2)}) copy-start(f32[128]{0:T(128)} %param.13) | copy-start | bytes 1540
  45.0 4.2 %copy-start.9 = (bf16[128,128]{1,0:T(8,128)(2,1)S(1)}, bf16[128,128]{1,0:T(8,128)(2,1)}, u32[]{:S(2)}) copy-start(bf16[128,128]{1,0:T(8,128)(2,1)} %wq_ref.1) | copy-start | bytes 98308
  45.0 4.2 %copy-start.10 = (bf16[128,128]{1,0:T(8,128)(2,1)S(1)}, bf16[128,128]{1,0:T(8,128)(2,1)}, u32[]{:S(2)}) copy-start(bf16[128,128]{1,0:T(8,128)(2,1)} %wk_ref.1) | copy-start | bytes 98308
  45.0 4.2 %copy-start.11 = (bf16[128,128]{1,0:T(8,128)(2,1)S(1)}, bf16[128,128]{1,0:T(8,128)(2,1)}, u32[]{:S(2)}) copy-start(bf16[128,128]{1,0:T(8,128)(2,1)} %wv_ref.1) | copy-start | bytes 98308
  45.1 4.2 %copy-start.12 = (bf16[128,128]{1,0:T(8,128)(2,1)S(1)}, bf16[128,128]{1,0:T(8,128)(2,1)}, u32[]{:S(2)}) copy-start(bf16[128,128]{1,0:T(8,128)(2,1)} %wg_ref.1) | copy-start | bytes 98308
  45.1 4.2 %copy-start.13 = (bf16[128,128]{1,0:T(8,128)(2,1)S(1)}, bf16[128,128]{1,0:T(8,128)(2,1)}, u32[]{:S(2)}) copy-start(bf16[128,128]{1,0:T(8,128)(2,1)} %wo_ref.1) | copy-start | bytes 98308
  46.2 3.0 %collective-permute-start = (bf16[128,32,128]{2,1,0:T(8,128)(2,1)}, bf16[128,32,128]{2,1,0:T(8,128)(2,1)S(1)}, u32[]{:S(2)}, u32[]{:S(2)}) collective-permute-start(bf16[128,32,128]{2,1,0:T(8,128)(2,1)} %slice.4), channel_id=1, source_target_pairs={{0,1},{1,0},{2,3},{3,2},{4,5},{5,4},{6,7},{7,6},{8,9},{9,8},{10,11... | collective-permute-start | bytes 3145736 | tf_op jit(solution)/shard_map/ppermute | solution.py:421
  49.2 17.0 %copy-start.2 = (bf16[128,32,128]{2,1,0:T(8,128)(2,1)}, bf16[128,32,128]{2,1,0:T(8,128)(2,1)S(1)}, u32[]{:S(2)}) copy-start(bf16[128,32,128]{2,1,0:T(8,128)(2,1)S(1)} %collective-permute-done.other_ref) | copy-start | bytes 3145732
  66.2 26.4 %all-to-all-start.1 = ((bf16[128,40,128]{2,1,0:T(8,128)(2,1)}), bf16[128,40,128]{2,1,0:T(8,128)(2,1)S(1)}, u32[]{:S(2)}, u32[]{:S(2)}) async-start(bf16[128,40,128]{2,1,0:T(8,128)(2,1)} %get-tuple-element.34), calls=%async_computation.1 | async-start | bytes 2621440 | tf_op jit(solution)/shard_map/all_to_all | solution.py:446
  70.5 1.6 %copy-start = (bf16[8,256,512]{2,1,0:T(8,128)(2,1)S(1)}, bf16[8,256,512]{2,1,0:T(8,128)(2,1)}, u32[]{:S(2)}) copy-start(bf16[8,256,512]{2,1,0:T(8,128)(2,1)} %get-tuple-element.29.d_ref) | copy-start | bytes 6291460
  72.1 1.2 %copy-start.3 = (bf16[128,32,128]{2,1,0:T(8,128)(2,1)S(1)}, bf16[128,32,128]{2,1,0:T(8,128)(2,1)}, u32[]{:S(2)}) copy-start(bf16[128,32,128]{2,1,0:T(8,128)(2,1)} %copy-done.2) | copy-start | bytes 3145732
  73.3 5.3 %copy-start.5 = (bf16[2048,128]{1,0:T(8,128)(2,1)S(1)}, bf16[2048,128]{1,0:T(8,128)(2,1)}, u32[]{:S(2)}) copy-start(bf16[2048,128]{1,0:T(8,128)(2,1)} %copy-done.4) | copy-start | bytes 1572868
  75.7 16.9 %copy-start.6 = (bf16[128,4]{0,1:T(4,128)(2,1)S(1)}, bf16[128,4]{0,1:T(4,128)(2,1)}, u32[]{:S(2)}) copy-start(bf16[128,4]{0,1:T(4,128)(2,1)} %param.18) | copy-start | bytes 3076
  75.8 2.8 %collective-permute-start.1 = (bf16[128,16,128]{2,1,0:T(8,128)(2,1)S(1)}, bf16[128,16,128]{2,1,0:T(8,128)(2,1)S(1)}, u32[]{:S(2)}, u32[]{:S(2)}) collective-permute-start(bf16[128,16,128]{2,1,0:T(8,128)(2,1)S(1)} %get-tuple-element.32), channel_id=1, source_target_pairs={{0,1},{1,0},{2,3},{3,2},{4,5},{5,4},{6,7},{7,6},{8,9},{9,8},{10,11... | collective-permute-start | bytes 1572872 | tf_op jit(solution)/shard_map/ppermute | solution.py:456
  94.2 4.5 %copy-start.1 = (bf16[64,32,128]{2,1,0:T(8,128)(2,1)S(1)}, bf16[64,32,128]{2,1,0:T(8,128)(2,1)}, u32[]{:S(2)}) copy-start(bf16[64,32,128]{2,1,0:T(8,128)(2,1)} %pair_ref.1) | copy-start | bytes 1572868
  94.2 23.8 %all-to-all-start.2 = ((bf16[128,32,128]{2,1,0:T(8,128)(2,1)}), bf16[128,32,128]{2,1,0:T(8,128)(2,1)S(1)}, u32[]{:S(2)}, u32[]{:S(2)}) async-start(bf16[128,32,128]{2,1,0:T(8,128)(2,1)} %get-tuple-element.37), calls=%async_computation.2 | async-start | bytes 2097152 | tf_op jit(solution)/shard_map/all_to_all | solution.py:475

commit v5 on v4

--- a/solution.py
+++ b/solution.py
@@ -100,9 +100,27 @@
     copies[-1].wait()
 
 
+def prepare_kernel(core_ref, mine_ref, wq_ref, wk_ref, wv_ref, wg_ref, wo_ref, bias_ref, w_ref):
+    core = core_ref[0]
+    groups, blocks, cols = 8, 16, 32
+    n = blocks * cols
+    low = lax.broadcasted_iota(jnp.int32, (n, C), 1) < 64
+    for slot, ref in enumerate((wq_ref, wg_ref, wk_ref, wv_ref)):
+        turned = jnp.transpose(ref[...].astype(F32)).astype(BF16)
+        w_ref[slot * 64 : (slot + 1) * 64, :] = jnp.where(core == 0, turned[0:64], turned[64:128])
+    w_ref[256:320, :] = jnp.where(core == 0, wo_ref[0:64, :], wo_ref[64:128, :])
+    for r in range(0, groups, 2):
+        b0 = mine_ref[r * blocks : (r + 1) * blocks, cols : 2 * cols, :].reshape(n, C).astype(F32)
+        b1 = mine_ref[(r + 1) * blocks : (r + 2) * blocks, cols : 2 * cols, :].reshape(n, C)
+        b1 = b1.astype(F32)
+        sl = slice(r * 64, r * 64 + 128)
+        bias_ref[0, :, sl] = jnp.where(low, b0, pltpu.roll(b1, 64, 1)) * LOG2E
+        bias_ref[1, :, sl] = jnp.where(low, pltpu.roll(b0, 64, 1), b1) * LOG2E
+
+
 def attend_kernel(
-    core_ref, mine_ref, other_ref, gain_ref, shift_ref, wq_ref, wk_ref, wv_ref, wg_ref, wo_ref,
-    out_hbm, d_hbm, w_scr, bias_scr, acc_scr, wacc_scr, rhs_scr, out_ref, d_ref, sems, d_sems,
+    core_ref, mine_ref, other_ref, gain_ref, shift_ref, bias_ref, w_ref,
+    out_hbm, d_hbm, acc_scr, wacc_scr, rhs_scr, out_ref, d_ref, sems, d_sems,
 ):
     core = core_ref[0]
     groups, blocks, cols, step_rows = 8, 16, 32, 4
@@ -110,19 +128,6 @@
     scale = DH ** (-0.5)
     lane = lax.broadcasted_iota(jnp.int32, (n, C), 1)
     low = lane < 64
-
-    for slot, ref in enumerate((wq_ref, wg_ref, wk_ref, wv_ref)):
-        turned = jnp.transpose(ref[...].astype(F32)).astype(BF16)
-        w_scr[slot * 64 : (slot + 1) * 64, :] = jnp.where(core == 0, turned[0:64], turned[64:128])
-    w_scr[256:320, :] = jnp.where(core == 0, wo_ref[0:64, :], wo_ref[64:128, :])
-
-    for r in range(0, groups, 2):
-        b0 = mine_ref[r * blocks : (r + 1) * blocks, cols : 2 * cols, :].reshape(n, C).astype(F32)
-        b1 = mine_ref[(r + 1) * blocks : (r + 2) * blocks, cols : 2 * cols, :].reshape(n, C)
-        b1 = b1.astype(F32)
-        sl = slice(r * 64, r * 64 + 128)
-        bias_scr[0, :, sl] = jnp.where(low, b0, pltpu.roll(b1, 64, 1)) * LOG2E
-        bias_scr[1, :, sl] = jnp.where(low, pltpu.roll(b0, 64, 1), b1) * LOG2E
     acc_scr[...] = jnp.zeros_like(acc_scr)
     wacc_scr[...] = jnp.zeros_like(wacc_scr)
     rhs_scr[...] = jnp.zeros_like(rhs_scr)
@@ -136,14 +141,14 @@
             grad = jnp.where(core == 0, other, mine)
             normed, _ = normalize(pair.astype(F32))
             x = (normed * gain_ref[...] + shift_ref[...]).astype(BF16)
-            wide = dot_nt(w_scr[0:256, :], x)
+            wide = dot_nt(w_ref[0:256, :], x)
             q_t = wide[0:64].astype(BF16)
             gate = jax.nn.sigmoid(wide[64:128])
             k_t = wide[128:192].astype(BF16)
             v_t = wide[192:256].astype(BF16)
-            dgated = dot_nt(w_scr[256:320, :], grad)
+            dgated = dot_nt(w_ref[256:320, :], grad)
             dob_t = (dgated * gate).astype(BF16)
-            kv = dot_nt(x, w_scr[128:256, :]).astype(BF16)
+            kv = dot_nt(x, w_ref[128:256, :]).astype(BF16)
             row.update(x=x, grad=grad, gate=gate, dgated=dgated)
             for h in range(2):
                 hs = slice(h * DH, (h + 1) * DH)
@@ -154,7 +159,7 @@
                 items[h].update(q=q_t[hs], k=k_t[hs], v=v_t[hs], dob=dob_t[hs])
 
         def score(t):
-            t["s"] = dot_nn(t["kv"], rhs_scr[t["slot"]]) * (scale * LOG2E) + bias_scr[t["h"]]
+            t["s"] = dot_nn(t["kv"], rhs_scr[t["slot"]]) * (scale * LOG2E) + bias_ref[t["h"]]
 
         def soften(t):
             expo = jnp.exp2(t["s"] - jnp.max(t["s"], axis=0, keepdims=True))
@@ -419,16 +424,19 @@
     mine = lax.all_to_all(packed.reshape(devices, 64, C), axes, 0, 0, tiled=True)
     swap = [(i, i ^ 1) for i in range(16)]
     other = lax.ppermute(mine[:, 0:cols, :], "col", swap)
-    terms, spread, turned_w = call(
+    bias, turned_w = call(
+        prepare_kernel,
+        (sds((2, 512, 512), F32), sds((320, C), BF16)),
+        6,
+        smem=1,
+        flops=10**8,
+        moved=4 * MIB,
+    )(core, mine, w_query, w_key, w_value, w_gate, w_out)
+    terms, spread = call(
         attend_kernel,
+        (pltpu.HBM((devices, 40, C), BF16), pltpu.HBM((8, 256, 512), BF16)),
+        6,
         (
-            pltpu.HBM((devices, 40, C), BF16),
-            pltpu.HBM((8, 256, 512), BF16),
-            sds((320, C), BF16),
-        ),
-        9,
-        (
-            pltpu.VMEM((2, 512, 512), F32),
             pltpu.VMEM((2, 512, 512), F32),
             pltpu.VMEM((328, C), F32),
             pltpu.VMEM((16, C, 512), BF16),
@@ -439,10 +447,10 @@
         ),
         smem=1,
         to_hbm=(0, 1),
-        vmem=36,
+        vmem=24,
         flops=10**10,
         moved=6 * MIB,
-    )(core, mine, other, gain, shift, w_query, w_key, w_value, w_gate, w_out)
+    )(core, mine, other, gain, shift, bias, turned_w)
     got = lax.all_to_all(terms, axes, 0, 0, tiled=True).reshape(rows, 2, 40, C)
     halves = sds((devices, cols // 2, C), BF16)
     keep, send, norms = call(

time: 121 us -> 120 us (level)
  transfers between devices with their start and end apart: 4 -> 4, of which waited for: 4 -> 4; matrix products, arithmetic and copies ran while one was open for 0% -> 0% of each run, Pallas kernels for 4% -> 5%
where the time goes in v5:
time: 120 us
  blocking collectives  41.8 us (35%)
  waiting for transfers between devices  34 us (28%)
  Pallas kernels  28.5 us (24%)
  starting transfers between devices  10.6 us (9%)
  local copies, waits for them, and re-layouts  3.98 us (3%)
    all_to_all x1, blocking collectives, on_device(): lax.all_to_all(packed.reshape(devices, 64, C), axes, 0, 0, tiled=True)  41.8 us
    all_to_all x1, waiting for transfers between devices, on_device(): last = lax.all_to_all(sums, axes, 0, 0, tiled=True).reshape(rows, 2, 32, C)  16.7 us
    pallas_call x1, Pallas kernels, on_device(): call(attend_kernel, (pltpu.HBM((devices, 40, C), BF16), pltpu.HBM((8, 256...  16.5 us
    all_to_all x1, waiting for transfers between devices, on_device(): got = lax.all_to_all(terms, axes, 0, 0, tiled=True).reshape(rows, 2, 40, C)  13.8 us
    all_to_all x1, starting transfers between devices, on_device(): last = lax.all_to_all(sums, axes, 0, 0, tiled=True).reshape(rows, 2, 32, C)  4.5 us
    all_to_all x1, starting transfers between devices, on_device(): got = lax.all_to_all(terms, axes, 0, 0, tiled=True).reshape(rows, 2, 40, C)  4.28 us
    unnamed x28, local copies, waits for them, and re-layouts  2.87 us
    pallas_call x1, Pallas kernels, on_device(): call(ready_kernel, sds((rows, 3 * cols, C), BF16), 4, (pltpu.VMEM((rows *...  2.59 us
  transfers between devices with their start and end apart: 4, of which 4 were waited for; matrix products, arithmetic and copies ran while one was open for 0% of the time, Pallas kernels for 5%

profile of v5, /device:TPU:1, one launch (start us, length us, event | category | flops | bytes accessed | tf_op | source)
XLA Modules:
  0.0 119.8 jit_solution(13725920047624977860)
XLA Ops:
  0.6 2.6 %shard_map.169 = (bf16[64,2,64,128]{3,2,1,0:T(8,128)(2,1)S(1)}, bf16[2048,128]{1,0:T(8,128)(2,1)S(1)}) custom-call(bf16[64,32,128]{2,1,0:T(8,128)(2,1)} %pair_ref.1, bf16[64,32,128]{2,1,0:T(8,128)(2,1)} %grad_hbm.1, f32[1,128]{1,0:T(1,128)} %bitcast.16, f32[1,128]{1,0:T(1,128)} %bitcast.21, bf16[4,128]{1,0:T(4,128)(2,1)} %bitcast.13), custom_call_target="tpu_custom_call" | custom-call | flops 100000000 | bytes 4194304 | tf_op jit(solution)/shard_map/pallas_call | solution.py:407
  3.2 0.0 copy-start.4
  3.2 41.8 %all_to_all.15.mine_ref = bf16[128,64,128]{2,1,0:T(8,128)(2,1)S(1)} all-to-all(bf16[128,64,128]{2,1,0:T(8,128)(2,1)S(1)} %bitcast.12), channel_id=1, replica_groups=mesh['row'=8,'col'=16] {'row','col'}, dimensions={0} | all-to-all | bytes 4194304 | tf_op jit(solution)/shard_map/all_to_all | solution.py:424
  45.0 0.0 copy-done.4
  45.0 0.0 copy-start.9
  45.0 0.0 copy-start.10
  45.1 0.0 copy-start.12
  45.1 0.0 copy-start.13
  45.1 1.1 slice.4
  46.2 0.5 collective-permute-start
  46.7 0.0 copy-done.6
  46.7 0.0 copy-done.7
  46.7 0.0 copy-done.9
  46.8 0.5 shard_map.170
  47.3 1.9 %collective-permute-done.other_ref = bf16[128,32,128]{2,1,0:T(8,128)(2,1)S(1)} collective-permute-done((bf16[128,32,128]{2,1,0:T(8,128)(2,1)}, bf16[128,32,128]{2,1,0:T(8,128)(2,1)S(1)}, u32[]{:S(2)}, u32[]{:S(2)}) %collective-permute-start) | collective-permute-done | bytes 1048608 | tf_op jit(solution)/shard_map/ppermute | solution.py:426
  49.2 16.5 %shard_map.171 = (bf16[128,40,128]{2,1,0:T(8,128)(2,1)}, bf16[8,256,512]{2,1,0:T(8,128)(2,1)}) custom-call(s32[1]{0:T(128)} %bitcast.core_ref, bf16[128,64,128]{2,1,0:T(8,128)(2,1)S(1)} %all_to_all.15.mine_ref, bf16[128,32,128]{2,1,0:T(8,128)(2,1)S(1)} %collective-permute-done.other_ref, f32[1,128]{1,0:T(1,128)S(1)} %bitcast.17, f32[1,128]{1,0:T(1,128)S(1)} %bitcast.22, ...), custom_call_target="tpu_custom_call" | custom-call | flops 10000000000 | bytes 6291456 | tf_op jit(solution)/shard_map/pallas_call | solution.py:435
  65.8 4.3 %all-to-all-start.1 = ((bf16[128,40,128]{2,1,0:T(8,128)(2,1)}), bf16[128,40,128]{2,1,0:T(8,128)(2,1)S(1)}, u32[]{:S(2)}, u32[]{:S(2)}) async-start(bf16[128,40,128]{2,1,0:T(8,128)(2,1)} %get-tuple-element.36), calls=%async_computation.1 | async-start | bytes 2621440 | tf_op jit(solution)/shard_map/all_to_all | solution.py:454
  70.1 0.0 copy-start
  70.1 1.6 %copy-done = bf16[8,256,512]{2,1,0:T(8,128)(2,1)S(1)} copy-done((bf16[8,256,512]{2,1,0:T(8,128)(2,1)S(1)}, bf16[8,256,512]{2,1,0:T(8,128)(2,1)}, u32[]{:S(2)}) %copy-start) | copy-done | bytes 2097176
  71.7 1.2 %copy-done.3 = bf16[128,32,128]{2,1,0:T(8,128)(2,1)S(1)} copy-done((bf16[128,32,128]{2,1,0:T(8,128)(2,1)S(1)}, bf16[128,32,128]{2,1,0:T(8,128)(2,1)}, u32[]{:S(2)}) %copy-start.3) | copy-done | bytes 1048600
  72.9 2.4 %shard_map.172 = (bf16[128,16,128]{2,1,0:T(8,128)(2,1)S(1)}, bf16[128,16,128]{2,1,0:T(8,128)(2,1)S(1)}, f32[16,128]{1,0:T(8,128)S(1)}) custom-call(s32[1]{0:T(128)} %bitcast.core_ref, bf16[128,64,128]{2,1,0:T(8,128)(2,1)S(1)} %all_to_all.15.mine_ref, bf16[128,32,128]{2,1,0:T(8,128)(2,1)S(1)} %copy-done.3, bf16[8,256,512]{2,1,0:T(8,128)(2,1)S(1)} %copy-done, ...), custom_call_target="tpu_custom_call" | custom-call | flops 1000000000 | bytes 6291456 | tf_op jit(solution)/shard_map/pallas_call | solution.py:456
  75.3 0.0 copy-start.11
  75.3 1.3 %collective-permute-start.1 = (bf16[128,16,128]{2,1,0:T(8,128)(2,1)S(1)}, bf16[128,16,128]{2,1,0:T(8,128)(2,1)S(1)}, u32[]{:S(2)}, u32[]{:S(2)}) collective-permute-start(bf16[128,16,128]{2,1,0:T(8,128)(2,1)S(1)} %get-tuple-element.34), channel_id=1, source_target_pairs={{0,1},{1,0},{2,3},{3,2},{4,5},{5,4},{6,7},{7,6},{8,9},{9,8},{10,11... | collective-permute-start | bytes 1572872 | tf_op jit(solution)/shard_map/ppermute | solution.py:464
  76.7 1.5 %collective-permute-done.1.came_ref = bf16[128,16,128]{2,1,0:T(8,128)(2,1)S(1)} collective-permute-done((bf16[128,16,128]{2,1,0:T(8,128)(2,1)S(1)}, bf16[128,16,128]{2,1,0:T(8,128)(2,1)S(1)}, u32[]{:S(2)}, u32[]{:S(2)}) %collective-permute-start.1) | collective-permute-done | bytes 524320 | tf_op jit(solution)/shard_map/ppermute | solution.py:464
  78.2 0.2 shard_map.173.held_ref
  78.4 13.8 %all-to-all-done.1 = bf16[128,40,128]{2,1,0:T(8,128)(2,1)S(1)} async-done(((bf16[128,40,128]{2,1,0:T(8,128)(2,1)}), bf16[128,40,128]{2,1,0:T(8,128)(2,1)S(1)}, u32[]{:S(2)}, u32[]{:S(2)}) %all-to-all-start.1) | async-done | bytes 1310752 | tf_op jit(solution)/shard_map/all_to_all | solution.py:454
  92.2 1.5 %shard_map.174 = (bf16[8,2048]{1,0:T(8,128)(2,1)S(1)}, bf16[128,32,128]{2,1,0:T(8,128)(2,1)}) custom-call(s32[1]{0:T(128)} %bitcast.core_ref, bf16[128,32,128]{2,1,0:T(8,128)(2,1)S(1)} %shard_map.173.held_ref, bf16[64,2,40,128]{3,2,1,0:T(8,128)(2,1)S(1)} %bitcast.10, f32[16,128]{1,0:T(8,128)S(1)} %get-tuple-element.37.norm_ref, f32[1,128]{1,0:T(1,128)S(1)} %bitcast.18, ...), custom_call_target="tpu_custom_call" | custom-call | flops 100000000 | bytes 4194304 | tf_op jit(solution)/shard_map/pallas_call | solution.py:468
  93.7 0.0 copy-start.1
  93.8 4.5 %all-to-all-start.2 = ((bf16[128,32,128]{2,1,0:T(8,128)(2,1)}), bf16[128,32,128]{2,1,0:T(8,128)(2,1)S(1)}, u32[]{:S(2)}, u32[]{:S(2)}) async-start(bf16[128,32,128]{2,1,0:T(8,128)(2,1)} %get-tuple-element.39), calls=%async_computation.2 | async-start | bytes 2097152 | tf_op jit(solution)/shard_map/all_to_all | solution.py:483
  98.3 2.6 %shard_map.175.ready_ref = bf16[64,96,128]{2,1,0:T(8,128)(2,1)S(1)} custom-call(bf16[8,2048]{1,0:T(8,128)(2,1)S(1)} %get-tuple-element.38.z_ref, bf16[64,32,128]{2,1,0:T(8,128)(2,1)S(1)} %copy-done.1, f32[1,128]{1,0:T(1,128)S(1)} %bitcast.19, bf16[4,128]{1,0:T(4,128)(2,1)S(1)} %bitcast.15), custom_call_target="tpu_custom_call" | custom-call | flops 100000000 | bytes 8388608 | tf_op jit(solution)/shard_map/pallas_call | solution.py:484
  100.9 16.7 %all-to-all-done.2 = bf16[128,32,128]{2,1,0:T(8,128)(2,1)S(1)} async-done(((bf16[128,32,128]{2,1,0:T(8,128)(2,1)}), bf16[128,32,128]{2,1,0:T(8,128)(2,1)S(1)}, u32[]{:S(2)}, u32[]{:S(2)}) %all-to-all-start.2) | async-done | bytes 1048608 | tf_op jit(solution)/shard_map/all_to_all | solution.py:483
  117.5 2.1 %shard_map.176 = (bf16[64,32,128]{2,1,0:T(8,128)(2,1)}, f32[1,128]{1,0:T(1,128)}, f32[1,128]{1,0:T(1,128)}, f32[128,128]{1,0:T(8,128)}, f32[128,128]{1,0:T(8,128...) custom-call(bf16[64,96,128]{2,1,0:T(8,128)(2,1)S(1)} %shard_map.175.ready_ref, ...), custom_call_target="tpu_custom_call" | custom-call | bytes 8388608 | tf_op jit(solution)/shard_map/pallas_call | solution.py:493
  (14 shorter events, 0.0 us)
Async XLA Ops:
  3.2 41.8 %copy-start.4 = (bf16[2048,128]{1,0:T(8,128)(2,1)}, bf16[2048,128]{1,0:T(8,128)(2,1)S(1)}, u32[]{:S(2)}) copy-start(bf16[2048,128]{1,0:T(8,128)(2,1)S(1)} %get-tuple-element.35.nt_ref) | copy-start | bytes 1572868
  45.0 1.7 %copy-start.6 = (bf16[128,128]{1,0:T(8,128)(2,1)S(1)}, bf16[128,128]{1,0:T(8,128)(2,1)}, u32[]{:S(2)}) copy-start(bf16[128,128]{1,0:T(8,128)(2,1)} %wq_ref.1) | copy-start | bytes 98308
  45.0 1.7 %copy-start.7 = (bf16[128,128]{1,0:T(8,128)(2,1)S(1)}, bf16[128,128]{1,0:T(8,128)(2,1)}, u32[]{:S(2)}) copy-start(bf16[128,128]{1,0:T(8,128)(2,1)} %wk_ref.1) | copy-start | bytes 98308
  45.0 1.7 %copy-start.8 = (bf16[128,128]{1,0:T(8,128)(2,1)S(1)}, bf16[128,128]{1,0:T(8,128)(2,1)}, u32[]{:S(2)}) copy-start(bf16[128,128]{1,0:T(8,128)(2,1)} %wv_ref.1) | copy-start | bytes 98308
  45.0 1.7 %copy-start.9 = (bf16[128,128]{1,0:T(8,128)(2,1)S(1)}, bf16[128,128]{1,0:T(8,128)(2,1)}, u32[]{:S(2)}) copy-start(bf16[128,128]{1,0:T(8,128)(2,1)} %wg_ref.1) | copy-start | bytes 98308
  45.0 1.7 %copy-start.10 = (bf16[128,128]{1,0:T(8,128)(2,1)S(1)}, bf16[128,128]{1,0:T(8,128)(2,1)}, u32[]{:S(2)}) copy-start(bf16[128,128]{1,0:T(8,128)(2,1)} %wo_ref.1) | copy-start | bytes 98308
  45.1 4.2 %copy-start.12 = (f32[128]{0:T(128)S(1)}, f32[128]{0:T(128)}, u32[]{:S(2)}) copy-start(f32[128]{0:T(128)} %param.12) | copy-start | bytes 1540
  45.1 4.2 %copy-start.13 = (f32[128]{0:T(128)S(1)}, f32[128]{0:T(128)}, u32[]{:S(2)}) copy-start(f32[128]{0:T(128)} %param.13) | copy-start | bytes 1540
  46.2 3.0 %collective-permute-start = (bf16[128,32,128]{2,1,0:T(8,128)(2,1)}, bf16[128,32,128]{2,1,0:T(8,128)(2,1)S(1)}, u32[]{:S(2)}, u32[]{:S(2)}) collective-permute-start(bf16[128,32,128]{2,1,0:T(8,128)(2,1)} %slice.4), channel_id=1, source_target_pairs={{0,1},{1,0},{2,3},{3,2},{4,5},{5,4},{6,7},{7,6},{8,9},{9,8},{10,11... | collective-permute-start | bytes 3145736 | tf_op jit(solution)/shard_map/ppermute | solution.py:426
  49.2 16.6 %copy-start.2 = (bf16[128,32,128]{2,1,0:T(8,128)(2,1)}, bf16[128,32,128]{2,1,0:T(8,128)(2,1)S(1)}, u32[]{:S(2)}) copy-start(bf16[128,32,128]{2,1,0:T(8,128)(2,1)S(1)} %collective-permute-done.other_ref) | copy-start | bytes 3145732
  65.8 26.4 %all-to-all-start.1 = ((bf16[128,40,128]{2,1,0:T(8,128)(2,1)}), bf16[128,40,128]{2,1,0:T(8,128)(2,1)S(1)}, u32[]{:S(2)}, u32[]{:S(2)}) async-start(bf16[128,40,128]{2,1,0:T(8,128)(2,1)} %get-tuple-element.36), calls=%async_computation.1 | async-start | bytes 2621440 | tf_op jit(solution)/shard_map/all_to_all | solution.py:454
  70.1 1.6 %copy-start = (bf16[8,256,512]{2,1,0:T(8,128)(2,1)S(1)}, bf16[8,256,512]{2,1,0:T(8,128)(2,1)}, u32[]{:S(2)}) copy-start(bf16[8,256,512]{2,1,0:T(8,128)(2,1)} %get-tuple-element.32.d_ref) | copy-start | bytes 6291460
  71.7 1.2 %copy-start.3 = (bf16[128,32,128]{2,1,0:T(8,128)(2,1)S(1)}, bf16[128,32,128]{2,1,0:T(8,128)(2,1)}, u32[]{:S(2)}) copy-start(bf16[128,32,128]{2,1,0:T(8,128)(2,1)} %copy-done.2) | copy-start | bytes 3145732
  72.9 5.3 %copy-start.5 = (bf16[2048,128]{1,0:T(8,128)(2,1)S(1)}, bf16[2048,128]{1,0:T(8,128)(2,1)}, u32[]{:S(2)}) copy-start(bf16[2048,128]{1,0:T(8,128)(2,1)} %copy-done.4) | copy-start | bytes 1572868
  75.3 16.9 %copy-start.11 = (bf16[128,4]{0,1:T(4,128)(2,1)S(1)}, bf16[128,4]{0,1:T(4,128)(2,1)}, u32[]{:S(2)}) copy-start(bf16[128,4]{0,1:T(4,128)(2,1)} %param.18) | copy-start | bytes 3076
  75.3 2.9 %collective-permute-start.1 = (bf16[128,16,128]{2,1,0:T(8,128)(2,1)S(1)}, bf16[128,16,128]{2,1,0:T(8,128)(2,1)S(1)}, u32[]{:S(2)}, u32[]{:S(2)}) collective-permute-start(bf16[128,16,128]{2,1,0:T(8,128)(2,1)S(1)} %get-tuple-element.34), channel_id=1, source_target_pairs={{0,1},{1,0},{2,3},{3,2},{4,5},{5,4},{6,7},{7,6},{8,9},{9,8},{10,11... | collective-permute-start | bytes 1572872 | tf_op jit(solution)/shard_map/ppermute | solution.py:464
  93.7 4.5 %copy-start.1 = (bf16[64,32,128]{2,1,0:T(8,128)(2,1)S(1)}, bf16[64,32,128]{2,1,0:T(8,128)(2,1)}, u32[]{:S(2)}) copy-start(bf16[64,32,128]{2,1,0:T(8,128)(2,1)} %pair_ref.1) | copy-start | bytes 1572868
  93.8 23.8 %all-to-all-start.2 = ((bf16[128,32,128]{2,1,0:T(8,128)(2,1)}), bf16[128,32,128]{2,1,0:T(8,128)(2,1)S(1)}, u32[]{:S(2)}, u32[]{:S(2)}) async-start(bf16[128,32,128]{2,1,0:T(8,128)(2,1)} %get-tuple-element.39), calls=%async_computation.2 | async-start | bytes 2097152 | tf_op jit(solution)/shard_map/all_to_all | solution.py:483

commit v6 on v5

--- a/solution.py
+++ b/solution.py
@@ -72,7 +72,8 @@
         pltpu.make_async_copy(src, dst, sems.at[i])
         for i, (src, dst) in enumerate(
             (
-                (pair_hbm, out_ref.at[:, 0, 0:cols, :]),
+                (pair_hbm.at[0 : rows // 2], out_ref.at[0 : rows // 2, 0, 0:cols, :]),
+                (pair_hbm.at[rows // 2 : rows], out_ref.at[rows // 2 : rows, 0, 0:cols, :]),
                 (gain_hbm, gain_scr),
                 (shift_hbm, shift_scr),
                 (wb_hbm, wb_scr),
@@ -82,10 +83,13 @@
     ]
     for copy in copies:
         copy.start()
-    for copy in copies[:-1]:
+    size = rows * cols // 2
+    for p in range(2):
+        copies[p].wait()
+        part = out_ref[p * rows // 2 : (p + 1) * rows // 2, 0, 0:cols, :]
+        n_scr[p * size : (p + 1) * size, :] = normalize(part.reshape(size, C).astype(F32))[0]
+    for copy in copies[2:-1]:
         copy.wait()
-    normed, _ = normalize(out_ref[:, 0, 0:cols, :].reshape(rows * cols, C).astype(F32))
-    n_scr[...] = normed
     for k in range(cols):
         part = n_scr[pl.ds(k, rows, stride=cols), :]
         nt_ref[k * rows : (k + 1) * rows, :] = part.astype(BF16)
@@ -415,7 +419,7 @@
             pltpu.VMEM((1, C), F32),
             pltpu.VMEM((H, C), BF16),
             turned_scr,
-            pltpu.SemaphoreType.DMA((5,)),
+            pltpu.SemaphoreType.DMA((6,)),
         ),
         hbm=5,
         flops=10**8,
@@ -508,7 +512,7 @@
             pltpu.VMEM((2, 328, C), F32),
             pltpu.VMEM(pair.shape, BF16),
             pltpu.VMEM((5, C, C), F32),
-            pltpu.SemaphoreType.DMA((4,)),
+            pltpu.SemaphoreType.DMA((8,)),
             pltpu.SemaphoreType.DMA((5,)),
         ),
         to_hbm=(0, 3, 4, 5, 6, 8),

time: 120 us -> 120 us (level)
  no operation moved by 1% of the time
where the time goes in v6:
time: 120 us
  blocking collectives  41.8 us (35%)
  waiting for transfers between devices  34 us (28%)
  Pallas kernels  28.7 us (24%)
  starting transfers between devices  10.7 us (9%)
  local copies, waits for them, and re-layouts  3.98 us (3%)
    all_to_all x1, blocking collectives, on_device(): lax.all_to_all(packed.reshape(devices, 64, C), axes, 0, 0, tiled=True)  41.8 us
    all_to_all x1, waiting for transfers between devices, on_device(): last = lax.all_to_all(sums, axes, 0, 0, tiled=True).reshape(rows, 2, 32, C)  16.7 us
    pallas_call x1, Pallas kernels, on_device(): call(attend_kernel, (pltpu.HBM((devices, 40, C), BF16), pltpu.HBM((8, 256...  16.5 us
    all_to_all x1, waiting for transfers between devices, on_device(): got = lax.all_to_all(terms, axes, 0, 0, tiled=True).reshape(rows, 2, 40, C)  13.8 us
    all_to_all x1, starting transfers between devices, on_device(): last = lax.all_to_all(sums, axes, 0, 0, tiled=True).reshape(rows, 2, 32, C)  4.5 us
    all_to_all x1, starting transfers between devices, on_device(): got = lax.all_to_all(terms, axes, 0, 0, tiled=True).reshape(rows, 2, 40, C)  4.29 us
    unnamed x28, local copies, waits for them, and re-layouts  2.87 us
    pallas_call x1, Pallas kernels, on_device(): call(pack_kernel, (sds((rows, 2, 64, C), BF16), sds((rows * cols, C), BF1...  2.81 us
  transfers between devices with their start and end apart: 4, of which 4 were waited for; matrix products, arithmetic and copies ran while one was open for 0% of the time, Pallas kernels for 5%

profile of v6, /device:TPU:1, one launch (start us, length us, event | category | flops | bytes accessed | tf_op | source)
XLA Modules:
  0.0 120.1 jit_solution(4992498601150545716)
XLA Ops:
  0.6 2.8 %shard_map.169 = (bf16[64,2,64,128]{3,2,1,0:T(8,128)(2,1)S(1)}, bf16[2048,128]{1,0:T(8,128)(2,1)S(1)}) custom-call(bf16[64,32,128]{2,1,0:T(8,128)(2,1)} %pair_ref.1, bf16[64,32,128]{2,1,0:T(8,128)(2,1)} %grad_hbm.1, f32[1,128]{1,0:T(1,128)} %bitcast.16, f32[1,128]{1,0:T(1,128)} %bitcast.21, bf16[4,128]{1,0:T(4,128)(2,1)} %bitcast.13), custom_call_target="tpu_custom_call" | custom-call | flops 100000000 | bytes 4194304 | tf_op jit(solution)/shard_map/pallas_call | solution.py:411
  3.5 0.0 copy-start.4
  3.5 41.8 %all_to_all.15.mine_ref = bf16[128,64,128]{2,1,0:T(8,128)(2,1)S(1)} all-to-all(bf16[128,64,128]{2,1,0:T(8,128)(2,1)S(1)} %bitcast.12), channel_id=1, replica_groups=mesh['row'=8,'col'=16] {'row','col'}, dimensions={0} | all-to-all | bytes 4194304 | tf_op jit(solution)/shard_map/all_to_all | solution.py:428
  45.3 0.0 copy-done.4
  45.3 0.0 copy-start.9
  45.3 0.0 copy-start.10
  45.3 0.0 copy-start.12
  45.3 0.0 copy-start.13
  45.3 1.1 slice.4
  46.4 0.5 collective-permute-start
  47.0 0.0 copy-done.6
  47.0 0.0 copy-done.7
  47.0 0.0 copy-done.8
  47.0 0.5 shard_map.170
  47.5 1.9 %collective-permute-done.other_ref = bf16[128,32,128]{2,1,0:T(8,128)(2,1)S(1)} collective-permute-done((bf16[128,32,128]{2,1,0:T(8,128)(2,1)}, bf16[128,32,128]{2,1,0:T(8,128)(2,1)S(1)}, u32[]{:S(2)}, u32[]{:S(2)}) %collective-permute-start) | collective-permute-done | bytes 1048608 | tf_op jit(solution)/shard_map/ppermute | solution.py:430
  49.5 16.5 %shard_map.171 = (bf16[128,40,128]{2,1,0:T(8,128)(2,1)}, bf16[8,256,512]{2,1,0:T(8,128)(2,1)}) custom-call(s32[1]{0:T(128)} %bitcast.core_ref, bf16[128,64,128]{2,1,0:T(8,128)(2,1)S(1)} %all_to_all.15.mine_ref, bf16[128,32,128]{2,1,0:T(8,128)(2,1)S(1)} %collective-permute-done.other_ref, f32[1,128]{1,0:T(1,128)S(1)} %bitcast.17, f32[1,128]{1,0:T(1,128)S(1)} %bitcast.22, ...), custom_call_target="tpu_custom_call" | custom-call | flops 10000000000 | bytes 6291456 | tf_op jit(solution)/shard_map/pallas_call | solution.py:439
  66.0 4.3 %all-to-all-start.1 = ((bf16[128,40,128]{2,1,0:T(8,128)(2,1)}), bf16[128,40,128]{2,1,0:T(8,128)(2,1)S(1)}, u32[]{:S(2)}, u32[]{:S(2)}) async-start(bf16[128,40,128]{2,1,0:T(8,128)(2,1)} %get-tuple-element.36), calls=%async_computation.1 | async-start | bytes 2621440 | tf_op jit(solution)/shard_map/all_to_all | solution.py:458
  70.3 1.6 %copy-done = bf16[8,256,512]{2,1,0:T(8,128)(2,1)S(1)} copy-done((bf16[8,256,512]{2,1,0:T(8,128)(2,1)S(1)}, bf16[8,256,512]{2,1,0:T(8,128)(2,1)}, u32[]{:S(2)}) %copy-start) | copy-done | bytes 2097176
  71.9 1.2 %copy-done.3 = bf16[128,32,128]{2,1,0:T(8,128)(2,1)S(1)} copy-done((bf16[128,32,128]{2,1,0:T(8,128)(2,1)S(1)}, bf16[128,32,128]{2,1,0:T(8,128)(2,1)}, u32[]{:S(2)}) %copy-start.3) | copy-done | bytes 1048600
  73.1 2.4 %shard_map.172 = (bf16[128,16,128]{2,1,0:T(8,128)(2,1)S(1)}, bf16[128,16,128]{2,1,0:T(8,128)(2,1)S(1)}, f32[16,128]{1,0:T(8,128)S(1)}) custom-call(s32[1]{0:T(128)} %bitcast.core_ref, bf16[128,64,128]{2,1,0:T(8,128)(2,1)S(1)} %all_to_all.15.mine_ref, bf16[128,32,128]{2,1,0:T(8,128)(2,1)S(1)} %copy-done.3, bf16[8,256,512]{2,1,0:T(8,128)(2,1)S(1)} %copy-done, ...), custom_call_target="tpu_custom_call" | custom-call | flops 1000000000 | bytes 6291456 | tf_op jit(solution)/shard_map/pallas_call | solution.py:460
  75.6 0.0 copy-start.11
  75.6 1.3 %collective-permute-start.1 = (bf16[128,16,128]{2,1,0:T(8,128)(2,1)S(1)}, bf16[128,16,128]{2,1,0:T(8,128)(2,1)S(1)}, u32[]{:S(2)}, u32[]{:S(2)}) collective-permute-start(bf16[128,16,128]{2,1,0:T(8,128)(2,1)S(1)} %get-tuple-element.34), channel_id=1, source_target_pairs={{0,1},{1,0},{2,3},{3,2},{4,5},{5,4},{6,7},{7,6},{8,9},{9,8},{10,11... | collective-permute-start | bytes 1572872 | tf_op jit(solution)/shard_map/ppermute | solution.py:468
  76.9 1.5 %collective-permute-done.1.came_ref = bf16[128,16,128]{2,1,0:T(8,128)(2,1)S(1)} collective-permute-done((bf16[128,16,128]{2,1,0:T(8,128)(2,1)S(1)}, bf16[128,16,128]{2,1,0:T(8,128)(2,1)S(1)}, u32[]{:S(2)}, u32[]{:S(2)}) %collective-permute-start.1) | collective-permute-done | bytes 524320 | tf_op jit(solution)/shard_map/ppermute | solution.py:468
  78.5 0.2 shard_map.173.held_ref
  78.6 13.8 %all-to-all-done.1 = bf16[128,40,128]{2,1,0:T(8,128)(2,1)S(1)} async-done(((bf16[128,40,128]{2,1,0:T(8,128)(2,1)}), bf16[128,40,128]{2,1,0:T(8,128)(2,1)S(1)}, u32[]{:S(2)}, u32[]{:S(2)}) %all-to-all-start.1) | async-done | bytes 1310752 | tf_op jit(solution)/shard_map/all_to_all | solution.py:458
  92.5 0.0 copy-done.11
  92.5 1.5 %shard_map.174 = (bf16[8,2048]{1,0:T(8,128)(2,1)S(1)}, bf16[128,32,128]{2,1,0:T(8,128)(2,1)}) custom-call(s32[1]{0:T(128)} %bitcast.core_ref, bf16[128,32,128]{2,1,0:T(8,128)(2,1)S(1)} %shard_map.173.held_ref, bf16[64,2,40,128]{3,2,1,0:T(8,128)(2,1)S(1)} %bitcast.10, f32[16,128]{1,0:T(8,128)S(1)} %get-tuple-element.37.norm_ref, f32[1,128]{1,0:T(1,128)S(1)} %bitcast.18, ...), custom_call_target="tpu_custom_call" | custom-call | flops 100000000 | bytes 4194304 | tf_op jit(solution)/shard_map/pallas_call | solution.py:472
  94.0 0.0 copy-start.1
  94.0 4.5 %all-to-all-start.2 = ((bf16[128,32,128]{2,1,0:T(8,128)(2,1)}), bf16[128,32,128]{2,1,0:T(8,128)(2,1)S(1)}, u32[]{:S(2)}, u32[]{:S(2)}) async-start(bf16[128,32,128]{2,1,0:T(8,128)(2,1)} %get-tuple-element.39), calls=%async_computation.2 | async-start | bytes 2097152 | tf_op jit(solution)/shard_map/all_to_all | solution.py:487
  98.5 2.6 %shard_map.175.ready_ref = bf16[64,96,128]{2,1,0:T(8,128)(2,1)S(1)} custom-call(bf16[8,2048]{1,0:T(8,128)(2,1)S(1)} %get-tuple-element.38.z_ref, bf16[64,32,128]{2,1,0:T(8,128)(2,1)S(1)} %copy-done.1, f32[1,128]{1,0:T(1,128)S(1)} %bitcast.19, bf16[4,128]{1,0:T(4,128)(2,1)S(1)} %bitcast.15), custom_call_target="tpu_custom_call" | custom-call | flops 100000000 | bytes 8388608 | tf_op jit(solution)/shard_map/pallas_call | solution.py:488
  101.1 16.7 %all-to-all-done.2 = bf16[128,32,128]{2,1,0:T(8,128)(2,1)S(1)} async-done(((bf16[128,32,128]{2,1,0:T(8,128)(2,1)}), bf16[128,32,128]{2,1,0:T(8,128)(2,1)S(1)}, u32[]{:S(2)}, u32[]{:S(2)}) %all-to-all-start.2) | async-done | bytes 1048608 | tf_op jit(solution)/shard_map/all_to_all | solution.py:487
  117.8 2.1 %shard_map.176 = (bf16[64,32,128]{2,1,0:T(8,128)(2,1)}, f32[1,128]{1,0:T(1,128)}, f32[1,128]{1,0:T(1,128)}, f32[128,128]{1,0:T(8,128)}, f32[128,128]{1,0:T(8,128...) custom-call(bf16[64,96,128]{2,1,0:T(8,128)(2,1)S(1)} %shard_map.175.ready_ref, ...), custom_call_target="tpu_custom_call" | custom-call | bytes 8388608 | tf_op jit(solution)/shard_map/pallas_call | solution.py:497
  (14 shorter events, 0.0 us)
Async XLA Ops:
  3.5 41.8 %copy-start.4 = (bf16[2048,128]{1,0:T(8,128)(2,1)}, bf16[2048,128]{1,0:T(8,128)(2,1)S(1)}, u32[]{:S(2)}) copy-start(bf16[2048,128]{1,0:T(8,128)(2,1)S(1)} %get-tuple-element.35.nt_ref) | copy-start | bytes 1572868
  45.3 1.7 %copy-start.6 = (bf16[128,128]{1,0:T(8,128)(2,1)S(1)}, bf16[128,128]{1,0:T(8,128)(2,1)}, u32[]{:S(2)}) copy-start(bf16[128,128]{1,0:T(8,128)(2,1)} %wq_ref.1) | copy-start | bytes 98308
  45.3 1.7 %copy-start.7 = (bf16[128,128]{1,0:T(8,128)(2,1)S(1)}, bf16[128,128]{1,0:T(8,128)(2,1)}, u32[]{:S(2)}) copy-start(bf16[128,128]{1,0:T(8,128)(2,1)} %wk_ref.1) | copy-start | bytes 98308
  45.3 1.7 %copy-start.8 = (bf16[128,128]{1,0:T(8,128)(2,1)S(1)}, bf16[128,128]{1,0:T(8,128)(2,1)}, u32[]{:S(2)}) copy-start(bf16[128,128]{1,0:T(8,128)(2,1)} %wv_ref.1) | copy-start | bytes 98308
  45.3 1.7 %copy-start.9 = (bf16[128,128]{1,0:T(8,128)(2,1)S(1)}, bf16[128,128]{1,0:T(8,128)(2,1)}, u32[]{:S(2)}) copy-start(bf16[128,128]{1,0:T(8,128)(2,1)} %wg_ref.1) | copy-start | bytes 98308
  45.3 1.7 %copy-start.10 = (bf16[128,128]{1,0:T(8,128)(2,1)S(1)}, bf16[128,128]{1,0:T(8,128)(2,1)}, u32[]{:S(2)}) copy-start(bf16[128,128]{1,0:T(8,128)(2,1)} %wo_ref.1) | copy-start | bytes 98308
  45.3 4.2 %copy-start.12 = (f32[128]{0:T(128)S(1)}, f32[128]{0:T(128)}, u32[]{:S(2)}) copy-start(f32[128]{0:T(128)} %param.12) | copy-start | bytes 1540
  45.3 4.2 %copy-start.13 = (f32[128]{0:T(128)S(1)}, f32[128]{0:T(128)}, u32[]{:S(2)}) copy-start(f32[128]{0:T(128)} %param.13) | copy-start | bytes 1540
  46.4 3.0 %collective-permute-start = (bf16[128,32,128]{2,1,0:T(8,128)(2,1)}, bf16[128,32,128]{2,1,0:T(8,128)(2,1)S(1)}, u32[]{:S(2)}, u32[]{:S(2)}) collective-permute-start(bf16[128,32,128]{2,1,0:T(8,128)(2,1)} %slice.4), channel_id=1, source_target_pairs={{0,1},{1,0},{2,3},{3,2},{4,5},{5,4},{6,7},{7,6},{8,9},{9,8},{10,11... | collective-permute-start | bytes 3145736 | tf_op jit(solution)/shard_map/ppermute | solution.py:430
  49.5 16.6 %copy-start.2 = (bf16[128,32,128]{2,1,0:T(8,128)(2,1)}, bf16[128,32,128]{2,1,0:T(8,128)(2,1)S(1)}, u32[]{:S(2)}) copy-start(bf16[128,32,128]{2,1,0:T(8,128)(2,1)S(1)} %collective-permute-done.other_ref) | copy-start | bytes 3145732
  66.0 26.4 %all-to-all-start.1 = ((bf16[128,40,128]{2,1,0:T(8,128)(2,1)}), bf16[128,40,128]{2,1,0:T(8,128)(2,1)S(1)}, u32[]{:S(2)}, u32[]{:S(2)}) async-start(bf16[128,40,128]{2,1,0:T(8,128)(2,1)} %get-tuple-element.36), calls=%async_computation.1 | async-start | bytes 2621440 | tf_op jit(solution)/shard_map/all_to_all | solution.py:458
  70.3 1.6 %copy-start = (bf16[8,256,512]{2,1,0:T(8,128)(2,1)S(1)}, bf16[8,256,512]{2,1,0:T(8,128)(2,1)}, u32[]{:S(2)}) copy-start(bf16[8,256,512]{2,1,0:T(8,128)(2,1)} %get-tuple-element.32.d_ref) | copy-start | bytes 6291460
  71.9 1.2 %copy-start.3 = (bf16[128,32,128]{2,1,0:T(8,128)(2,1)S(1)}, bf16[128,32,128]{2,1,0:T(8,128)(2,1)}, u32[]{:S(2)}) copy-start(bf16[128,32,128]{2,1,0:T(8,128)(2,1)} %copy-done.2) | copy-start | bytes 3145732
  73.1 5.3 %copy-start.5 = (bf16[2048,128]{1,0:T(8,128)(2,1)S(1)}, bf16[2048,128]{1,0:T(8,128)(2,1)}, u32[]{:S(2)}) copy-start(bf16[2048,128]{1,0:T(8,128)(2,1)} %copy-done.4) | copy-start | bytes 1572868
  75.6 16.9 %copy-start.11 = (bf16[128,4]{0,1:T(4,128)(2,1)S(1)}, bf16[128,4]{0,1:T(4,128)(2,1)}, u32[]{:S(2)}) copy-start(bf16[128,4]{0,1:T(4,128)(2,1)} %param.18) | copy-start | bytes 3076
  75.6 2.9 %collective-permute-start.1 = (bf16[128,16,128]{2,1,0:T(8,128)(2,1)S(1)}, bf16[128,16,128]{2,1,0:T(8,128)(2,1)S(1)}, u32[]{:S(2)}, u32[]{:S(2)}) collective-permute-start(bf16[128,16,128]{2,1,0:T(8,128)(2,1)S(1)} %get-tuple-element.34), channel_id=1, source_target_pairs={{0,1},{1,0},{2,3},{3,2},{4,5},{5,4},{6,7},{7,6},{8,9},{9,8},{10,11... | collective-permute-start | bytes 1572872 | tf_op jit(solution)/shard_map/ppermute | solution.py:468
  94.0 4.5 %copy-start.1 = (bf16[64,32,128]{2,1,0:T(8,128)(2,1)S(1)}, bf16[64,32,128]{2,1,0:T(8,128)(2,1)}, u32[]{:S(2)}) copy-start(bf16[64,32,128]{2,1,0:T(8,128)(2,1)} %pair_ref.1) | copy-start | bytes 1572868
  94.0 23.8 %all-to-all-start.2 = ((bf16[128,32,128]{2,1,0:T(8,128)(2,1)}), bf16[128,32,128]{2,1,0:T(8,128)(2,1)S(1)}, u32[]{:S(2)}, u32[]{:S(2)}) async-start(bf16[128,32,128]{2,1,0:T(8,128)(2,1)} %get-tuple-element.39), calls=%async_computation.2 | async-start | bytes 2097152 | tf_op jit(solution)/shard_map/all_to_all | solution.py:487
